TPU v7x, 32 devices: a whole 2x2x4 slice. The times are simulated.
32 devices in a mesh: grp: 2 (over y), ma: 4 (over z), freq: 2 (over x), bl: 2 (over core).
Axes of the slice: x: 2, y: 2, z: 4, core: 2. Of those that a mesh axis runs over, the one named last changes fastest.
Arguments:
- sky_modes: bfloat16 [32, 2, 128, 512], P('ma', None, 'grp'), parts along dimension 2, may hold values from -6 to 6
- beam_modes: bfloat16 [32, 2, 16, 512], P('ma'), may hold values from -0.25 to 0.25
- visibilities: bfloat16 [32, 32, 2, 128, 512], P('freq', 'ma', None, 'grp', 'bl'), parts along dimension 3, may hold values from -6 to 6
- fringe: float32 [32, 2, 512], P('freq', None, 'bl'), may hold values from -4 to 4
- noise_weight: float32 [32, 512], P('freq', 'bl'), may hold values from 0.0007 to 0.006
- feed_map: int32 [512], P('bl'), may hold values from 0 to 15
Outputs:
- beam_grad: float32 [32, 2, 32, 512], P('ma', None, 'grp', 'freq'), parts along dimension 2
There are 2 independent parts, one for each index of `grp`. A program takes and returns all parts, laid end to end along the dimension named above; an argument that names none is the same for every part. Nothing has to cross between parts.
All inputs are finite; a program needn't handle non-finite values.
Results may differ from a plain program's by a relative error of at most 0.00075.
Values may be sent and summed in bfloat16 or wider, within the bound.
No kernel may reach another device: no remote copies, remote signals or barrier semaphores. Data moves between devices by JAX's collectives and lax.ppermute only.
A program may use at most 64 MiB of HBM per device.

v0:
```python
import jax
import jax.numpy as jnp
from jax import lax
from jax.sharding import PartitionSpec as P


def swapped(array, axis, bit):
    return lax.ppermute(array, axis, [(i, i ^ 1 << bit) for i in range(lax.axis_size(axis))])


def shifted(array, axis, by):
    devices = lax.axis_size(axis)
    return lax.ppermute(array, axis, [(i, (i + by) % devices) for i in range(devices)])


def pair_product(pattern, a_re, a_im, b_re, b_im, accuracy):

    def single(left_side, right_side):
        return jnp.einsum(
            pattern, left_side, right_side, preferred_element_type=jnp.float32, precision=accuracy
        )

    return (single(a_re, b_re) - single(a_im, b_im), single(a_re, b_im) + single(a_im, b_re))


def turned_block(carried, leading):
    return jnp.concatenate([leading, jnp.flip(carried[1:], axis=0)], axis=0)


def body(sky_modes, beam_modes, visibilities, fringe, noise_weight, feed_map):
    slot_count = sky_modes.shape[0]
    classes = beam_modes.shape[2]
    highest = lax.Precision.HIGHEST
    bit_count = lax.axis_size("ma").bit_length() - 1
    slots = lax.axis_index("ma") * slot_count + jnp.arange(slot_count, dtype=jnp.int32)
    parity = jnp.where(slots % 2 == 0, 1.0, -1.0).astype(jnp.float32)[:, None, None]
    sky_re, sky_im = (sky_modes[:, 0], sky_modes[:, 1])
    beam_re, beam_im = (beam_modes[:, 0], beam_modes[:, 1])
    pattern = "kql,ksl->kqs"
    direct = pair_product(pattern, beam_re, beam_im, sky_re, sky_im, None)
    carried = sky_modes
    for position in range(bit_count):
        carried = swapped(carried, "ma", position)
    sky_far = turned_block(carried, shifted(carried[0:1], "ma", 1))
    crossed = pair_product(pattern, beam_re, beam_im, sky_far[:, 0], -sky_far[:, 1], None)
    resp_re = 0.5 * (direct[0] + parity * crossed[0])
    resp_im = 0.5 * (direct[1] + parity * crossed[1])
    onehot = feed_map[None, :] == jnp.arange(classes, dtype=jnp.int32)[:, None]
    chooser = onehot.astype(jnp.float32)
    spread_re = jnp.einsum(
        "kqs,qb->ksb", resp_re, chooser, preferred_element_type=jnp.float32, precision=highest
    )[None]
    spread_im = jnp.einsum(
        "kqs,qb->ksb", resp_im, chooser, preferred_element_type=jnp.float32, precision=highest
    )[None]
    fringe_re = fringe[:, 0][:, None, None, :]
    fringe_im = fringe[:, 1][:, None, None, :]
    weight = noise_weight[:, None, None, :]
    model_re = fringe_re * spread_re - fringe_im * spread_im
    model_im = fringe_re * spread_im + fringe_im * spread_re
    resid_re = weight * (model_re - visibilities[:, :, 0].astype(jnp.float32))
    resid_im = weight * (model_im - visibilities[:, :, 1].astype(jnp.float32))
    weighted_re = (fringe_re * resid_re + fringe_im * resid_im).astype(jnp.bfloat16)
    weighted_im = (fringe_re * resid_im - fringe_im * resid_re).astype(jnp.bfloat16)
    chooser_half = onehot.astype(jnp.bfloat16)
    pooled_re = jnp.einsum(
        "fksb,qb->kqs", weighted_re, chooser_half, preferred_element_type=jnp.float32
    )
    pooled_im = jnp.einsum(
        "fksb,qb->kqs", weighted_im, chooser_half, preferred_element_type=jnp.float32
    )
    nearby = sky_modes.astype(jnp.float32)
    own_re, own_im = pair_product(
        "kqs,ksl->kql", pooled_re, pooled_im, nearby[:, 0], -nearby[:, 1], highest
    )
    distant = sky_far.astype(jnp.float32)
    far_re, far_im = pair_product(
        "kqs,ksl->kql", pooled_re, pooled_im, distant[:, 0], distant[:, 1], highest
    )
    gradient = jnp.stack(
        [0.5 * (own_re + parity * far_re), 0.5 * (own_im + parity * far_im)], axis=1
    )
    summed = lax.psum_scatter(gradient, "freq", scatter_dimension=3, tiled=True)
    return lax.psum(summed, "bl")


def solution(mesh):
    in_specs = (
        P("ma", None, "grp", None),
        P("ma", None, None, None),
        P("freq", "ma", None, "grp", "bl"),
        P("freq", None, "bl"),
        P("freq", "bl"),
        P("bl"),
    )
    out_specs = P("ma", None, "grp", "freq")
    return jax.shard_map(body, mesh=mesh, in_specs=in_specs, out_specs=out_specs, check_vma=False)
```

profile of v0, /device:TPU:0, one launch (start us, length us, event | category | flops | bytes accessed | tf_op | source)
XLA Modules:
  0.0 147.0 jit_solution(17628468304406698381)
XLA Ops:
  6.5 0.0 copy-start.1
  6.5 0.0 copy-start.3
  6.5 0.0 copy-start.2
  6.5 0.0 reduce-scatter.2.cloned.1.call-start
  6.5 1.4 copy.13
  7.9 3.1 %collective-permute-start = (bf16[8,2,64,512]{3,2,0,1:T(8,128)(2,1)S(1)}, bf16[8,2,64,512]{3,2,0,1:T(8,128)(2,1)S(1)}, u32[]{:S(2)}, u32[]{:S(2)}) collective-permute-start(bf16[8,2,64,512]{3,2,0,1:T(8,128)(2,1)S(1)} %copy.13), channel_id=1, source_target_pairs={{0,4},{4,0},{8,12},{12,8},{1,5},{5,1},{9,13},{13,9},{2,6},{6,2},{1... | collective-permute-start | bytes 3145736 | tf_op jit(solution)/shard_map/ppermute | solution.py:8
  11.0 23.2 %collective-permute-done = bf16[8,2,64,512]{3,2,0,1:T(8,128)(2,1)S(1)} collective-permute-done((bf16[8,2,64,512]{3,2,0,1:T(8,128)(2,1)S(1)}, bf16[8,2,64,512]{3,2,0,1:T(8,128)(2,1)S(1)}, u32[]{:S(2)}, u32[]{:S(2)}) %collective-permute-start) | collective-permute-done | bytes 1048608 | tf_op jit(solution)/shard_map/ppermute | solution.py:8
  34.2 2.8 %collective-permute-start.1 = (bf16[8,2,64,512]{3,2,0,1:T(8,128)(2,1)S(1)}, bf16[8,2,64,512]{3,2,0,1:T(8,128)(2,1)S(1)}, u32[]{:S(2)}, u32[]{:S(2)}) collective-permute-start(bf16[8,2,64,512]{3,2,0,1:T(8,128)(2,1)S(1)} %collective-permute-done), channel_id=1, source_target_pairs={{0,8},{4,12},{8,0},{12,4},{1,9},{5,13},{9,1},{13,5},{2,10},{6,14},... | collective-permute-start | bytes 3145736 | tf_op jit(solution)/shard_map/ppermute | solution.py:8
  36.9 0.9 fusion.65
  37.8 1.4 fusion.25
  39.1 1.4 fusion.31
  40.5 1.4 convolution_add_fusion.3
  41.9 1.4 convolution_subtract_fusion.3
  43.2 38.6 %collective-permute-done.1 = bf16[8,2,64,512]{3,2,0,1:T(8,128)(2,1)S(1)} collective-permute-done((bf16[8,2,64,512]{3,2,0,1:T(8,128)(2,1)S(1)}, bf16[8,2,64,512]{3,2,0,1:T(8,128)(2,1)S(1)}, u32[]{:S(2)}, u32[]{:S(2)}) %collective-permute-start.1) | collective-permute-done | bytes 1048608 | tf_op jit(solution)/shard_map/ppermute | solution.py:8
  81.9 0.6 collective-permute-start.2
  82.5 0.1 slice.59
  82.5 0.1 rev.4
  82.6 6.3 %collective-permute-done.2 = bf16[1,2,64,512]{3,2,0,1:T(8,128)(2,1)S(1)} collective-permute-done((bf16[1,2,64,512]{3,2,0,1:T(8,128)(2,1)S(1)}, bf16[1,2,64,512]{3,2,0,1:T(8,128)(2,1)S(1)}, u32[]{:S(2)}, u32[]{:S(2)}) %collective-permute-start.2) | collective-permute-done | bytes 131104 | tf_op jit(solution)/shard_map/ppermute | solution.py:13
  88.9 0.1 fusion.23
  89.0 0.0 copy-start
  89.1 0.0 copy-done.1
  89.1 0.2 fusion.36
  89.3 0.3 fusion.29
  89.6 0.3 fusion.13
  89.8 0.2 fusion.17
  90.1 0.0 copy-done.3
  90.1 0.4 fusion.58
  90.5 0.4 fusion.56
  91.0 0.0 copy-done.2
  91.0 8.0 %convert_reduce_fusion = (bf16[8,64,256]{2,1,0:T(8,128)(2,1)S(1)}, bf16[8,64,256]{2,1,0:T(8,128)(2,1)S(1)}) fusion(f32[8,64,256]{2,1,0:T(8,128)S(1)} %fusion.58, f32[16,256]{1,0:T(8,128)S(1)} %get-tuple-element.11, f32[8,64,256]{2,1,0:T(8,128)S(1)} %fusion.56, f32[16,256]{1,0:T(8,128)S(1)} %copy-done.2, f32[16,256]{1,0:T(8,128)S(1)} %get-tuple-element.12, ...), kind=kLoop, calls=%fused_computation.4 | loop fusion | flops 50069504 | bytes 10010624 | tf_op jit(solution)/shard_map/fksb,qb->kqs/reduce_sum | solution.py:69
  98.9 0.2 convolution_bitcast_fusion
  99.1 0.3 fusion.67
  99.5 0.3 fusion.66
  99.8 0.0 copy-done
  99.8 0.7 fusion.20
  100.5 0.2 convolution_bitcast_fusion.1
  100.7 0.7 fusion.18
  101.4 0.3 convolution_add_fusion.1
  101.7 0.3 convolution_subtract_fusion.1
  102.1 0.3 fusion.9
  102.4 0.3 fusion.6
  102.7 0.8 pad_maximum_fusion.1
  103.6 0.0 reduce-scatter.2.cloned.1.call-update
  103.6 0.0 all-reduce.2.cloned.1.call-start
  103.7 14.0 %reduce-scatter.2.cloned.1.call-done = f32[8,2,16,256]{3,2,0,1:T(8,128)} async-done(((f32[8,2,16,512]{3,2,0,1:T(8,128)}), f32[8,2,16,256]{3,2,0,1:T(8,128)}) %reduce-scatter.2.cloned.1.call-update) | async-done | bytes 262160 | tf_op jit(solution)/shard_map/reduce_scatter | solution.py:83
  117.7 0.0 all-reduce.2.cloned.1.call-update
  117.7 20.7 %all-reduce.2.cloned.1.call-done = f32[8,2,16,256]{3,2,0,1:T(8,128)} async-done(((f32[8,2,16,256]{3,2,0,1:T(8,128)}), f32[8,2,16,256]{3,2,0,1:T(8,128)}) %all-reduce.2.cloned.1.call-update) | async-done | bytes 262160 | tf_op jit(solution)/shard_map/psum | solution.py:84
  138.4 1.7 %copy.18 = f32[8,2,16,256]{3,2,1,0:T(8,128)} copy(f32[8,2,16,256]{3,2,0,1:T(8,128)} %all-reduce.2.cloned.1.call-done) | data formatting | bytes 524288 | tf_op jit(solution)/shard_map/psum | solution.py:84
  (3 shorter events, 0.0 us)
Async XLA Ops:
  6.5 82.5 %copy-start.1 = (bf16[8,2,16,512]{3,2,1,0:T(8,128)(2,1)S(1)}, bf16[8,2,16,512]{3,2,1,0:T(8,128)(2,1)}, u32[]{:S(2)}) copy-start(bf16[8,2,16,512]{3,2,1,0:T(8,128)(2,1)} %param.7) | copy-start | bytes 786436
  6.5 83.5 %copy-start.3 = (s32[256]{0:T(256)S(1)}, s32[256]{0:T(256)}, u32[]{:S(2)}) copy-start(s32[256]{0:T(256)} %param.11) | copy-start | bytes 3076
  6.5 84.4 %copy-start.2 = (f32[16,256]{1,0:T(8,128)S(1)}, f32[16,256]{1,0:T(8,128)}, u32[]{:S(2)}) copy-start(f32[16,256]{1,0:T(8,128)} %param.10) | copy-start | bytes 49156
  6.5 111.2 %reduce-scatter.2.cloned.1.call-start = ((), (), s32[]{:S(2)}) async-start(), calls=%async_computation.1 | async-start | bytes 786432 | tf_op jit(solution)/shard_map/reduce_scatter | solution.py:83
  7.9 26.2 %collective-permute-start = (bf16[8,2,64,512]{3,2,0,1:T(8,128)(2,1)S(1)}, bf16[8,2,64,512]{3,2,0,1:T(8,128)(2,1)S(1)}, u32[]{:S(2)}, u32[]{:S(2)}) collective-permute-start(bf16[8,2,64,512]{3,2,0,1:T(8,128)(2,1)S(1)} %copy.13), channel_id=1, source_target_pairs={{0,4},{4,0},{8,12},{12,8},{1,5},{5,1},{9,13},{13,9},{2,6},{6,2},{1... | collective-permute-start | bytes 3145736 | tf_op jit(solution)/shard_map/ppermute | solution.py:8
  34.2 47.7 %collective-permute-start.1 = (bf16[8,2,64,512]{3,2,0,1:T(8,128)(2,1)S(1)}, bf16[8,2,64,512]{3,2,0,1:T(8,128)(2,1)S(1)}, u32[]{:S(2)}, u32[]{:S(2)}) collective-permute-start(bf16[8,2,64,512]{3,2,0,1:T(8,128)(2,1)S(1)} %collective-permute-done), channel_id=1, source_target_pairs={{0,8},{4,12},{8,0},{12,4},{1,9},{5,13},{9,1},{13,5},{2,10},{6,14},... | collective-permute-start | bytes 3145736 | tf_op jit(solution)/shard_map/ppermute | solution.py:8
  81.9 7.1 %collective-permute-start.2 = (bf16[1,2,64,512]{3,2,0,1:T(8,128)(2,1)S(1)}, bf16[1,2,64,512]{3,2,0,1:T(8,128)(2,1)S(1)}, u32[]{:S(2)}, u32[]{:S(2)}) collective-permute-start(bf16[1,2,64,512]{3,2,0,1:T(8,128)(2,1)S(1)} %slice.58), channel_id=1, source_target_pairs={{0,4},{4,8},{8,12},{12,0},{1,5},{5,9},{9,13},{13,1},{2,6},{6,10},{... | collective-permute-start | bytes 393224 | tf_op jit(solution)/shard_map/ppermute | solution.py:13
  89.0 10.8 %copy-start = (bf16[8,2,64,512]{3,2,1,0:T(8,128)(2,1)S(1)}, bf16[8,2,64,512]{3,2,1,0:T(8,128)(2,1)}, u32[]{:S(2)}) copy-start(bf16[8,2,64,512]{3,2,1,0:T(8,128)(2,1)} %param.6) | copy-start | bytes 3145732
  103.6 34.8 %all-reduce.2.cloned.1.call-start = ((), (), s32[]{:S(2)}) async-start(), calls=%async_computation.2 | async-start | bytes 524288 | tf_op jit(solution)/shard_map/psum | solution.py:84
Sparse Core Ops, SparseCore 0:
  103.7 13.9 reduce-scatter.1
  120.1 18.2 all-reduce.1
where the time goes:
time: 147 us
  waiting for transfers between devices  103 us (70%)
  between operations  13.6 us (9%)
  matrix products  11.1 us (8%)
  other arithmetic  8.9 us (6%)
  starting transfers between devices  6.45 us (4%)
  local copies, waits for them, and re-layouts  4.04 us (3%)
    ppermute x2, waiting for transfers between devices, swapped(): lax.ppermute(array, axis, [(i, i ^ 1 << bit) for i in range(lax.axis_size...  61.8 us
    psum x1, waiting for transfers between devices, body(): return lax.psum(summed, 'bl')  20.7 us
    reduce_scatter x1, waiting for transfers between devices, body(): summed = lax.psum_scatter(gradient, 'freq', scatter_dimension=3, tiled=True)  14 us
    dot_general x16, matrix products, single(): jnp.einsum(pattern, left_side, right_side, preferred_element_type=jnp.flo...  9.8 us
    reduce_sum x1, other arithmetic, body(): jnp.einsum('fksb,qb->kqs', weighted_im, chooser_half, preferred_element_t...  7.97 us
    ppermute x1, waiting for transfers between devices, shifted(): lax.ppermute(array, axis, [(i, (i + by) % devices) for i in range(devices)])  6.34 us
    ppermute x2, starting transfers between devices, swapped(): lax.ppermute(array, axis, [(i, i ^ 1 << bit) for i in range(lax.axis_size...  5.84 us
  transfers between devices with their start and end apart: 5, of which 5 were waited for; matrix products, arithmetic and copies ran while one was open for 4% of the time, Pallas kernels for 0%

commit v1 on v0

v1 whole, which is shorter than its diff:
```python
import functools

import jax
import jax.numpy as jnp
from jax import lax
from jax.experimental import pallas as pl
from jax.experimental.pallas import tpu as pltpu
from jax.sharding import PartitionSpec as P

BF = jnp.bfloat16
F32 = jnp.float32
NT = (((1,), (1,)), ((), ()))
NN = (((1,), (0,)), ((), ()))


def split3(x):
    top = x.astype(BF)
    rest = x - top.astype(F32)
    mid = rest.astype(BF)
    return top, mid, (rest - mid.astype(F32)).astype(BF)


def dot(a, b, dims):
    return lax.dot_general(a, b, dims, preferred_element_type=F32)


def my_place():
    return lax.axis_index("freq") * lax.axis_size("bl") + lax.axis_index("bl")


def pool_kernel(devices, classes, vis, fringe, noise, feeds, *refs):
    outs, (buf, ready, sems) = refs[:devices], refs[devices:]
    channels, slots, _, skies, lines = vis.shape
    copies = [pltpu.make_async_copy(vis.at[f], buf.at[f], sems.at[f]) for f in range(channels)]
    for copy in copies:
        copy.start()
    onehot = lax.broadcasted_iota(jnp.int32, (classes, lines), 0) == feeds[...]
    weight = noise[...]
    real = fringe[:, 0, :]
    imag = fringe[:, 1, :]
    gain = jnp.sum(weight * (real * real + imag * imag), axis=0, keepdims=True)
    gain = jnp.sum(jnp.where(onehot, gain, 0.0), axis=1, keepdims=True)
    parts_re = [p.astype(F32) for p in split3(weight * real)]
    parts_im = [p.astype(F32) for p in split3(-weight * imag)]

    def spread(part, f):
        return jnp.where(onehot, part[f : f + 1, :], 0.0)

    total = None
    for f in range(channels):
        rows_re = [spread(p, f) for p in parts_re]
        rows_im = [spread(p, f) for p in parts_im]
        left_re = jnp.concatenate([y for x in zip(rows_re, rows_im) for y in x], 0).astype(BF)
        left_im = jnp.concatenate([y for x in zip(rows_im, rows_re) for y in (-x[0], x[1])], 0).astype(BF)
        copies[f].wait()
        for part, left in ((0, left_re), (1, left_im)):
            term = dot(left, buf[f, :, part].reshape(slots * skies, lines), NT)
            total = term if total is None else total + term
    wide = 2 * classes
    total = total[:wide] + total[wide : 2 * wide] + total[2 * wide :]
    width = slots * skies // devices
    for d in range(devices):
        ready[d, :wide] = total[:, d * width : (d + 1) * width]
        ready[d, wide:] = jnp.broadcast_to(gain, (classes, width))
    place = my_place()
    for r in range(devices):
        outs[r][...] = ready[place ^ r]


def pool(vis, fringe, noise, feeds, devices, classes):
    channels, slots, _, skies, lines = vis.shape
    width = slots * skies // devices
    vmem = pl.BlockSpec(memory_space=pltpu.VMEM)
    return pl.pallas_call(
        functools.partial(pool_kernel, devices, classes),
        in_specs=[pl.BlockSpec(memory_space=pl.ANY), vmem, vmem, vmem],
        out_specs=[vmem] * devices,
        out_shape=[jax.ShapeDtypeStruct((3 * classes, width), F32)] * devices,
        scratch_shapes=[
            pltpu.VMEM(vis.shape, BF),
            pltpu.VMEM((devices, 3 * classes, width), F32),
            pltpu.SemaphoreType.DMA((channels,)),
        ],
        compiler_params=pltpu.CompilerParams(vmem_limit_bytes=48 << 20),
        cost_estimate=pl.CostEstimate(
            flops=2 * 6 * classes * vis.size, bytes_accessed=2 * vis.size, transcendentals=0
        ),
    )(vis, fringe, noise, feeds.reshape(1, lines))


def grad_kernel(devices, each, place, *refs):
    sky, beam = refs[:2]
    far = refs[2 : 2 + each]
    pooled = refs[2 + each : 2 + each + devices]
    outs = refs[2 + each + devices : -1]
    whole = refs[-1]
    _, _, skies, degrees = sky.shape
    classes = beam.shape[2]
    wide = 2 * classes
    sums = pooled[0][...]
    for ref in pooled[1:]:
        sums = sums + ref[...]
    gain = 0.5 * sums[wide:]
    for i in range(each):
        parity = jnp.where((place[0] * each + i) % 2 == 0, 1.0, -1.0).astype(F32)
        mine, other = sky[i], far[i][0]
        b_re, b_im = beam[i, 0].astype(F32), beam[i, 1].astype(F32)
        at = slice(i * skies, (i + 1) * skies)

        def rows(a, b):
            return jnp.concatenate([a, b], 0).astype(BF)

        resp = dot(rows(b_re, b_im), mine[0], NT) + dot(rows(-b_im, b_re), mine[1], NT)
        resp += parity * (dot(rows(b_re, b_im), other[0], NT) + dot(rows(b_im, -b_re), other[1], NT))
        scale = gain[:, at]
        p_re = 0.5 * (scale * resp[:classes] - sums[:classes, at])
        p_im = 0.5 * (scale * resp[classes:] - sums[classes:wide, at])
        near = jnp.concatenate([jnp.concatenate([p_re, p_im], 1), jnp.concatenate([p_im, -p_re], 1)], 0)
        away = parity * jnp.concatenate([jnp.concatenate([p_re, -p_im], 1), jnp.concatenate([p_im, p_re], 1)], 0)
        near = jnp.concatenate(split3(near), 0)
        away = jnp.concatenate(split3(away), 0)
        grad = dot(near, mine.reshape(2 * skies, degrees), NN) + dot(away, other.reshape(2 * skies, degrees), NN)
        grad = grad[:wide] + grad[wide : 2 * wide] + grad[2 * wide :]
        step = degrees // len(outs)
        for h in range(len(outs)):
            whole[h, i] = grad[:, h * step : (h + 1) * step]
    row = lax.axis_index("freq")
    for h in range(len(outs)):
        outs[h][...] = whole[row ^ h]


def gradient(sky, beam, far, pooled, devices, rows):
    slots, _, skies, degrees = sky.shape
    classes = beam.shape[2]
    each = slots // devices
    vmem = pl.BlockSpec(memory_space=pltpu.VMEM)
    shape = (each, 2 * classes, degrees // rows)
    out_spec = pl.BlockSpec(shape, lambda i, place: (0, 0, 0))
    return pl.pallas_call(
        functools.partial(grad_kernel, devices, each),
        grid_spec=pltpu.PrefetchScalarGridSpec(
            num_scalar_prefetch=1,
            grid=(1,),
            in_specs=[
                pl.BlockSpec((each, 2, skies, degrees), lambda i, place: (place[0], 0, 0, 0)),
                pl.BlockSpec((each, 2, classes, degrees), lambda i, place: (place[0], 0, 0, 0)),
                *[pl.BlockSpec(x.shape, lambda i, place: (0, 0, 0, 0)) for x in far],
                *[pl.BlockSpec(x.shape, lambda i, place: (0, 0)) for x in pooled],
            ],
            out_specs=[out_spec] * rows,
            scratch_shapes=[pltpu.VMEM((rows, *shape), F32)],
        ),
        out_shape=[jax.ShapeDtypeStruct(shape, F32)] * rows,
    )(my_place().astype(jnp.int32).reshape(1), sky, beam, *far, *pooled)


def join_kernel(each, *refs):
    pieces, out = refs[:-1], refs[-1]
    place = my_place()
    for r, piece in enumerate(pieces):
        out[pl.ds((place ^ r) * each, each)] = piece[...]


def join(pieces):
    each, rows, step = pieces[0].shape
    vmem = pl.BlockSpec(memory_space=pltpu.VMEM)
    return pl.pallas_call(
        functools.partial(join_kernel, each),
        in_specs=[vmem] * len(pieces),
        out_specs=vmem,
        out_shape=jax.ShapeDtypeStruct((each * len(pieces), rows, step), F32),
    )(*pieces)


def body(sky, beam, vis, fringe, noise, feeds):
    slots = sky.shape[0]
    classes = beam.shape[2]
    blocks, rows, cores = (lax.axis_size(x) for x in ("ma", "freq", "bl"))
    devices = rows * cores
    each = slots // devices
    place = my_place()

    far = []
    for i in range(each):
        sent = lax.dynamic_slice_in_dim(sky, (slots - (place * each + i)) % slots, 1, 0)
        pairs = []
        for a in range(blocks):
            for c in range(devices):
                to = (blocks - a) % blocks if c * each + i == 0 else blocks - 1 - a
                pairs.append((a * devices + c, to * devices + c))
        far.append(lax.ppermute(sent, ("ma", "freq", "bl"), pairs))

    def across(x, r):
        return lax.ppermute(x, ("freq", "bl"), [(c, c ^ r) for c in range(devices)]) if r else x

    pooled = pool(vis, fringe, noise, feeds, devices, classes)
    pooled = [across(x, r) for r, x in enumerate(pooled)]
    blocks_out = gradient(sky, beam, far, pooled, devices, rows)
    pieces = [across(blocks_out[r // cores], r) for r in range(devices)]
    out = join(pieces)
    return out.reshape(slots, 2, classes, out.shape[-1])


def solution(mesh):
    in_specs = (
        P("ma", None, "grp", None),
        P("ma", None, None, None),
        P("freq", "ma", None, "grp", "bl"),
        P("freq", None, "bl"),
        P("freq", "bl"),
        P("bl"),
    )
    out_specs = P("ma", None, "grp", "freq")
    return jax.shard_map(body, mesh=mesh, in_specs=in_specs, out_specs=out_specs, check_vma=False)
```

time: 147 us -> 32.2 us (0.22)
  waiting for transfers between devices: 103 us -> 7.2 us
  between operations: 13.6 us -> 0.08 us
  matrix products: 11.1 us -> 0 us
  other arithmetic: 8.9 us -> 0 us
  Pallas kernels: 0 us -> 8.57 us
  starting transfers between devices: 6.45 us -> 11 us
    ppermute x3 -> x8, waiting for transfers between devices: 68.1 us -> 7.2 us  [the longest x6 7.19 us: across(): lax.ppermute(x, ('freq', 'bl'), [(c, c ^ r) for c in range(devices)])]
    psum x1 -> x0, waiting for transfers between devices: 20.7 us -> none  [body(): return lax.psum(summed, 'bl')]
    reduce_scatter x1 -> x0, waiting for transfers between devices: 14 us -> none  [body(): summed = lax.psum_scatter(gradient, 'freq', scatter_dimension=3, tiled=True)]
    dot_general x20 -> x0, matrix products: 11.1 us -> none  [the longest x16 9.8 us: single(): jnp.einsum(pattern, left_side, right_side, preferred_element_type=jnp.flo...]
    pallas_call x0 -> x3, Pallas kernels: none -> 8.57 us  [the longest x1 4.22 us: pool(): pl.pallas_call(functools.partial(pool_kernel, devices, classes), in_specs...]
    reduce_sum x1 -> x0, other arithmetic: 7.97 us -> none  [body(): jnp.einsum('fksb,qb->kqs', weighted_im, chooser_half, preferred_element_t...]
    ppermute x3 -> x8, starting transfers between devices: 6.41 us -> 11 us  [the longest x2 5.77 us: body(): far.append(lax.ppermute(sent, ('ma', 'freq', 'bl'), pairs))]
    unnamed x9 -> x24, local copies, waits for them, and re-layouts: 1.37 us -> 4.04 us
  transfers between devices with their start and end apart: 5 -> 8, of which waited for: 5 -> 4; matrix products, arithmetic and copies ran while one was open for 4% -> 0% of each run, Pallas kernels for 0% -> 13%
where the time goes in v1:
time: 32.2 us; the launch traced here: 31.9 us
  starting transfers between devices  11 us (34%)
  Pallas kernels  8.57 us (27%)
  waiting for transfers between devices  7.2 us (22%)
  local copies, waits for them, and re-layouts  5.02 us (16%)
    ppermute x6, waiting for transfers between devices, across(): lax.ppermute(x, ('freq', 'bl'), [(c, c ^ r) for c in range(devices)])  7.19 us
    ppermute x2, starting transfers between devices, body(): far.append(lax.ppermute(sent, ('ma', 'freq', 'bl'), pairs))  5.77 us
    ppermute x6, starting transfers between devices, across(): lax.ppermute(x, ('freq', 'bl'), [(c, c ^ r) for c in range(devices)])  5.25 us
    pallas_call x1, Pallas kernels, pool(): pl.pallas_call(functools.partial(pool_kernel, devices, classes), in_specs...  4.22 us
    unnamed x24, local copies, waits for them, and re-layouts  4.04 us
    pallas_call x1, Pallas kernels, gradient(): pl.pallas_call(functools.partial(grad_kernel, devices, each), grid_spec=p...  2.68 us
    pallas_call x1, Pallas kernels, join(): pl.pallas_call(functools.partial(join_kernel, each), in_specs=[vmem] * le...  1.66 us
    dynamic_slice x1, local copies, waits for them, and re-layouts, body(): lax.dynamic_slice_in_dim(sky, (slots - (place * each + i)) % slots, 1, 0)  0.98 us
  transfers between devices with their start and end apart: 8, of which 4 were waited for; matrix products, arithmetic and copies ran while one was open for 0% of the time, Pallas kernels for 13%

profile of v1, /device:TPU:0, one launch (start us, length us, event | category | flops | bytes accessed | tf_op | source)
XLA Modules:
  0.0 31.9 jit_solution(13042061747853042262)
XLA Ops:
  0.0 1.0 %constant_dynamic-slice_fusion = (bf16[1,2,64,512]{3,2,1,0:T(8,128)(2,1)S(1)}, bf16[1,2,64,512]{3,2,1,0:T(8,128)(2,1)S(1)}) fusion(bf16[8,2,64,512]{3,2,1,0:T(8,128)(2,1)} %refs_0_.1, s32[]{:T(128)S(6)} %select_n.20, s32[]{:T(128)S(6)} %select_n.18), kind=kLoop, calls=%fused_computation | loop fusion | bytes 524296 | tf_op jit(solution)/shard_map/dynamic_slice | solution.py:185
  1.0 5.1 %collective-permute-start.1 = (bf16[1,2,64,512]{3,2,1,0:T(8,128)(2,1)S(1)}, bf16[1,2,64,512]{3,2,1,0:T(8,128)(2,1)S(1)}, u32[]{:S(2)}, u32[]{:S(2)}) collective-permute-start(bf16[1,2,64,512]{3,2,1,0:T(8,128)(2,1)S(1)} %get-tuple-element.17), channel_id=1, source_target_pairs={{0,12},{1,13},{2,14},{3,15},{4,8},{5,9},{6,10},{7,11},{8,4},{9,5},... | collective-permute-start | bytes 393224 | tf_op jit(solution)/shard_map/ppermute | solution.py:191
  6.1 0.7 %collective-permute-start = (bf16[1,2,64,512]{3,2,1,0:T(8,128)(2,1)S(1)}, bf16[1,2,64,512]{3,2,1,0:T(8,128)(2,1)S(1)}, u32[]{:S(2)}, u32[]{:S(2)}) collective-permute-start(bf16[1,2,64,512]{3,2,1,0:T(8,128)(2,1)S(1)} %get-tuple-element.18), channel_id=1, source_target_pairs={{0,0},{1,13},{2,14},{3,15},{4,12},{5,9},{6,10},{7,11},{8,8},{9,5},... | collective-permute-start | bytes 393224 | tf_op jit(solution)/shard_map/ppermute | solution.py:191
  6.8 0.0 copy-start
  6.8 0.7 %copy-done = f32[16,2,256]{2,1,0:T(2,128)S(1)} copy-done((f32[16,2,256]{2,1,0:T(2,128)S(1)}, f32[16,2,256]{2,1,0:T(2,128)}, u32[]{:S(2)}) %copy-start) | copy-done | bytes 32792
  7.5 0.0 copy-start.2
  7.5 0.7 %copy-done.2 = f32[16,256]{1,0:T(8,128)S(1)} copy-done((f32[16,256]{1,0:T(8,128)S(1)}, f32[16,256]{1,0:T(8,128)}, u32[]{:S(2)}) %copy-start.2) | copy-done | bytes 16408
  8.2 0.0 copy-start.3
  8.2 0.7 %copy-done.3 = s32[256]{0:T(256)S(1)} copy-done((s32[256]{0:T(256)S(1)}, s32[256]{0:T(256)}, u32[]{:S(2)}) %copy-start.3) | copy-done | bytes 1048
  8.9 4.2 %shard_map.64 = (f32[48,128]{1,0:T(8,128)S(1)}, f32[48,128]{1,0:T(8,128)S(1)}, f32[48,128]{1,0:T(8,128)S(1)}, f32[48,128]{1,0:T(8,128)S(1)}) custom-call(bf16[16,8,2,64,256]{4,3,2,1,0:T(8,128)(2,1)} %vis.1, f32[16,2,256]{2,1,0:T(2,128)S(1)} %copy-done, f32[16,256]{1,0:T(8,128)S(1)} %copy-done.2, s32[1,256]{1,0:T(1,128)S(1)} %bitcast.3), custom_call_target="tpu_custom_call" | custom-call | flops 805306368 | bytes 8388608 | tf_op jit(solution)/shard_map/pallas_call | solution.py:74
  13.2 0.0 copy-start.1
  13.2 0.6 %copy-done.1 = f32[48,128]{1,0:T(8,128)} copy-done((f32[48,128]{1,0:T(8,128)}, f32[48,128]{1,0:T(8,128)S(1)}, u32[]{:S(2)}) %copy-start.1) | copy-done | bytes 24600
  13.8 0.8 %collective-permute-start.2 = (f32[48,128]{1,0:T(8,128)S(1)}, f32[48,128]{1,0:T(8,128)S(1)}, u32[]{:S(2)}, u32[]{:S(2)}) collective-permute-start(f32[48,128]{1,0:T(8,128)S(1)} %get-tuple-element.12), channel_id=1, source_target_pairs={{0,1},{1,0},{2,3},{3,2},{4,5},{5,4},{6,7},{7,6},{8,9},{9,8},{10,11... | collective-permute-start | bytes 73736 | tf_op jit(solution)/shard_map/ppermute | solution.py:194
  14.6 2.1 %collective-permute-start.3 = (f32[48,128]{1,0:T(8,128)S(1)}, f32[48,128]{1,0:T(8,128)S(1)}, u32[]{:S(2)}, u32[]{:S(2)}) collective-permute-start(f32[48,128]{1,0:T(8,128)S(1)} %get-tuple-element.13), channel_id=1, source_target_pairs={{0,2},{1,3},{2,0},{3,1},{4,6},{5,7},{6,4},{7,5},{8,10},{9,11},{10,... | collective-permute-start | bytes 73736 | tf_op jit(solution)/shard_map/ppermute | solution.py:194
  16.7 0.1 collective-permute-start.4
  16.9 0.0 collective-permute-done.2.refs_5_
  16.9 0.0 copy-start.9
  16.9 1.7 %collective-permute-done.3.refs_6_ = f32[48,128]{1,0:T(8,128)S(1)} collective-permute-done((f32[48,128]{1,0:T(8,128)S(1)}, f32[48,128]{1,0:T(8,128)S(1)}, u32[]{:S(2)}, u32[]{:S(2)}) %collective-permute-start.3) | collective-permute-done | bytes 24608 | tf_op jit(solution)/shard_map/ppermute | solution.py:194
  18.6 0.0 copy-start.10
  18.6 1.4 %collective-permute-done.4.refs_7_ = f32[48,128]{1,0:T(8,128)S(1)} collective-permute-done((f32[48,128]{1,0:T(8,128)S(1)}, f32[48,128]{1,0:T(8,128)S(1)}, u32[]{:S(2)}, u32[]{:S(2)}) %collective-permute-start.4) | collective-permute-done | bytes 24608 | tf_op jit(solution)/shard_map/ppermute | solution.py:194
  20.0 0.0 copy-start.11
  20.0 0.0 collective-permute-done.1.refs_3_
  20.0 0.0 copy-start.4
  20.0 0.0 collective-permute-done.refs_2_
  20.0 0.0 copy-start.5
  20.0 0.0 copy-done.9
  20.0 0.0 copy-done.10
  20.0 0.6 %copy-done.11 = f32[48,128]{1,0:T(8,128)} copy-done((f32[48,128]{1,0:T(8,128)}, f32[48,128]{1,0:T(8,128)S(1)}, u32[]{:S(2)}) %copy-start.11) | copy-done | bytes 24600
  20.6 0.1 copy-done.4
  20.6 0.0 copy-done.5
  20.7 2.7 %shard_map.65 = (f32[2,32,256]{2,1,0:T(8,128)}, f32[2,32,256]{2,1,0:T(8,128)}) custom-call(s32[1]{0:T(128)} %bitcast.place, bf16[8,2,64,512]{3,2,1,0:T(8,128)(2,1)} %refs_0_.1, bf16[8,2,16,512]{3,2,1,0:T(8,128)(2,1)} %refs_1_.1, bf16[1,2,64,512]{3,2,1,0:T(8,128)(2,1)} %copy-done.5, bf16[1,2,64,512]{3,2,1,0:T(8,128)(2,1)} %copy-done.4, f32[48,128]{1,0:T(8,128)} %copy-done.1, ...), custom_call_target="tpu_custom_call" | custom-call | tf_op jit(solution)/shard_map/pallas_call | solution.py:139
  23.4 0.2 collective-permute-start.5
  23.6 0.6 %collective-permute-start.7 = (f32[2,32,256]{2,1,0:T(8,128)}, f32[2,32,256]{2,1,0:T(8,128)S(1)}, u32[]{:S(2)}, u32[]{:S(2)}) collective-permute-start(f32[2,32,256]{2,1,0:T(8,128)} %get-tuple-element.16), channel_id=1, source_target_pairs={{0,3},{1,2},{2,1},{3,0},{4,7},{5,6},{6,5},{7,4},{8,11},{9,10},{10,... | collective-permute-start | bytes 196616 | tf_op jit(solution)/shard_map/ppermute | solution.py:194
  24.2 1.4 %collective-permute-start.6 = (f32[2,32,256]{2,1,0:T(8,128)}, f32[2,32,256]{2,1,0:T(8,128)S(1)}, u32[]{:S(2)}, u32[]{:S(2)}) collective-permute-start(f32[2,32,256]{2,1,0:T(8,128)} %get-tuple-element.16), channel_id=1, source_target_pairs={{0,2},{1,3},{2,0},{3,1},{4,6},{5,7},{6,4},{7,5},{8,10},{9,11},{10,... | collective-permute-start | bytes 196616 | tf_op jit(solution)/shard_map/ppermute | solution.py:194
  25.5 0.0 collective-permute-done.5.refs_1_
  25.5 0.0 copy-start.6
  25.5 2.3 %collective-permute-done.7.refs_3_ = f32[2,32,256]{2,1,0:T(8,128)S(1)} collective-permute-done((f32[2,32,256]{2,1,0:T(8,128)}, f32[2,32,256]{2,1,0:T(8,128)S(1)}, u32[]{:S(2)}, u32[]{:S(2)}) %collective-permute-start.7) | collective-permute-done | bytes 65568 | tf_op jit(solution)/shard_map/ppermute | solution.py:194
  27.8 0.0 copy-start.7
  27.8 1.8 %collective-permute-done.6.refs_2_ = f32[2,32,256]{2,1,0:T(8,128)S(1)} collective-permute-done((f32[2,32,256]{2,1,0:T(8,128)}, f32[2,32,256]{2,1,0:T(8,128)S(1)}, u32[]{:S(2)}, u32[]{:S(2)}) %collective-permute-start.6) | collective-permute-done | bytes 65568 | tf_op jit(solution)/shard_map/ppermute | solution.py:194
  29.6 0.0 copy-done.6
  29.6 0.0 copy-done.7
  29.6 0.0 copy-start.8
  29.6 0.6 %copy-done.8 = f32[2,32,256]{2,1,0:T(8,128)} copy-done((f32[2,32,256]{2,1,0:T(8,128)}, f32[2,32,256]{2,1,0:T(8,128)S(1)}, u32[]{:S(2)}) %copy-start.8) | copy-done | bytes 65560
  30.2 1.7 %shard_map.66 = f32[8,32,256]{2,1,0:T(8,128)} custom-call(f32[2,32,256]{2,1,0:T(8,128)} %get-tuple-element.15.refs_0_, f32[2,32,256]{2,1,0:T(8,128)} %copy-done.6, f32[2,32,256]{2,1,0:T(8,128)} %copy-done.8, f32[2,32,256]{2,1,0:T(8,128)} %copy-done.7), custom_call_target="tpu_custom_call" | custom-call | tf_op jit(solution)/shard_map/pallas_call | solution.py:167
Async XLA Ops:
  1.0 19.0 %collective-permute-start.1 = (bf16[1,2,64,512]{3,2,1,0:T(8,128)(2,1)S(1)}, bf16[1,2,64,512]{3,2,1,0:T(8,128)(2,1)S(1)}, u32[]{:S(2)}, u32[]{:S(2)}) collective-permute-start(bf16[1,2,64,512]{3,2,1,0:T(8,128)(2,1)S(1)} %get-tuple-element.17), channel_id=1, source_target_pairs={{0,12},{1,13},{2,14},{3,15},{4,8},{5,9},{6,10},{7,11},{8,4},{9,5},... | collective-permute-start | bytes 393224 | tf_op jit(solution)/shard_map/ppermute | solution.py:191
  6.1 13.9 %collective-permute-start = (bf16[1,2,64,512]{3,2,1,0:T(8,128)(2,1)S(1)}, bf16[1,2,64,512]{3,2,1,0:T(8,128)(2,1)S(1)}, u32[]{:S(2)}, u32[]{:S(2)}) collective-permute-start(bf16[1,2,64,512]{3,2,1,0:T(8,128)(2,1)S(1)} %get-tuple-element.18), channel_id=1, source_target_pairs={{0,0},{1,13},{2,14},{3,15},{4,12},{5,9},{6,10},{7,11},{8,8},{9,5},... | collective-permute-start | bytes 393224 | tf_op jit(solution)/shard_map/ppermute | solution.py:191
  6.8 0.8 %copy-start = (f32[16,2,256]{2,1,0:T(2,128)S(1)}, f32[16,2,256]{2,1,0:T(2,128)}, u32[]{:S(2)}) copy-start(f32[16,2,256]{2,1,0:T(2,128)} %fringe.1) | copy-start | bytes 98308
  7.5 0.7 %copy-start.2 = (f32[16,256]{1,0:T(8,128)S(1)}, f32[16,256]{1,0:T(8,128)}, u32[]{:S(2)}) copy-start(f32[16,256]{1,0:T(8,128)} %noise.1) | copy-start | bytes 49156
  8.2 0.7 %copy-start.3 = (s32[256]{0:T(256)S(1)}, s32[256]{0:T(256)}, u32[]{:S(2)}) copy-start(s32[256]{0:T(256)} %param.11) | copy-start | bytes 3076
  13.2 0.6 %copy-start.1 = (f32[48,128]{1,0:T(8,128)}, f32[48,128]{1,0:T(8,128)S(1)}, u32[]{:S(2)}) copy-start(f32[48,128]{1,0:T(8,128)S(1)} %get-tuple-element.11.refs_4_) | copy-start | bytes 73732
  13.8 3.1 %collective-permute-start.2 = (f32[48,128]{1,0:T(8,128)S(1)}, f32[48,128]{1,0:T(8,128)S(1)}, u32[]{:S(2)}, u32[]{:S(2)}) collective-permute-start(f32[48,128]{1,0:T(8,128)S(1)} %get-tuple-element.12), channel_id=1, source_target_pairs={{0,1},{1,0},{2,3},{3,2},{4,5},{5,4},{6,7},{7,6},{8,9},{9,8},{10,11... | collective-permute-start | bytes 73736 | tf_op jit(solution)/shard_map/ppermute | solution.py:194
  14.6 4.0 %collective-permute-start.3 = (f32[48,128]{1,0:T(8,128)S(1)}, f32[48,128]{1,0:T(8,128)S(1)}, u32[]{:S(2)}, u32[]{:S(2)}) collective-permute-start(f32[48,128]{1,0:T(8,128)S(1)} %get-tuple-element.13), channel_id=1, source_target_pairs={{0,2},{1,3},{2,0},{3,1},{4,6},{5,7},{6,4},{7,5},{8,10},{9,11},{10,... | collective-permute-start | bytes 73736 | tf_op jit(solution)/shard_map/ppermute | solution.py:194
  16.7 3.3 %collective-permute-start.4 = (f32[48,128]{1,0:T(8,128)S(1)}, f32[48,128]{1,0:T(8,128)S(1)}, u32[]{:S(2)}, u32[]{:S(2)}) collective-permute-start(f32[48,128]{1,0:T(8,128)S(1)} %get-tuple-element.14), channel_id=1, source_target_pairs={{0,3},{1,2},{2,1},{3,0},{4,7},{5,6},{6,5},{7,4},{8,11},{9,10},{10,... | collective-permute-start | bytes 73736 | tf_op jit(solution)/shard_map/ppermute | solution.py:194
  16.9 3.1 %copy-start.9 = (f32[48,128]{1,0:T(8,128)}, f32[48,128]{1,0:T(8,128)S(1)}, u32[]{:S(2)}) copy-start(f32[48,128]{1,0:T(8,128)S(1)} %collective-permute-done.2.refs_5_) | copy-start | bytes 73732
  18.6 1.4 %copy-start.10 = (f32[48,128]{1,0:T(8,128)}, f32[48,128]{1,0:T(8,128)S(1)}, u32[]{:S(2)}) copy-start(f32[48,128]{1,0:T(8,128)S(1)} %collective-permute-done.3.refs_6_) | copy-start | bytes 73732
  20.0 0.6 %copy-start.11 = (f32[48,128]{1,0:T(8,128)}, f32[48,128]{1,0:T(8,128)S(1)}, u32[]{:S(2)}) copy-start(f32[48,128]{1,0:T(8,128)S(1)} %collective-permute-done.4.refs_7_) | copy-start | bytes 73732
  20.0 0.7 %copy-start.4 = (bf16[1,2,64,512]{3,2,1,0:T(8,128)(2,1)}, bf16[1,2,64,512]{3,2,1,0:T(8,128)(2,1)S(1)}, u32[]{:S(2)}) copy-start(bf16[1,2,64,512]{3,2,1,0:T(8,128)(2,1)S(1)} %collective-permute-done.1.refs_3_) | copy-start | bytes 393220
  20.0 0.7 %copy-start.5 = (bf16[1,2,64,512]{3,2,1,0:T(8,128)(2,1)}, bf16[1,2,64,512]{3,2,1,0:T(8,128)(2,1)S(1)}, u32[]{:S(2)}) copy-start(bf16[1,2,64,512]{3,2,1,0:T(8,128)(2,1)S(1)} %collective-permute-done.refs_2_) | copy-start | bytes 393220
  23.4 2.1 %collective-permute-start.5 = (f32[2,32,256]{2,1,0:T(8,128)}, f32[2,32,256]{2,1,0:T(8,128)S(1)}, u32[]{:S(2)}, u32[]{:S(2)}) collective-permute-start(f32[2,32,256]{2,1,0:T(8,128)} %get-tuple-element.15.refs_0_), channel_id=1, source_target_pairs={{0,1},{1,0},{2,3},{3,2},{4,5},{5,4},{6,7},{7,6},{8,9},{9,8},{10,11... | collective-permute-start | bytes 196616 | tf_op jit(solution)/shard_map/ppermute | solution.py:194
  23.6 4.2 %collective-permute-start.7 = (f32[2,32,256]{2,1,0:T(8,128)}, f32[2,32,256]{2,1,0:T(8,128)S(1)}, u32[]{:S(2)}, u32[]{:S(2)}) collective-permute-start(f32[2,32,256]{2,1,0:T(8,128)} %get-tuple-element.16), channel_id=1, source_target_pairs={{0,3},{1,2},{2,1},{3,0},{4,7},{5,6},{6,5},{7,4},{8,11},{9,10},{10,... | collective-permute-start | bytes 196616 | tf_op jit(solution)/shard_map/ppermute | solution.py:194
  24.2 5.4 %collective-permute-start.6 = (f32[2,32,256]{2,1,0:T(8,128)}, f32[2,32,256]{2,1,0:T(8,128)S(1)}, u32[]{:S(2)}, u32[]{:S(2)}) collective-permute-start(f32[2,32,256]{2,1,0:T(8,128)} %get-tuple-element.16), channel_id=1, source_target_pairs={{0,2},{1,3},{2,0},{3,1},{4,6},{5,7},{6,4},{7,5},{8,10},{9,11},{10,... | collective-permute-start | bytes 196616 | tf_op jit(solution)/shard_map/ppermute | solution.py:194
  25.5 4.1 %copy-start.6 = (f32[2,32,256]{2,1,0:T(8,128)}, f32[2,32,256]{2,1,0:T(8,128)S(1)}, u32[]{:S(2)}) copy-start(f32[2,32,256]{2,1,0:T(8,128)S(1)} %collective-permute-done.5.refs_1_) | copy-start | bytes 196612
  27.8 1.8 %copy-start.7 = (f32[2,32,256]{2,1,0:T(8,128)}, f32[2,32,256]{2,1,0:T(8,128)S(1)}, u32[]{:S(2)}) copy-start(f32[2,32,256]{2,1,0:T(8,128)S(1)} %collective-permute-done.7.refs_3_) | copy-start | bytes 196612
  29.6 0.6 %copy-start.8 = (f32[2,32,256]{2,1,0:T(8,128)}, f32[2,32,256]{2,1,0:T(8,128)S(1)}, u32[]{:S(2)}) copy-start(f32[2,32,256]{2,1,0:T(8,128)S(1)} %collective-permute-done.6.refs_2_) | copy-start | bytes 196612

commit v2 on v1

v2 whole, which is shorter than its diff:
```python
import functools

import jax
import jax.numpy as jnp
from jax import lax
from jax.experimental import pallas as pl
from jax.experimental.pallas import tpu as pltpu
from jax.sharding import PartitionSpec as P

BF = jnp.bfloat16
F32 = jnp.float32
AHEAD = 6
NT = (((1,), (1,)), ((), ()))
NN = (((1,), (0,)), ((), ()))


def split3(x):
    top = x.astype(BF)
    rest = x - top.astype(F32)
    mid = rest.astype(BF)
    return top, mid, (rest - mid.astype(F32)).astype(BF)


def dot(a, b, dims):
    return lax.dot_general(a, b, dims, preferred_element_type=F32)


def my_place():
    return lax.axis_index("freq") * lax.axis_size("bl") + lax.axis_index("bl")


def rows(a, b):
    return jnp.concatenate([a, b], 0).astype(BF)


def pool_kernel(devices, classes, vis, fringe, noise, feeds, *refs):
    outs = refs[:devices]
    buf, fringe_v, noise_v, feeds_v, ready, sems, small = refs[devices:]
    channels, slots, _, skies, lines = vis.shape
    ahead = min(AHEAD, channels)
    little = [
        pltpu.make_async_copy(src, dst, small.at[i])
        for i, (src, dst) in enumerate([(feeds, feeds_v), (fringe, fringe_v), (noise, noise_v)])
    ]
    copies = [pltpu.make_async_copy(vis.at[f], buf.at[f], sems.at[f]) for f in range(channels)]
    for copy in little + copies[:ahead]:
        copy.start()
    for copy in little:
        copy.wait()
    onehot = lax.broadcasted_iota(jnp.int32, (classes, lines), 0) == feeds_v[...]
    weight = noise_v[...]
    real = fringe_v[:, 0, :]
    imag = fringe_v[:, 1, :]
    gain = jnp.sum(weight * (real * real + imag * imag), axis=0, keepdims=True)
    gain = jnp.sum(jnp.where(onehot, gain, 0.0), axis=1, keepdims=True)
    parts_re = [p.astype(F32) for p in split3(weight * real)]
    parts_im = [p.astype(F32) for p in split3(-weight * imag)]

    def spread(part, f):
        return jnp.where(onehot, part[f : f + 1, :], 0.0)

    total = None
    for f in range(channels):
        rows_re = [spread(p, f) for p in parts_re]
        rows_im = [spread(p, f) for p in parts_im]
        left_re = jnp.concatenate([y for x in zip(rows_re, rows_im) for y in x], 0).astype(BF)
        left_im = jnp.concatenate([y for x in zip(rows_im, rows_re) for y in (-x[0], x[1])], 0).astype(BF)
        copies[f].wait()
        if f + ahead < channels:
            copies[f + ahead].start()
        for part, left in ((0, left_re), (1, left_im)):
            term = dot(left, buf[f, :, part].reshape(slots * skies, lines), NT)
            total = term if total is None else total + term
    wide = 2 * classes
    total = total[:wide] + total[wide : 2 * wide] + total[2 * wide :]
    width = slots * skies // devices
    for d in range(devices):
        ready[d, :wide] = total[:, d * width : (d + 1) * width]
        ready[d, wide:] = jnp.broadcast_to(gain, (classes, width))
    place = my_place()
    for r in range(devices):
        outs[r][...] = ready[place ^ r]


def pool(vis, fringe, noise, feeds, devices, classes):
    channels, slots, _, skies, lines = vis.shape
    width = slots * skies // devices
    vmem = pl.BlockSpec(memory_space=pltpu.VMEM)
    feeds = feeds.reshape(1, lines)
    return pl.pallas_call(
        functools.partial(pool_kernel, devices, classes),
        in_specs=[pl.BlockSpec(memory_space=pl.ANY)] * 4,
        out_specs=[vmem] * devices,
        out_shape=[jax.ShapeDtypeStruct((3 * classes, width), F32)] * devices,
        scratch_shapes=[
            pltpu.VMEM(vis.shape, BF),
            pltpu.VMEM(fringe.shape, F32),
            pltpu.VMEM(noise.shape, F32),
            pltpu.VMEM(feeds.shape, jnp.int32),
            pltpu.VMEM((devices, 3 * classes, width), F32),
            pltpu.SemaphoreType.DMA((channels,)),
            pltpu.SemaphoreType.DMA((3,)),
        ],
        compiler_params=pltpu.CompilerParams(vmem_limit_bytes=60 << 20),
        cost_estimate=pl.CostEstimate(
            flops=2 * 6 * classes * vis.size, bytes_accessed=2 * vis.size, transcendentals=0
        ),
    )(vis, fringe, noise, feeds)


def near_kernel(sky, beam, *outs):
    for i, out in enumerate(outs):
        b_re, b_im = beam[i, 0].astype(F32), beam[i, 1].astype(F32)
        out[...] = dot(rows(b_re, b_im), sky[i, 0], NT) + dot(rows(-b_im, b_re), sky[i, 1], NT)


def near(sky, beam):
    each, _, skies, _ = sky.shape
    vmem = pl.BlockSpec(memory_space=pltpu.VMEM)
    return pl.pallas_call(
        near_kernel,
        in_specs=[vmem] * 2,
        out_specs=[vmem] * each,
        out_shape=[jax.ShapeDtypeStruct((2 * beam.shape[2], skies), F32)] * each,
        compiler_params=pltpu.CompilerParams(vmem_limit_bytes=8 << 20),
        cost_estimate=pl.CostEstimate(flops=1000, bytes_accessed=1000, transcendentals=0),
    )(sky, beam)


def grad_kernel(cuts, sky, beam, *refs):
    each, _, skies, degrees = sky.shape
    direct, far, pooled = refs[:each], refs[each : 2 * each], refs[2 * each : -cuts - 1]
    outs, whole = refs[-cuts - 1 : -1], refs[-1]
    classes = beam.shape[2]
    wide = 2 * classes
    step = degrees // cuts
    place = my_place()
    sums = pooled[0][...]
    for ref in pooled[1:]:
        sums = sums + ref[...]
    gain = 0.5 * sums[wide:]
    for i in range(each):
        at = slice(i * skies, (i + 1) * skies)
        parity = jnp.where((place * each + i) % 2 == 0, 1.0, -1.0).astype(F32)
        mine, other = sky[i], far[i][0]
        b_re, b_im = beam[i, 0].astype(F32), beam[i, 1].astype(F32)
        crossed = dot(rows(b_re, b_im), other[0], NT) + dot(rows(b_im, -b_re), other[1], NT)
        resp = direct[i][...] + parity * crossed
        p_re = 0.5 * (gain[:, at] * resp[:classes] - sums[:classes, at])
        p_im = 0.5 * (gain[:, at] * resp[classes:] - sums[classes:wide, at])
        own = jnp.concatenate([jnp.concatenate([p_re, p_im], 1), jnp.concatenate([p_im, -p_re], 1)], 0)
        away = parity * jnp.concatenate([jnp.concatenate([p_re, -p_im], 1), jnp.concatenate([p_im, p_re], 1)], 0)
        own = jnp.concatenate(split3(own), 0)
        away = jnp.concatenate(split3(away), 0)
        grad = dot(own, mine.reshape(2 * skies, degrees), NN) + dot(away, other.reshape(2 * skies, degrees), NN)
        grad = grad[:wide] + grad[wide : 2 * wide] + grad[2 * wide :]
        for h in range(cuts):
            whole[h, i] = grad[:, h * step : (h + 1) * step]
    row = lax.axis_index("freq")
    for h in range(cuts):
        outs[h][...] = whole[row ^ h]


def gradient(cuts, sky, beam, direct, far, pooled):
    each = sky.shape[0]
    classes, degrees = beam.shape[2:]
    vmem = pl.BlockSpec(memory_space=pltpu.VMEM)
    shape = (each, 2 * classes, degrees // cuts)
    return pl.pallas_call(
        functools.partial(grad_kernel, cuts),
        in_specs=[vmem] * (2 + 2 * each + len(pooled)),
        out_specs=[vmem] * cuts,
        out_shape=[jax.ShapeDtypeStruct(shape, F32)] * cuts,
        scratch_shapes=[pltpu.VMEM((cuts, *shape), F32)],
        compiler_params=pltpu.CompilerParams(vmem_limit_bytes=8 << 20),
    )(sky, beam, *direct, *far, *pooled)


def join_kernel(*refs):
    pieces, out = refs[:-1], refs[-1]
    each = pieces[0].shape[0]
    place = my_place()
    for r, piece in enumerate(pieces):
        out[pl.ds((place ^ r) * each, each)] = piece[...]


def join(pieces):
    each, wide, step = pieces[0].shape
    vmem = pl.BlockSpec(memory_space=pltpu.VMEM)
    return pl.pallas_call(
        join_kernel,
        in_specs=[vmem] * len(pieces),
        out_specs=vmem,
        out_shape=jax.ShapeDtypeStruct((each * len(pieces), wide, step), F32),
        compiler_params=pltpu.CompilerParams(vmem_limit_bytes=8 << 20),
    )(*pieces)


def body(sky, beam, vis, fringe, noise, feeds):
    slots = sky.shape[0]
    classes = beam.shape[2]
    blocks, cuts, cores = (lax.axis_size(x) for x in ("ma", "freq", "bl"))
    devices = cuts * cores
    each = slots // devices
    place = my_place()

    def across(x, r):
        return lax.ppermute(x, ("freq", "bl"), [(c, c ^ r) for c in range(devices)]) if r else x

    def mirror_of(i, sky):
        return lax.dynamic_slice_in_dim(sky, (slots - (place * each + i)) % slots, 1, 0)

    def mirrored(i, sent):
        pairs = []
        for a in range(blocks):
            for c in range(devices):
                to = (blocks - a) % blocks if c * each + i == 0 else blocks - 1 - a
                pairs.append((a * devices + c, to * devices + c))
        return lax.ppermute(sent, ("ma", "freq", "bl"), pairs)

    last = each - 1
    sent = mirror_of(last, sky)
    far = [None] * last + [mirrored(last, sent)]
    vis, _ = lax.optimization_barrier((vis, sent))
    sums = pool(vis, fringe, noise, feeds, devices, classes)
    *sums, later, later_beam = lax.optimization_barrier((*sums, sky, beam))
    for i in range(last):
        sent = mirror_of(i, later)
        far[i] = mirrored(i, sent)
        *sums, later, later_beam, _ = lax.optimization_barrier((*sums, later, later_beam, sent))
    pooled = [across(x, r) for r, x in enumerate(sums)]
    own = lax.dynamic_slice_in_dim(later, place * each, each, 0)
    own_beam = lax.dynamic_slice_in_dim(later_beam, place * each, each, 0)
    direct = near(own, own_beam)
    cut = gradient(cuts, own, own_beam, direct, far, pooled)
    cut = [across(x, h * cores) for h, x in enumerate(cut)]
    pieces = [across(x, r) for x in cut for r in range(cores)]
    out = join(pieces)
    return out.reshape(slots, 2, classes, out.shape[-1])


def solution(mesh):
    in_specs = (
        P("ma", None, "grp", None),
        P("ma", None, None, None),
        P("freq", "ma", None, "grp", "bl"),
        P("freq", None, "bl"),
        P("freq", "bl"),
        P("bl"),
    )
    out_specs = P("ma", None, "grp", "freq")
    return jax.shard_map(body, mesh=mesh, in_specs=in_specs, out_specs=out_specs, check_vma=False)
```

time: 32.2 us -> 28.4 us (0.88)
  local copies, waits for them, and re-layouts: 5.02 us -> 2.86 us
  waiting for transfers between devices: 7.2 us -> 5.83 us
  Pallas kernels: 8.57 us -> 7.46 us
  starting transfers between devices: 11 us -> 11.9 us
    pallas_call x2 -> x3, Pallas kernels: 4.35 us -> 1.78 us  [the longest x1 0.87 us: gradient(): pl.pallas_call(functools.partial(grad_kernel, cuts), in_specs=[vmem] * (2...]
    unnamed x24 -> x4, local copies, waits for them, and re-layouts: 4.04 us -> 1.96 us
    pallas_call x1, Pallas kernels: 4.22 us -> 5.68 us  [pool(): pl.pallas_call(functools.partial(pool_kernel, devices, classes), in_specs...]
    ppermute x6, waiting for transfers between devices: 7.19 us -> 5.83 us  [across(): lax.ppermute(x, ('freq', 'bl'), [(c, c ^ r) for c in range(devices)])]
    ppermute x6, starting transfers between devices: 5.25 us -> 6.15 us  [across(): lax.ppermute(x, ('freq', 'bl'), [(c, c ^ r) for c in range(devices)])]
    dynamic_slice x1 -> x4, local copies, waits for them, and re-layouts: 0.98 us -> 0.89 us  [the longest x1 0.85 us: body(): own_beam = lax.dynamic_slice_in_dim(later_beam, place * each, each, 0)]
  transfers between devices with their start and end apart: 8 -> 8, of which waited for: 4 -> 4; matrix products, arithmetic and copies ran while one was open for 0% -> 3% of each run, Pallas kernels for 13% -> 21%
where the time goes in v2:
time: 28.4 us; the launch traced here: 28.1 us
  starting transfers between devices  11.9 us (42%)
  Pallas kernels  7.46 us (26%)
  waiting for transfers between devices  5.83 us (21%)
  local copies, waits for them, and re-layouts  2.86 us (10%)
    ppermute x6, starting transfers between devices, across(): lax.ppermute(x, ('freq', 'bl'), [(c, c ^ r) for c in range(devices)])  6.15 us
    ppermute x6, waiting for transfers between devices, across(): lax.ppermute(x, ('freq', 'bl'), [(c, c ^ r) for c in range(devices)])  5.83 us
    ppermute x2, starting transfers between devices, mirrored(): return lax.ppermute(sent, ('ma', 'freq', 'bl'), pairs)  5.78 us
    pallas_call x1, Pallas kernels, pool(): pl.pallas_call(functools.partial(pool_kernel, devices, classes), in_specs...  5.68 us
    unnamed x4, local copies, waits for them, and re-layouts  1.96 us
    pallas_call x1, Pallas kernels, gradient(): pl.pallas_call(functools.partial(grad_kernel, cuts), in_specs=[vmem] * (2...  0.87 us
    dynamic_slice x1, local copies, waits for them, and re-layouts, body(): own_beam = lax.dynamic_slice_in_dim(later_beam, place * each, each, 0)  0.85 us
    pallas_call x1, Pallas kernels, join(): pl.pallas_call(join_kernel, in_specs=[vmem] * len(pieces), out_specs=vmem...  0.73 us
  transfers between devices with their start and end apart: 8, of which 4 were waited for; matrix products, arithmetic and copies ran while one was open for 3% of the time, Pallas kernels for 21%

profile of v2, /device:TPU:0, one launch (start us, length us, event | category | flops | bytes accessed | tf_op | source)
XLA Modules:
  0.0 28.1 jit_solution(7301734124882204060)
XLA Ops:
  0.0 0.0 copy-start
  0.0 1.2 %copy-done = bf16[8,2,64,512]{3,2,1,0:T(8,128)(2,1)S(1)} copy-done((bf16[8,2,64,512]{3,2,1,0:T(8,128)(2,1)S(1)}, bf16[8,2,64,512]{3,2,1,0:T(8,128)(2,1)}, u32[]{:S(2)}) %copy-start) | copy-done | bytes 1048600
  1.2 5.1 %collective-permute-start.1 = (bf16[1,2,64,512]{3,2,1,0:T(8,128)(2,1)S(1)}, bf16[1,2,64,512]{3,2,1,0:T(8,128)(2,1)S(1)}, u32[]{:S(2)}, u32[]{:S(2)}) collective-permute-start(bf16[1,2,64,512]{3,2,1,0:T(8,128)(2,1)S(1)} %constant_dynamic-slice_fusion.3), channel_id=1, source_target_pairs={{0,12},{1,13},{2,14},{3,15},{4,8},{5,9},{6,10},{7,11},{8,4},{9,5},... | collective-permute-start | bytes 393224 | tf_op jit(solution)/shard_map/ppermute | solution.py:219
  6.4 5.7 %shard_map.64 = (f32[48,128]{1,0:T(8,128)}, f32[48,128]{1,0:T(8,128)}, f32[48,128]{1,0:T(8,128)}, f32[48,128]{1,0:T(8,128)}) custom-call(bf16[16,8,2,64,256]{4,3,2,1,0:T(8,128)(2,1)} %vis, f32[16,2,256]{2,1,0:T(2,128)} %fringe.1, f32[16,256]{1,0:T(8,128)} %noise.1, s32[1,256]{1,0:T(1,128)} %bitcast.2), custom_call_target="tpu_custom_call" | custom-call | flops 805306368 | bytes 8388608 | tf_op jit(solution)/shard_map/pallas_call | solution.py:90
  12.1 0.7 %collective-permute-start = (bf16[1,2,64,512]{3,2,1,0:T(8,128)(2,1)S(1)}, bf16[1,2,64,512]{3,2,1,0:T(8,128)(2,1)S(1)}, u32[]{:S(2)}, u32[]{:S(2)}) collective-permute-start(bf16[1,2,64,512]{3,2,1,0:T(8,128)(2,1)S(1)} %constant_dynamic-slice_fusion.2), channel_id=1, source_target_pairs={{0,0},{1,13},{2,14},{3,15},{4,12},{5,9},{6,10},{7,11},{8,8},{9,5},... | collective-permute-start | bytes 393224 | tf_op jit(solution)/shard_map/ppermute | solution.py:219
  12.7 0.9 %collective-permute-start.2 = (f32[48,128]{1,0:T(8,128)}, f32[48,128]{1,0:T(8,128)S(1)}, u32[]{:S(2)}, u32[]{:S(2)}) collective-permute-start(f32[48,128]{1,0:T(8,128)} %get-tuple-element.42), channel_id=1, source_target_pairs={{0,1},{1,0},{2,3},{3,2},{4,5},{5,4},{6,7},{7,6},{8,9},{9,8},{10,11... | collective-permute-start | bytes 73736 | tf_op jit(solution)/shard_map/ppermute | solution.py:208
  13.6 2.2 %collective-permute-start.3 = (f32[48,128]{1,0:T(8,128)}, f32[48,128]{1,0:T(8,128)S(1)}, u32[]{:S(2)}, u32[]{:S(2)}) collective-permute-start(f32[48,128]{1,0:T(8,128)} %get-tuple-element.43), channel_id=1, source_target_pairs={{0,2},{1,3},{2,0},{3,1},{4,6},{5,7},{6,4},{7,5},{8,10},{9,11},{10,... | collective-permute-start | bytes 73736 | tf_op jit(solution)/shard_map/ppermute | solution.py:208
  15.8 0.1 collective-permute-start.4
  15.9 0.9 %constant_dynamic-slice_fusion.beam = bf16[2,2,16,512]{3,2,1,0:T(8,128)(2,1)S(1)} fusion(bf16[8,2,16,512]{3,2,1,0:T(8,128)(2,1)} %param.7, s32[]{:T(128)S(6)} %select_n.25), kind=kLoop, calls=%fused_computation | loop fusion | bytes 131076 | tf_op jit(solution)/shard_map/dynamic_slice | solution.py:233
  16.8 0.2 shard_map.65
  17.0 0.0 collective-permute-done.2.refs_5_
  17.0 0.9 %collective-permute-done.3.refs_6_ = f32[48,128]{1,0:T(8,128)S(1)} collective-permute-done((f32[48,128]{1,0:T(8,128)}, f32[48,128]{1,0:T(8,128)S(1)}, u32[]{:S(2)}, u32[]{:S(2)}) %collective-permute-start.3) | collective-permute-done | bytes 24608 | tf_op jit(solution)/shard_map/ppermute | solution.py:208
  17.9 1.4 %collective-permute-done.4.refs_7_ = f32[48,128]{1,0:T(8,128)S(1)} collective-permute-done((f32[48,128]{1,0:T(8,128)}, f32[48,128]{1,0:T(8,128)S(1)}, u32[]{:S(2)}, u32[]{:S(2)}) %collective-permute-start.4) | collective-permute-done | bytes 24608 | tf_op jit(solution)/shard_map/ppermute | solution.py:208
  19.3 0.0 collective-permute-done.refs_2_
  19.3 0.0 collective-permute-done.1.refs_3_
  19.3 0.0 copy-start.1
  19.3 0.7 %copy-done.1 = f32[48,128]{1,0:T(8,128)S(1)} copy-done((f32[48,128]{1,0:T(8,128)S(1)}, f32[48,128]{1,0:T(8,128)}, u32[]{:S(2)}) %copy-start.1) | copy-done | bytes 24600
  20.1 0.9 %shard_map.66 = (f32[2,32,256]{2,1,0:T(8,128)S(1)}, f32[2,32,256]{2,1,0:T(8,128)S(1)}) custom-call(bf16[2,2,64,512]{3,2,1,0:T(8,128)(2,1)S(1)} %constant_dynamic-slice_fusion.1.sky, bf16[2,2,16,512]{3,2,1,0:T(8,128)(2,1)S(1)} %constant_dynamic-slice_fusion.beam, f32[32,64]{1,0:T(8,128)S(1)} %get-tuple-element.39.refs_0_, ...), custom_call_target="tpu_custom_call" | custom-call | tf_op jit(solution)/shard_map/pallas_call | solution.py:169
  20.9 3.0 %collective-permute-start.6 = (f32[2,32,256]{2,1,0:T(8,128)S(1)}, f32[2,32,256]{2,1,0:T(8,128)S(1)}, u32[]{:S(2)}, u32[]{:S(2)}) collective-permute-start(f32[2,32,256]{2,1,0:T(8,128)S(1)} %get-tuple-element.46), channel_id=1, source_target_pairs={{0,2},{1,3},{2,0},{3,1},{4,6},{5,7},{6,4},{7,5},{8,10},{9,11},{10,... | collective-permute-start | bytes 196616 | tf_op jit(solution)/shard_map/ppermute | solution.py:208
  23.9 0.0 collective-permute-start.5
  23.9 2.2 %collective-permute-done.6.refs_2_ = f32[2,32,256]{2,1,0:T(8,128)S(1)} collective-permute-done((f32[2,32,256]{2,1,0:T(8,128)S(1)}, f32[2,32,256]{2,1,0:T(8,128)S(1)}, u32[]{:S(2)}, u32[]{:S(2)}) %collective-permute-start.6) | collective-permute-done | bytes 65568 | tf_op jit(solution)/shard_map/ppermute | solution.py:208
  26.2 0.0 collective-permute-start.7
  26.2 0.0 collective-permute-done.5.refs_1_
  26.2 1.2 %collective-permute-done.7.refs_3_ = f32[2,32,256]{2,1,0:T(8,128)S(1)} collective-permute-done((f32[2,32,256]{2,1,0:T(8,128)S(1)}, f32[2,32,256]{2,1,0:T(8,128)S(1)}, u32[]{:S(2)}, u32[]{:S(2)}) %collective-permute-start.7) | collective-permute-done | bytes 65568 | tf_op jit(solution)/shard_map/ppermute | solution.py:208
  27.4 0.7 %shard_map.67 = f32[8,32,256]{2,1,0:T(8,128)} custom-call(f32[2,32,256]{2,1,0:T(8,128)S(1)} %get-tuple-element.45.refs_0_, f32[2,32,256]{2,1,0:T(8,128)S(1)} %collective-permute-done.5.refs_1_, f32[2,32,256]{2,1,0:T(8,128)S(1)} %collective-permute-done.6.refs_2_, f32[2,32,256]{2,1,0:T(8,128)S(1)} %collective-permute-done.7.refs_3_), custom_call_target="tpu_custom_call" | custom-call | tf_op jit(solution)/shard_map/pallas_call | solution.py:190
  (3 shorter events, 0.0 us)
Async XLA Ops:
  0.0 1.2 %copy-start = (bf16[8,2,64,512]{3,2,1,0:T(8,128)(2,1)S(1)}, bf16[8,2,64,512]{3,2,1,0:T(8,128)(2,1)}, u32[]{:S(2)}) copy-start(bf16[8,2,64,512]{3,2,1,0:T(8,128)(2,1)} %param.6) | copy-start | bytes 3145732
  1.2 18.1 %collective-permute-start.1 = (bf16[1,2,64,512]{3,2,1,0:T(8,128)(2,1)S(1)}, bf16[1,2,64,512]{3,2,1,0:T(8,128)(2,1)S(1)}, u32[]{:S(2)}, u32[]{:S(2)}) collective-permute-start(bf16[1,2,64,512]{3,2,1,0:T(8,128)(2,1)S(1)} %constant_dynamic-slice_fusion.3), channel_id=1, source_target_pairs={{0,12},{1,13},{2,14},{3,15},{4,8},{5,9},{6,10},{7,11},{8,4},{9,5},... | collective-permute-start | bytes 393224 | tf_op jit(solution)/shard_map/ppermute | solution.py:219
  12.1 7.2 %collective-permute-start = (bf16[1,2,64,512]{3,2,1,0:T(8,128)(2,1)S(1)}, bf16[1,2,64,512]{3,2,1,0:T(8,128)(2,1)S(1)}, u32[]{:S(2)}, u32[]{:S(2)}) collective-permute-start(bf16[1,2,64,512]{3,2,1,0:T(8,128)(2,1)S(1)} %constant_dynamic-slice_fusion.2), channel_id=1, source_target_pairs={{0,0},{1,13},{2,14},{3,15},{4,12},{5,9},{6,10},{7,11},{8,8},{9,5},... | collective-permute-start | bytes 393224 | tf_op jit(solution)/shard_map/ppermute | solution.py:219
  12.7 4.2 %collective-permute-start.2 = (f32[48,128]{1,0:T(8,128)}, f32[48,128]{1,0:T(8,128)S(1)}, u32[]{:S(2)}, u32[]{:S(2)}) collective-permute-start(f32[48,128]{1,0:T(8,128)} %get-tuple-element.42), channel_id=1, source_target_pairs={{0,1},{1,0},{2,3},{3,2},{4,5},{5,4},{6,7},{7,6},{8,9},{9,8},{10,11... | collective-permute-start | bytes 73736 | tf_op jit(solution)/shard_map/ppermute | solution.py:208
  13.6 4.2 %collective-permute-start.3 = (f32[48,128]{1,0:T(8,128)}, f32[48,128]{1,0:T(8,128)S(1)}, u32[]{:S(2)}, u32[]{:S(2)}) collective-permute-start(f32[48,128]{1,0:T(8,128)} %get-tuple-element.43), channel_id=1, source_target_pairs={{0,2},{1,3},{2,0},{3,1},{4,6},{5,7},{6,4},{7,5},{8,10},{9,11},{10,... | collective-permute-start | bytes 73736 | tf_op jit(solution)/shard_map/ppermute | solution.py:208
  15.8 3.5 %collective-permute-start.4 = (f32[48,128]{1,0:T(8,128)}, f32[48,128]{1,0:T(8,128)S(1)}, u32[]{:S(2)}, u32[]{:S(2)}) collective-permute-start(f32[48,128]{1,0:T(8,128)} %get-tuple-element.44), channel_id=1, source_target_pairs={{0,3},{1,2},{2,1},{3,0},{4,7},{5,6},{6,5},{7,4},{8,11},{9,10},{10,... | collective-permute-start | bytes 73736 | tf_op jit(solution)/shard_map/ppermute | solution.py:208
  19.3 0.7 %copy-start.1 = (f32[48,128]{1,0:T(8,128)S(1)}, f32[48,128]{1,0:T(8,128)}, u32[]{:S(2)}) copy-start(f32[48,128]{1,0:T(8,128)} %get-tuple-element.41.refs_4_) | copy-start | bytes 73732
  20.9 5.2 %collective-permute-start.6 = (f32[2,32,256]{2,1,0:T(8,128)S(1)}, f32[2,32,256]{2,1,0:T(8,128)S(1)}, u32[]{:S(2)}, u32[]{:S(2)}) collective-permute-start(f32[2,32,256]{2,1,0:T(8,128)S(1)} %get-tuple-element.46), channel_id=1, source_target_pairs={{0,2},{1,3},{2,0},{3,1},{4,6},{5,7},{6,4},{7,5},{8,10},{9,11},{10,... | collective-permute-start | bytes 196616 | tf_op jit(solution)/shard_map/ppermute | solution.py:208
  23.9 2.3 %collective-permute-start.5 = (f32[2,32,256]{2,1,0:T(8,128)S(1)}, f32[2,32,256]{2,1,0:T(8,128)S(1)}, u32[]{:S(2)}, u32[]{:S(2)}) collective-permute-start(f32[2,32,256]{2,1,0:T(8,128)S(1)} %get-tuple-element.45.refs_0_), channel_id=1, source_target_pairs={{0,1},{1,0},{2,3},{3,2},{4,5},{5,4},{6,7},{7,6},{8,9},{9,8},{10,11... | collective-permute-start | bytes 196616 | tf_op jit(solution)/shard_map/ppermute | solution.py:208
  26.2 1.3 %collective-permute-start.7 = (f32[2,32,256]{2,1,0:T(8,128)S(1)}, f32[2,32,256]{2,1,0:T(8,128)S(1)}, u32[]{:S(2)}, u32[]{:S(2)}) collective-permute-start(f32[2,32,256]{2,1,0:T(8,128)S(1)} %collective-permute-done.6.refs_2_), channel_id=1, source_target_pairs={{0,1},{1,0},{2,3},{3,2},{4,5},{5,4},{6,7},{7,6},{8,9},{9,8},{10,11... | collective-permute-start | bytes 196616 | tf_op jit(solution)/shard_map/ppermute | solution.py:208

commit v3 on v2

--- a/solution.py
+++ b/solution.py
@@ -108,28 +108,30 @@
     )(vis, fringe, noise, feeds)
 
 
-def near_kernel(sky, beam, *outs):
+def near_kernel(sky, beam, held, passed, *outs):
+    passed[...] = held[...]
     for i, out in enumerate(outs):
         b_re, b_im = beam[i, 0].astype(F32), beam[i, 1].astype(F32)
         out[...] = dot(rows(b_re, b_im), sky[i, 0], NT) + dot(rows(-b_im, b_re), sky[i, 1], NT)
 
 
-def near(sky, beam):
+def near(sky, beam, held):
     each, _, skies, _ = sky.shape
     vmem = pl.BlockSpec(memory_space=pltpu.VMEM)
     return pl.pallas_call(
         near_kernel,
-        in_specs=[vmem] * 2,
-        out_specs=[vmem] * each,
-        out_shape=[jax.ShapeDtypeStruct((2 * beam.shape[2], skies), F32)] * each,
+        in_specs=[vmem] * 3,
+        out_specs=[vmem] * (each + 1),
+        out_shape=[jax.ShapeDtypeStruct(held.shape, F32)]
+        + [jax.ShapeDtypeStruct((2 * beam.shape[2], skies), F32)] * each,
         compiler_params=pltpu.CompilerParams(vmem_limit_bytes=8 << 20),
-        cost_estimate=pl.CostEstimate(flops=1000, bytes_accessed=1000, transcendentals=0),
-    )(sky, beam)
-
-
-def grad_kernel(cuts, sky, beam, *refs):
+    )(sky, beam, held)
+
+
+def grad_kernel(cuts, fars, sky, beam, *refs):
     each, _, skies, degrees = sky.shape
-    direct, far, pooled = refs[:each], refs[each : 2 * each], refs[2 * each : -cuts - 1]
+    direct, far = refs[:each], refs[each : each + fars]
+    pooled = refs[each + fars : -cuts - 1]
     outs, whole = refs[-cuts - 1 : -1], refs[-1]
     classes = beam.shape[2]
     wide = 2 * classes
@@ -142,7 +144,13 @@
     for i in range(each):
         at = slice(i * skies, (i + 1) * skies)
         parity = jnp.where((place * each + i) % 2 == 0, 1.0, -1.0).astype(F32)
-        mine, other = sky[i], far[i][0]
+        mine = sky[i]
+        if i:
+            other = far[0][each - 1 - i + jnp.where(place == 0, 1, 0)]
+        else:
+            block, blocks = lax.axis_index("ma"), lax.axis_size("ma")
+            other = jnp.where((2 * block) % blocks == 0, mine, far[-1][0])
+            other = jnp.where(place == 0, other, far[0][each - 1])
         b_re, b_im = beam[i, 0].astype(F32), beam[i, 1].astype(F32)
         crossed = dot(rows(b_re, b_im), other[0], NT) + dot(rows(b_im, -b_re), other[1], NT)
         resp = direct[i][...] + parity * crossed
@@ -167,8 +175,8 @@
     vmem = pl.BlockSpec(memory_space=pltpu.VMEM)
     shape = (each, 2 * classes, degrees // cuts)
     return pl.pallas_call(
-        functools.partial(grad_kernel, cuts),
-        in_specs=[vmem] * (2 + 2 * each + len(pooled)),
+        functools.partial(grad_kernel, cuts, len(far)),
+        in_specs=[vmem] * (2 + each + len(far) + len(pooled)),
         out_specs=[vmem] * cuts,
         out_shape=[jax.ShapeDtypeStruct(shape, F32)] * cuts,
         scratch_shapes=[pltpu.VMEM((cuts, *shape), F32)],
@@ -207,31 +215,21 @@
     def across(x, r):
         return lax.ppermute(x, ("freq", "bl"), [(c, c ^ r) for c in range(devices)]) if r else x
 
-    def mirror_of(i, sky):
-        return lax.dynamic_slice_in_dim(sky, (slots - (place * each + i)) % slots, 1, 0)
-
-    def mirrored(i, sent):
-        pairs = []
-        for a in range(blocks):
-            for c in range(devices):
-                to = (blocks - a) % blocks if c * each + i == 0 else blocks - 1 - a
-                pairs.append((a * devices + c, to * devices + c))
-        return lax.ppermute(sent, ("ma", "freq", "bl"), pairs)
-
-    last = each - 1
-    sent = mirror_of(last, sky)
-    far = [None] * last + [mirrored(last, sent)]
+    def mirrored(sent, pairs):
+        return lax.ppermute(
+            sent, ("ma", "freq", "bl"), [(a * devices + c, b * devices + c) for a, b, c in pairs]
+        )
+
+    sent = lax.dynamic_slice_in_dim(sky, slots + 1 - (place + 1) * each, each, 0)
+    own = lax.dynamic_slice_in_dim(sky, place * each, each, 0)
+    own_beam = lax.dynamic_slice_in_dim(beam, place * each, each, 0)
+    far = [mirrored(sent, [(a, blocks - 1 - a, c) for a in range(blocks) for c in range(devices)])]
     vis, _ = lax.optimization_barrier((vis, sent))
     sums = pool(vis, fringe, noise, feeds, devices, classes)
-    *sums, later, later_beam = lax.optimization_barrier((*sums, sky, beam))
-    for i in range(last):
-        sent = mirror_of(i, later)
-        far[i] = mirrored(i, sent)
-        *sums, later, later_beam, _ = lax.optimization_barrier((*sums, later, later_beam, sent))
     pooled = [across(x, r) for r, x in enumerate(sums)]
-    own = lax.dynamic_slice_in_dim(later, place * each, each, 0)
-    own_beam = lax.dynamic_slice_in_dim(later_beam, place * each, each, 0)
-    direct = near(own, own_beam)
+    first = lax.optimization_barrier((own, sums[0]))[0][:1]
+    far.append(mirrored(first, [(a, blocks - a, 0) for a in range(1, blocks) if 2 * a != blocks]))
+    pooled[0], *direct = near(own, own_beam, pooled[0])
     cut = gradient(cuts, own, own_beam, direct, far, pooled)
     cut = [across(x, h * cores) for h, x in enumerate(cut)]
     pieces = [across(x, r) for x in cut for r in range(cores)]

time: 28.4 us -> 25.2 us (0.89)
  starting transfers between devices: 11.9 us -> 8.59 us
  waiting for transfers between devices: 5.83 us -> 6.93 us
  local copies, waits for them, and re-layouts: 2.86 us -> 1.86 us
    ppermute x6, starting transfers between devices: 6.15 us -> 2.81 us  [across(): lax.ppermute(x, ('freq', 'bl'), [(c, c ^ r) for c in range(devices)])]
    unnamed x4, local copies, waits for them, and re-layouts: 1.96 us -> 0.74 us
    ppermute x6, waiting for transfers between devices: 5.83 us -> 6.93 us  [across(): lax.ppermute(x, ('freq', 'bl'), [(c, c ^ r) for c in range(devices)])]
    dynamic_slice x4 -> x2, local copies, waits for them, and re-layouts: 0.89 us -> 1.12 us  [the longest x1 1.11 us: body(): lax.dynamic_slice_in_dim(sky, slots + 1 - (place + 1) * each, each, 0)]
  transfers between devices with their start and end apart: 8 -> 8, of which waited for: 4 -> 4; matrix products, arithmetic and copies ran while one was open for 3% -> 0% of each run, Pallas kernels for 21% -> 24%
where the time goes in v3:
time: 25.2 us; the launch traced here: 24.9 us
  starting transfers between devices  8.59 us (34%)
  Pallas kernels  7.47 us (30%)
  waiting for transfers between devices  6.93 us (28%)
  local copies, waits for them, and re-layouts  1.86 us (7%)
    ppermute x6, waiting for transfers between devices, across(): lax.ppermute(x, ('freq', 'bl'), [(c, c ^ r) for c in range(devices)])  6.93 us
    ppermute x2, starting transfers between devices, mirrored(): lax.ppermute(sent, ('ma', 'freq', 'bl'), [(a * devices + c, b * devices +...  5.78 us
    pallas_call x1, Pallas kernels, pool(): pl.pallas_call(functools.partial(pool_kernel, devices, classes), in_specs...  5.68 us
    ppermute x6, starting transfers between devices, across(): lax.ppermute(x, ('freq', 'bl'), [(c, c ^ r) for c in range(devices)])  2.81 us
    dynamic_slice x1, local copies, waits for them, and re-layouts, body(): lax.dynamic_slice_in_dim(sky, slots + 1 - (place + 1) * each, each, 0)  1.11 us
    pallas_call x1, Pallas kernels, gradient(): pl.pallas_call(functools.partial(grad_kernel, cuts, len(far)), in_specs=[...  0.88 us
    unnamed x4, local copies, waits for them, and re-layouts  0.74 us
    pallas_call x1, Pallas kernels, join(): pl.pallas_call(join_kernel, in_specs=[vmem] * len(pieces), out_specs=vmem...  0.73 us
  transfers between devices with their start and end apart: 8, of which 4 were waited for; matrix products, arithmetic and copies ran while one was open for 0% of the time, Pallas kernels for 24%

profile of v3, /device:TPU:0, one launch (start us, length us, event | category | flops | bytes accessed | tf_op | source)
XLA Modules:
  0.0 24.9 jit_solution(753176556970217635)
XLA Ops:
  0.0 0.0 copy-start
  0.0 1.1 %constant_dynamic-slice_fusion = (bf16[2,2,64,512]{3,2,1,0:T(8,128)(2,1)S(1)}, bf16[2,2,64,512]{3,2,1,0:T(8,128)(2,1)S(1)}) fusion(bf16[8,2,64,512]{3,2,1,0:T(8,128)(2,1)} %param.6, s32[]{:T(128)S(6)} %select_n.8, s32[]{:T(128)S(6)} %select_n.7), kind=kLoop, calls=%fused_computation | loop fusion | bytes 1048584 | tf_op jit(solution)/shard_map/dynamic_slice | solution.py:223
  1.1 5.1 %collective-permute-start = (bf16[2,2,64,512]{3,2,1,0:T(8,128)(2,1)S(1)}, bf16[2,2,64,512]{3,2,1,0:T(8,128)(2,1)S(1)}, u32[]{:S(2)}, u32[]{:S(2)}) collective-permute-start(bf16[2,2,64,512]{3,2,1,0:T(8,128)(2,1)S(1)} %get-tuple-element.27), channel_id=1, source_target_pairs={{0,12},{1,13},{2,14},{3,15},{4,8},{5,9},{6,10},{7,11},{8,4},{9,5},... | collective-permute-start | bytes 786440 | tf_op jit(solution)/shard_map/ppermute | solution.py:219
  6.2 5.7 %shard_map.64 = (f32[48,128]{1,0:T(8,128)}, f32[48,128]{1,0:T(8,128)}, f32[48,128]{1,0:T(8,128)}, f32[48,128]{1,0:T(8,128)}) custom-call(bf16[16,8,2,64,256]{4,3,2,1,0:T(8,128)(2,1)} %vis, f32[16,2,256]{2,1,0:T(2,128)} %fringe.1, f32[16,256]{1,0:T(8,128)} %noise.1, s32[1,256]{1,0:T(1,128)} %bitcast.2), custom_call_target="tpu_custom_call" | custom-call | flops 805306368 | bytes 8388608 | tf_op jit(solution)/shard_map/pallas_call | solution.py:90
  11.9 0.7 %collective-permute-start.1 = (bf16[1,2,64,512]{3,2,1,0:T(8,128)(2,1)S(1)}, bf16[1,2,64,512]{3,2,1,0:T(8,128)(2,1)S(1)}, u32[]{:S(2)}, u32[]{:S(2)}) collective-permute-start(bf16[1,2,64,512]{3,2,1,0:T(8,128)(2,1)S(1)} %slice.3), channel_id=1, source_target_pairs={{4,12},{12,4},{20,28},{28,20}} | collective-permute-start | bytes 393224 | tf_op jit(solution)/shard_map/ppermute | solution.py:219
  12.6 0.1 collective-permute-start.2
  12.7 1.6 %collective-permute-start.3 = (f32[48,128]{1,0:T(8,128)}, f32[48,128]{1,0:T(8,128)S(1)}, u32[]{:S(2)}, u32[]{:S(2)}) collective-permute-start(f32[48,128]{1,0:T(8,128)} %get-tuple-element.23), channel_id=1, source_target_pairs={{0,2},{1,3},{2,0},{3,1},{4,6},{5,7},{6,4},{7,5},{8,10},{9,11},{10,... | collective-permute-start | bytes 73736 | tf_op jit(solution)/shard_map/ppermute | solution.py:216
  14.3 0.3 %collective-permute-start.4 = (f32[48,128]{1,0:T(8,128)}, f32[48,128]{1,0:T(8,128)S(1)}, u32[]{:S(2)}, u32[]{:S(2)}) collective-permute-start(f32[48,128]{1,0:T(8,128)} %get-tuple-element.24), channel_id=1, source_target_pairs={{0,3},{1,2},{2,1},{3,0},{4,7},{5,6},{6,5},{7,4},{8,11},{9,10},{10,... | collective-permute-start | bytes 73736 | tf_op jit(solution)/shard_map/ppermute | solution.py:216
  14.6 0.0 copy-done
  14.6 0.0 copy-start.1
  14.6 0.7 %copy-done.1 = f32[48,128]{1,0:T(8,128)S(1)} copy-done((f32[48,128]{1,0:T(8,128)S(1)}, f32[48,128]{1,0:T(8,128)}, u32[]{:S(2)}) %copy-start.1) | copy-done | bytes 24600
  15.3 0.2 shard_map.65
  15.5 0.0 collective-permute-done.2.refs_5_
  15.5 1.3 %collective-permute-done.3.refs_6_ = f32[48,128]{1,0:T(8,128)S(1)} collective-permute-done((f32[48,128]{1,0:T(8,128)}, f32[48,128]{1,0:T(8,128)S(1)}, u32[]{:S(2)}, u32[]{:S(2)}) %collective-permute-start.3) | collective-permute-done | bytes 24608 | tf_op jit(solution)/shard_map/ppermute | solution.py:216
  16.8 0.9 %collective-permute-done.4.refs_7_ = f32[48,128]{1,0:T(8,128)S(1)} collective-permute-done((f32[48,128]{1,0:T(8,128)}, f32[48,128]{1,0:T(8,128)S(1)}, u32[]{:S(2)}, u32[]{:S(2)}) %collective-permute-start.4) | collective-permute-done | bytes 24608 | tf_op jit(solution)/shard_map/ppermute | solution.py:216
  17.7 0.0 collective-permute-done.1.refs_3_
  17.7 0.0 collective-permute-done.refs_2_
  17.7 0.9 %shard_map.66 = (f32[2,32,256]{2,1,0:T(8,128)S(1)}, f32[2,32,256]{2,1,0:T(8,128)S(1)}) custom-call(bf16[2,2,64,512]{3,2,1,0:T(8,128)(2,1)S(1)} %get-tuple-element.20.sky, bf16[2,2,16,512]{3,2,1,0:T(8,128)(2,1)S(1)} %constant_dynamic-slice_fusion.1.beam, f32[32,64]{1,0:T(8,128)S(1)} %get-tuple-element.18.refs_0_, f32[32,64]{1,0:T(8,128)S(1)} %get-tuple-element.19.refs_1_, ...), custom_call_target="tpu_custom_call" | custom-call | tf_op jit(solution)/shard_map/pallas_call | solution.py:177
  18.6 0.9 %collective-permute-start.6 = (f32[2,32,256]{2,1,0:T(8,128)S(1)}, f32[2,32,256]{2,1,0:T(8,128)S(1)}, u32[]{:S(2)}, u32[]{:S(2)}) collective-permute-start(f32[2,32,256]{2,1,0:T(8,128)S(1)} %get-tuple-element.26), channel_id=1, source_target_pairs={{0,2},{1,3},{2,0},{3,1},{4,6},{5,7},{6,4},{7,5},{8,10},{9,11},{10,... | collective-permute-start | bytes 196616 | tf_op jit(solution)/shard_map/ppermute | solution.py:216
  19.5 0.0 collective-permute-start.5
  19.5 3.5 %collective-permute-done.6.refs_2_ = f32[2,32,256]{2,1,0:T(8,128)S(1)} collective-permute-done((f32[2,32,256]{2,1,0:T(8,128)S(1)}, f32[2,32,256]{2,1,0:T(8,128)S(1)}, u32[]{:S(2)}, u32[]{:S(2)}) %collective-permute-start.6) | collective-permute-done | bytes 65568 | tf_op jit(solution)/shard_map/ppermute | solution.py:216
  22.9 0.0 collective-permute-start.7
  22.9 0.0 collective-permute-done.5.refs_1_
  22.9 1.2 %collective-permute-done.7.refs_3_ = f32[2,32,256]{2,1,0:T(8,128)S(1)} collective-permute-done((f32[2,32,256]{2,1,0:T(8,128)S(1)}, f32[2,32,256]{2,1,0:T(8,128)S(1)}, u32[]{:S(2)}, u32[]{:S(2)}) %collective-permute-start.7) | collective-permute-done | bytes 65568 | tf_op jit(solution)/shard_map/ppermute | solution.py:216
  24.2 0.7 %shard_map.67 = f32[8,32,256]{2,1,0:T(8,128)} custom-call(f32[2,32,256]{2,1,0:T(8,128)S(1)} %get-tuple-element.25.refs_0_, f32[2,32,256]{2,1,0:T(8,128)S(1)} %collective-permute-done.5.refs_1_, f32[2,32,256]{2,1,0:T(8,128)S(1)} %collective-permute-done.6.refs_2_, f32[2,32,256]{2,1,0:T(8,128)S(1)} %collective-permute-done.7.refs_3_), custom_call_target="tpu_custom_call" | custom-call | tf_op jit(solution)/shard_map/pallas_call | solution.py:198
  (2 shorter events, 0.0 us)
Async XLA Ops:
  0.0 14.6 %copy-start = (bf16[8,2,16,512]{3,2,1,0:T(8,128)(2,1)S(1)}, bf16[8,2,16,512]{3,2,1,0:T(8,128)(2,1)}, u32[]{:S(2)}) copy-start(bf16[8,2,16,512]{3,2,1,0:T(8,128)(2,1)} %param.7) | copy-start | bytes 786436
  1.1 16.6 %collective-permute-start = (bf16[2,2,64,512]{3,2,1,0:T(8,128)(2,1)S(1)}, bf16[2,2,64,512]{3,2,1,0:T(8,128)(2,1)S(1)}, u32[]{:S(2)}, u32[]{:S(2)}) collective-permute-start(bf16[2,2,64,512]{3,2,1,0:T(8,128)(2,1)S(1)} %get-tuple-element.27), channel_id=1, source_target_pairs={{0,12},{1,13},{2,14},{3,15},{4,8},{5,9},{6,10},{7,11},{8,4},{9,5},... | collective-permute-start | bytes 786440 | tf_op jit(solution)/shard_map/ppermute | solution.py:219
  11.9 5.8 %collective-permute-start.1 = (bf16[1,2,64,512]{3,2,1,0:T(8,128)(2,1)S(1)}, bf16[1,2,64,512]{3,2,1,0:T(8,128)(2,1)S(1)}, u32[]{:S(2)}, u32[]{:S(2)}) collective-permute-start(bf16[1,2,64,512]{3,2,1,0:T(8,128)(2,1)S(1)} %slice.3), channel_id=1, source_target_pairs={{4,12},{12,4},{20,28},{28,20}} | collective-permute-start | bytes 393224 | tf_op jit(solution)/shard_map/ppermute | solution.py:219
  12.6 2.9 %collective-permute-start.2 = (f32[48,128]{1,0:T(8,128)}, f32[48,128]{1,0:T(8,128)S(1)}, u32[]{:S(2)}, u32[]{:S(2)}) collective-permute-start(f32[48,128]{1,0:T(8,128)} %get-tuple-element.22), channel_id=1, source_target_pairs={{0,1},{1,0},{2,3},{3,2},{4,5},{5,4},{6,7},{7,6},{8,9},{9,8},{10,11... | collective-permute-start | bytes 73736 | tf_op jit(solution)/shard_map/ppermute | solution.py:216
  12.7 4.1 %collective-permute-start.3 = (f32[48,128]{1,0:T(8,128)}, f32[48,128]{1,0:T(8,128)S(1)}, u32[]{:S(2)}, u32[]{:S(2)}) collective-permute-start(f32[48,128]{1,0:T(8,128)} %get-tuple-element.23), channel_id=1, source_target_pairs={{0,2},{1,3},{2,0},{3,1},{4,6},{5,7},{6,4},{7,5},{8,10},{9,11},{10,... | collective-permute-start | bytes 73736 | tf_op jit(solution)/shard_map/ppermute | solution.py:216
  14.3 3.5 %collective-permute-start.4 = (f32[48,128]{1,0:T(8,128)}, f32[48,128]{1,0:T(8,128)S(1)}, u32[]{:S(2)}, u32[]{:S(2)}) collective-permute-start(f32[48,128]{1,0:T(8,128)} %get-tuple-element.24), channel_id=1, source_target_pairs={{0,3},{1,2},{2,1},{3,0},{4,7},{5,6},{6,5},{7,4},{8,11},{9,10},{10,... | collective-permute-start | bytes 73736 | tf_op jit(solution)/shard_map/ppermute | solution.py:216
  14.6 0.7 %copy-start.1 = (f32[48,128]{1,0:T(8,128)S(1)}, f32[48,128]{1,0:T(8,128)}, u32[]{:S(2)}) copy-start(f32[48,128]{1,0:T(8,128)} %get-tuple-element.17.held) | copy-start | bytes 73732
  18.6 4.3 %collective-permute-start.6 = (f32[2,32,256]{2,1,0:T(8,128)S(1)}, f32[2,32,256]{2,1,0:T(8,128)S(1)}, u32[]{:S(2)}, u32[]{:S(2)}) collective-permute-start(f32[2,32,256]{2,1,0:T(8,128)S(1)} %get-tuple-element.26), channel_id=1, source_target_pairs={{0,2},{1,3},{2,0},{3,1},{4,6},{5,7},{6,4},{7,5},{8,10},{9,11},{10,... | collective-permute-start | bytes 196616 | tf_op jit(solution)/shard_map/ppermute | solution.py:216
  19.5 3.5 %collective-permute-start.5 = (f32[2,32,256]{2,1,0:T(8,128)S(1)}, f32[2,32,256]{2,1,0:T(8,128)S(1)}, u32[]{:S(2)}, u32[]{:S(2)}) collective-permute-start(f32[2,32,256]{2,1,0:T(8,128)S(1)} %get-tuple-element.25.refs_0_), channel_id=1, source_target_pairs={{0,1},{1,0},{2,3},{3,2},{4,5},{5,4},{6,7},{7,6},{8,9},{9,8},{10,11... | collective-permute-start | bytes 196616 | tf_op jit(solution)/shard_map/ppermute | solution.py:216
  22.9 1.3 %collective-permute-start.7 = (f32[2,32,256]{2,1,0:T(8,128)S(1)}, f32[2,32,256]{2,1,0:T(8,128)S(1)}, u32[]{:S(2)}, u32[]{:S(2)}) collective-permute-start(f32[2,32,256]{2,1,0:T(8,128)S(1)} %collective-permute-done.6.refs_2_), channel_id=1, source_target_pairs={{0,1},{1,0},{2,3},{3,2},{4,5},{5,4},{6,7},{7,6},{8,9},{9,8},{10,11... | collective-permute-start | bytes 196616 | tf_op jit(solution)/shard_map/ppermute | solution.py:216

commit v4 on v3

--- a/solution.py
+++ b/solution.py
@@ -108,59 +108,76 @@
     )(vis, fringe, noise, feeds)
 
 
-def near_kernel(sky, beam, held, passed, *outs):
-    passed[...] = held[...]
+def hold_kernel(x, out):
+    out[...] = x[...]
+
+
+def hold(x):
+    vmem = pl.BlockSpec(memory_space=pltpu.VMEM)
+    return pl.pallas_call(
+        hold_kernel,
+        in_specs=[vmem],
+        out_specs=vmem,
+        out_shape=jax.ShapeDtypeStruct(x.shape, x.dtype),
+        compiler_params=pltpu.CompilerParams(vmem_limit_bytes=8 << 20),
+    )(x)
+
+
+def mirror(far, sky, i):
+    each = sky.shape[0]
+    first = my_place() == 0
+    if i:
+        return far[0][each - 1 - i + jnp.where(first, 1, 0)]
+    block, blocks = lax.axis_index("ma"), lax.axis_size("ma")
+    other = jnp.where((2 * block) % blocks == 0, sky[i], far[1][0])
+    return jnp.where(first, other, far[0][each - 1])
+
+
+def parity_of(slot):
+    return jnp.where(slot % 2 == 0, 1.0, -1.0).astype(F32)
+
+
+def response_kernel(sky, beam, first, second, *outs):
     for i, out in enumerate(outs):
+        other = mirror((first, second), sky, i)
         b_re, b_im = beam[i, 0].astype(F32), beam[i, 1].astype(F32)
-        out[...] = dot(rows(b_re, b_im), sky[i, 0], NT) + dot(rows(-b_im, b_re), sky[i, 1], NT)
-
-
-def near(sky, beam, held):
+        direct = dot(rows(b_re, b_im), sky[i, 0], NT) + dot(rows(-b_im, b_re), sky[i, 1], NT)
+        crossed = dot(rows(b_re, b_im), other[0], NT) + dot(rows(b_im, -b_re), other[1], NT)
+        out[...] = direct + parity_of(my_place() * len(outs) + i) * crossed
+
+
+def response(sky, beam, far):
     each, _, skies, _ = sky.shape
     vmem = pl.BlockSpec(memory_space=pltpu.VMEM)
     return pl.pallas_call(
-        near_kernel,
-        in_specs=[vmem] * 3,
-        out_specs=[vmem] * (each + 1),
-        out_shape=[jax.ShapeDtypeStruct(held.shape, F32)]
-        + [jax.ShapeDtypeStruct((2 * beam.shape[2], skies), F32)] * each,
-        compiler_params=pltpu.CompilerParams(vmem_limit_bytes=8 << 20),
-    )(sky, beam, held)
-
-
-def grad_kernel(cuts, fars, sky, beam, *refs):
+        response_kernel,
+        in_specs=[vmem] * (2 + len(far)),
+        out_specs=[vmem] * each,
+        out_shape=[jax.ShapeDtypeStruct((2 * beam.shape[2], skies), F32)] * each,
+        compiler_params=pltpu.CompilerParams(vmem_limit_bytes=8 << 20),
+    )(sky, beam, *far)
+
+
+def grad_kernel(cuts, devices, sky, first, second, *refs):
     each, _, skies, degrees = sky.shape
-    direct, far = refs[:each], refs[each : each + fars]
-    pooled = refs[each + fars : -cuts - 1]
-    outs, whole = refs[-cuts - 1 : -1], refs[-1]
-    classes = beam.shape[2]
-    wide = 2 * classes
+    found, pooled, outs, whole = refs[:each], refs[each : each + devices], refs[each + devices : -1], refs[-1]
+    wide = found[0].shape[0]
+    classes = wide // 2
     step = degrees // cuts
-    place = my_place()
-    sums = pooled[0][...]
-    for ref in pooled[1:]:
-        sums = sums + ref[...]
+    sums = functools.reduce(jnp.add, [ref[...] for ref in pooled])
     gain = 0.5 * sums[wide:]
     for i in range(each):
         at = slice(i * skies, (i + 1) * skies)
-        parity = jnp.where((place * each + i) % 2 == 0, 1.0, -1.0).astype(F32)
-        mine = sky[i]
-        if i:
-            other = far[0][each - 1 - i + jnp.where(place == 0, 1, 0)]
-        else:
-            block, blocks = lax.axis_index("ma"), lax.axis_size("ma")
-            other = jnp.where((2 * block) % blocks == 0, mine, far[-1][0])
-            other = jnp.where(place == 0, other, far[0][each - 1])
-        b_re, b_im = beam[i, 0].astype(F32), beam[i, 1].astype(F32)
-        crossed = dot(rows(b_re, b_im), other[0], NT) + dot(rows(b_im, -b_re), other[1], NT)
-        resp = direct[i][...] + parity * crossed
+        parity = parity_of(my_place() * each + i)
+        other = mirror((first, second), sky, i)
+        resp = found[i][...]
         p_re = 0.5 * (gain[:, at] * resp[:classes] - sums[:classes, at])
         p_im = 0.5 * (gain[:, at] * resp[classes:] - sums[classes:wide, at])
         own = jnp.concatenate([jnp.concatenate([p_re, p_im], 1), jnp.concatenate([p_im, -p_re], 1)], 0)
         away = parity * jnp.concatenate([jnp.concatenate([p_re, -p_im], 1), jnp.concatenate([p_im, p_re], 1)], 0)
         own = jnp.concatenate(split3(own), 0)
         away = jnp.concatenate(split3(away), 0)
-        grad = dot(own, mine.reshape(2 * skies, degrees), NN) + dot(away, other.reshape(2 * skies, degrees), NN)
+        grad = dot(own, sky[i].reshape(2 * skies, degrees), NN) + dot(away, other.reshape(2 * skies, degrees), NN)
         grad = grad[:wide] + grad[wide : 2 * wide] + grad[2 * wide :]
         for h in range(cuts):
             whole[h, i] = grad[:, h * step : (h + 1) * step]
@@ -169,39 +186,47 @@
         outs[h][...] = whole[row ^ h]
 
 
-def gradient(cuts, sky, beam, direct, far, pooled):
-    each = sky.shape[0]
-    classes, degrees = beam.shape[2:]
-    vmem = pl.BlockSpec(memory_space=pltpu.VMEM)
-    shape = (each, 2 * classes, degrees // cuts)
-    return pl.pallas_call(
-        functools.partial(grad_kernel, cuts, len(far)),
-        in_specs=[vmem] * (2 + each + len(far) + len(pooled)),
+def gradient(cuts, sky, far, found, pooled):
+    each, _, _, degrees = sky.shape
+    vmem = pl.BlockSpec(memory_space=pltpu.VMEM)
+    shape = (each, found[0].shape[0], degrees // cuts)
+    return pl.pallas_call(
+        functools.partial(grad_kernel, cuts, len(pooled)),
+        in_specs=[vmem] * (1 + len(far) + each + len(pooled)),
         out_specs=[vmem] * cuts,
         out_shape=[jax.ShapeDtypeStruct(shape, F32)] * cuts,
         scratch_shapes=[pltpu.VMEM((cuts, *shape), F32)],
         compiler_params=pltpu.CompilerParams(vmem_limit_bytes=8 << 20),
-    )(sky, beam, *direct, *far, *pooled)
-
-
-def join_kernel(*refs):
-    pieces, out = refs[:-1], refs[-1]
+    )(sky, *far, *found, *pooled)
+
+
+def join_kernel(ranks, *refs):
+    pieces, out, sems = refs[: len(ranks)], refs[-2], refs[-1]
     each = pieces[0].shape[0]
     place = my_place()
-    for r, piece in enumerate(pieces):
-        out[pl.ds((place ^ r) * each, each)] = piece[...]
-
-
-def join(pieces):
+    copies = [
+        pltpu.make_async_copy(piece, out.at[pl.ds((place ^ r) * each, each)], sems.at[n])
+        for n, (r, piece) in enumerate(zip(ranks, pieces))
+    ]
+    for copy in copies:
+        copy.start()
+    for copy in copies:
+        copy.wait()
+
+
+def join(devices, ranks, pieces, begun=None):
     each, wide, step = pieces[0].shape
-    vmem = pl.BlockSpec(memory_space=pltpu.VMEM)
-    return pl.pallas_call(
-        join_kernel,
-        in_specs=[vmem] * len(pieces),
-        out_specs=vmem,
-        out_shape=jax.ShapeDtypeStruct((each * len(pieces), wide, step), F32),
-        compiler_params=pltpu.CompilerParams(vmem_limit_bytes=8 << 20),
-    )(*pieces)
+    more = [] if begun is None else [begun]
+    anywhere = pl.BlockSpec(memory_space=pl.ANY)
+    return pl.pallas_call(
+        functools.partial(join_kernel, ranks),
+        in_specs=[pl.BlockSpec(memory_space=pltpu.VMEM)] * len(pieces) + [anywhere] * len(more),
+        out_specs=anywhere,
+        out_shape=jax.ShapeDtypeStruct((each * devices, wide, step), F32),
+        scratch_shapes=[pltpu.SemaphoreType.DMA((len(pieces),))],
+        input_output_aliases={len(pieces): 0} if more else {},
+        compiler_params=pltpu.CompilerParams(vmem_limit_bytes=8 << 20),
+    )(*pieces, *more)
 
 
 def body(sky, beam, vis, fringe, noise, feeds):
@@ -229,11 +254,16 @@
     pooled = [across(x, r) for r, x in enumerate(sums)]
     first = lax.optimization_barrier((own, sums[0]))[0][:1]
     far.append(mirrored(first, [(a, blocks - a, 0) for a in range(1, blocks) if 2 * a != blocks]))
-    pooled[0], *direct = near(own, own_beam, pooled[0])
-    cut = gradient(cuts, own, own_beam, direct, far, pooled)
+    pooled[0] = hold(pooled[0])
+    found = response(own, own_beam, far)
+    cut = gradient(cuts, own, far, found, pooled)
     cut = [across(x, h * cores) for h, x in enumerate(cut)]
     pieces = [across(x, r) for x in cut for r in range(cores)]
-    out = join(pieces)
+    early = [r for r in range(devices) if r < cores or r % cores == 0]
+    late = [r for r in range(devices) if r not in early]
+    out = join(devices, early, [pieces[r] for r in early])
+    if late:
+        out = join(devices, late, [pieces[r] for r in late], out)
     return out.reshape(slots, 2, classes, out.shape[-1])
 
 

time: 25.2 us -> 24.5 us (0.972)
  waiting for transfers between devices: 6.93 us -> 6.12 us
    ppermute x6, waiting for transfers between devices: 6.93 us -> 6.11 us  [across(): lax.ppermute(x, ('freq', 'bl'), [(c, c ^ r) for c in range(devices)])]
    pallas_call x3 -> x5, Pallas kernels: 1.79 us -> 1.95 us  [the longest x2 1.34 us: join(): pl.pallas_call(functools.partial(join_kernel, ranks), in_specs=[pl.BlockS...]
  transfers between devices with their start and end apart: 8 -> 8, of which waited for: 4 -> 4; matrix products, arithmetic and copies ran while one was open for 0% -> 0% of each run, Pallas kernels for 24% -> 27%
where the time goes in v4:
time: 24.5 us; the launch traced here: 24.3 us
  starting transfers between devices  8.59 us (35%)
  Pallas kernels  7.62 us (31%)
  waiting for transfers between devices  6.12 us (25%)
  local copies, waits for them, and re-layouts  1.86 us (8%)
    ppermute x6, waiting for transfers between devices, across(): lax.ppermute(x, ('freq', 'bl'), [(c, c ^ r) for c in range(devices)])  6.11 us
    ppermute x2, starting transfers between devices, mirrored(): lax.ppermute(sent, ('ma', 'freq', 'bl'), [(a * devices + c, b * devices +...  5.78 us
    pallas_call x1, Pallas kernels, pool(): pl.pallas_call(functools.partial(pool_kernel, devices, classes), in_specs...  5.68 us
    ppermute x6, starting transfers between devices, across(): lax.ppermute(x, ('freq', 'bl'), [(c, c ^ r) for c in range(devices)])  2.81 us
    pallas_call x2, Pallas kernels, join(): pl.pallas_call(functools.partial(join_kernel, ranks), in_specs=[pl.BlockS...  1.34 us
    dynamic_slice x1, local copies, waits for them, and re-layouts, body(): lax.dynamic_slice_in_dim(sky, slots + 1 - (place + 1) * each, each, 0)  1.11 us
    unnamed x4, local copies, waits for them, and re-layouts  0.74 us
  transfers between devices with their start and end apart: 8, of which 4 were waited for; matrix products, arithmetic and copies ran while one was open for 0% of the time, Pallas kernels for 27%

profile of v4, /device:TPU:0, one launch (start us, length us, event | category | flops | bytes accessed | tf_op | source)
XLA Modules:
  0.0 24.3 jit_solution(16045631403965636220)
XLA Ops:
  0.0 0.0 copy-start
  0.0 1.1 %constant_dynamic-slice_fusion.1 = (bf16[2,2,64,512]{3,2,1,0:T(8,128)(2,1)S(1)}, bf16[2,2,64,512]{3,2,1,0:T(8,128)(2,1)S(1)}) fusion(bf16[8,2,64,512]{3,2,1,0:T(8,128)(2,1)} %param.6, s32[]{:T(128)S(6)} %select_n.8, s32[]{:T(128)S(6)} %select_n.7), kind=kLoop, calls=%fused_computation.1 | loop fusion | bytes 1048584 | tf_op jit(solution)/shard_map/dynamic_slice | solution.py:248
  1.1 5.1 %collective-permute-start = (bf16[2,2,64,512]{3,2,1,0:T(8,128)(2,1)S(1)}, bf16[2,2,64,512]{3,2,1,0:T(8,128)(2,1)S(1)}, u32[]{:S(2)}, u32[]{:S(2)}) collective-permute-start(bf16[2,2,64,512]{3,2,1,0:T(8,128)(2,1)S(1)} %get-tuple-element.25), channel_id=1, source_target_pairs={{0,12},{1,13},{2,14},{3,15},{4,8},{5,9},{6,10},{7,11},{8,4},{9,5},... | collective-permute-start | bytes 786440 | tf_op jit(solution)/shard_map/ppermute | solution.py:244
  6.2 5.7 %shard_map.64 = (f32[48,128]{1,0:T(8,128)}, f32[48,128]{1,0:T(8,128)}, f32[48,128]{1,0:T(8,128)}, f32[48,128]{1,0:T(8,128)}) custom-call(bf16[16,8,2,64,256]{4,3,2,1,0:T(8,128)(2,1)} %vis, f32[16,2,256]{2,1,0:T(2,128)} %fringe.1, f32[16,256]{1,0:T(8,128)} %noise.1, s32[1,256]{1,0:T(1,128)} %bitcast.2), custom_call_target="tpu_custom_call" | custom-call | flops 805306368 | bytes 8388608 | tf_op jit(solution)/shard_map/pallas_call | solution.py:90
  11.9 0.7 %collective-permute-start.1 = (bf16[1,2,64,512]{3,2,1,0:T(8,128)(2,1)S(1)}, bf16[1,2,64,512]{3,2,1,0:T(8,128)(2,1)S(1)}, u32[]{:S(2)}, u32[]{:S(2)}) collective-permute-start(bf16[1,2,64,512]{3,2,1,0:T(8,128)(2,1)S(1)} %slice.3), channel_id=1, source_target_pairs={{4,12},{12,4},{20,28},{28,20}} | collective-permute-start | bytes 393224 | tf_op jit(solution)/shard_map/ppermute | solution.py:244
  12.6 0.1 collective-permute-start.2
  12.7 1.6 %collective-permute-start.3 = (f32[48,128]{1,0:T(8,128)}, f32[48,128]{1,0:T(8,128)S(1)}, u32[]{:S(2)}, u32[]{:S(2)}) collective-permute-start(f32[48,128]{1,0:T(8,128)} %get-tuple-element.21), channel_id=1, source_target_pairs={{0,2},{1,3},{2,0},{3,1},{4,6},{5,7},{6,4},{7,5},{8,10},{9,11},{10,... | collective-permute-start | bytes 73736 | tf_op jit(solution)/shard_map/ppermute | solution.py:241
  14.3 0.3 %collective-permute-start.4 = (f32[48,128]{1,0:T(8,128)}, f32[48,128]{1,0:T(8,128)S(1)}, u32[]{:S(2)}, u32[]{:S(2)}) collective-permute-start(f32[48,128]{1,0:T(8,128)} %get-tuple-element.22), channel_id=1, source_target_pairs={{0,3},{1,2},{2,1},{3,0},{4,7},{5,6},{6,5},{7,4},{8,11},{9,10},{10,... | collective-permute-start | bytes 73736 | tf_op jit(solution)/shard_map/ppermute | solution.py:241
  14.6 0.0 copy-done
  14.6 0.0 copy-start.1
  14.6 0.7 %copy-done.1 = f32[48,128]{1,0:T(8,128)S(1)} copy-done((f32[48,128]{1,0:T(8,128)S(1)}, f32[48,128]{1,0:T(8,128)}, u32[]{:S(2)}) %copy-start.1) | copy-done | bytes 24600
  15.3 0.0 collective-permute-done.1.second
  15.3 0.0 collective-permute-done.first
  15.3 0.3 %shard_map.65 = (f32[32,64]{1,0:T(8,128)S(1)}, f32[32,64]{1,0:T(8,128)S(1)}) custom-call(bf16[2,2,64,512]{3,2,1,0:T(8,128)(2,1)S(1)} %get-tuple-element.17.sky, bf16[2,2,16,512]{3,2,1,0:T(8,128)(2,1)S(1)} %constant_dynamic-slice_fusion.beam, bf16[2,2,64,512]{3,2,1,0:T(8,128)(2,1)S(1)} %collective-permute-done.first, ...), custom_call_target="tpu_custom_call" | custom-call | tf_op jit(solution)/shard_map/pallas_call | solution.py:152
  15.6 0.0 collective-permute-done.2.refs_3_
  15.6 1.2 %collective-permute-done.3.refs_4_ = f32[48,128]{1,0:T(8,128)S(1)} collective-permute-done((f32[48,128]{1,0:T(8,128)}, f32[48,128]{1,0:T(8,128)S(1)}, u32[]{:S(2)}, u32[]{:S(2)}) %collective-permute-start.3) | collective-permute-done | bytes 24608 | tf_op jit(solution)/shard_map/ppermute | solution.py:241
  16.8 0.9 %collective-permute-done.4.refs_5_ = f32[48,128]{1,0:T(8,128)S(1)} collective-permute-done((f32[48,128]{1,0:T(8,128)}, f32[48,128]{1,0:T(8,128)S(1)}, u32[]{:S(2)}, u32[]{:S(2)}) %collective-permute-start.4) | collective-permute-done | bytes 24608 | tf_op jit(solution)/shard_map/ppermute | solution.py:241
  17.7 0.3 %shard_map.67 = (f32[2,32,256]{2,1,0:T(8,128)S(1)}, f32[2,32,256]{2,1,0:T(8,128)S(1)}) custom-call(bf16[2,2,64,512]{3,2,1,0:T(8,128)(2,1)S(1)} %get-tuple-element.17.sky, bf16[2,2,64,512]{3,2,1,0:T(8,128)(2,1)S(1)} %collective-permute-done.first, bf16[1,2,64,512]{3,2,1,0:T(8,128)(2,1)S(1)} %collective-permute-done.1.second, ...), custom_call_target="tpu_custom_call" | custom-call | tf_op jit(solution)/shard_map/pallas_call | solution.py:193
  18.1 0.9 %collective-permute-start.5 = (f32[2,32,256]{2,1,0:T(8,128)S(1)}, f32[2,32,256]{2,1,0:T(8,128)S(1)}, u32[]{:S(2)}, u32[]{:S(2)}) collective-permute-start(f32[2,32,256]{2,1,0:T(8,128)S(1)} %get-tuple-element.23), channel_id=1, source_target_pairs={{0,2},{1,3},{2,0},{3,1},{4,6},{5,7},{6,4},{7,5},{8,10},{9,11},{10,... | collective-permute-start | bytes 196616 | tf_op jit(solution)/shard_map/ppermute | solution.py:241
  18.9 0.0 collective-permute-start.7
  18.9 3.5 %collective-permute-done.5.refs_2_ = f32[2,32,256]{2,1,0:T(8,128)S(1)} collective-permute-done((f32[2,32,256]{2,1,0:T(8,128)S(1)}, f32[2,32,256]{2,1,0:T(8,128)S(1)}, u32[]{:S(2)}, u32[]{:S(2)}) %collective-permute-start.5) | collective-permute-done | bytes 65568 | tf_op jit(solution)/shard_map/ppermute | solution.py:241
  22.4 0.0 collective-permute-start.6
  22.4 0.0 collective-permute-done.7.refs_1_
  22.4 0.7 %shard_map.68.refs_1_ = f32[8,32,256]{2,1,0:T(8,128)} custom-call(f32[2,32,256]{2,1,0:T(8,128)S(1)} %get-tuple-element.24.refs_0_, f32[2,32,256]{2,1,0:T(8,128)S(1)} %collective-permute-done.7.refs_1_, f32[2,32,256]{2,1,0:T(8,128)S(1)} %collective-permute-done.5.refs_2_), custom_call_target="tpu_custom_call" | custom-call | tf_op jit(solution)/shard_map/pallas_call | solution.py:221
  23.1 0.5 %collective-permute-done.6.refs_0_ = f32[2,32,256]{2,1,0:T(8,128)S(1)} collective-permute-done((f32[2,32,256]{2,1,0:T(8,128)S(1)}, f32[2,32,256]{2,1,0:T(8,128)S(1)}, u32[]{:S(2)}, u32[]{:S(2)}) %collective-permute-start.6) | collective-permute-done | bytes 65568 | tf_op jit(solution)/shard_map/ppermute | solution.py:241
  23.6 0.6 %shard_map.69 = f32[8,32,256]{2,1,0:T(8,128)} custom-call(f32[2,32,256]{2,1,0:T(8,128)S(1)} %collective-permute-done.6.refs_0_, f32[8,32,256]{2,1,0:T(8,128)} %shard_map.68.refs_1_), custom_call_target="tpu_custom_call", output_to_operand_aliasing={{}: (1, {})} | custom-call | tf_op jit(solution)/shard_map/pallas_call | solution.py:221
  (3 shorter events, 0.0 us)
Async XLA Ops:
  0.0 14.6 %copy-start = (bf16[8,2,16,512]{3,2,1,0:T(8,128)(2,1)S(1)}, bf16[8,2,16,512]{3,2,1,0:T(8,128)(2,1)}, u32[]{:S(2)}) copy-start(bf16[8,2,16,512]{3,2,1,0:T(8,128)(2,1)} %param.7) | copy-start | bytes 786436
  1.1 14.2 %collective-permute-start = (bf16[2,2,64,512]{3,2,1,0:T(8,128)(2,1)S(1)}, bf16[2,2,64,512]{3,2,1,0:T(8,128)(2,1)S(1)}, u32[]{:S(2)}, u32[]{:S(2)}) collective-permute-start(bf16[2,2,64,512]{3,2,1,0:T(8,128)(2,1)S(1)} %get-tuple-element.25), channel_id=1, source_target_pairs={{0,12},{1,13},{2,14},{3,15},{4,8},{5,9},{6,10},{7,11},{8,4},{9,5},... | collective-permute-start | bytes 786440 | tf_op jit(solution)/shard_map/ppermute | solution.py:244
  11.9 3.4 %collective-permute-start.1 = (bf16[1,2,64,512]{3,2,1,0:T(8,128)(2,1)S(1)}, bf16[1,2,64,512]{3,2,1,0:T(8,128)(2,1)S(1)}, u32[]{:S(2)}, u32[]{:S(2)}) collective-permute-start(bf16[1,2,64,512]{3,2,1,0:T(8,128)(2,1)S(1)} %slice.3), channel_id=1, source_target_pairs={{4,12},{12,4},{20,28},{28,20}} | collective-permute-start | bytes 393224 | tf_op jit(solution)/shard_map/ppermute | solution.py:244
  12.6 3.0 %collective-permute-start.2 = (f32[48,128]{1,0:T(8,128)}, f32[48,128]{1,0:T(8,128)S(1)}, u32[]{:S(2)}, u32[]{:S(2)}) collective-permute-start(f32[48,128]{1,0:T(8,128)} %get-tuple-element.20), channel_id=1, source_target_pairs={{0,1},{1,0},{2,3},{3,2},{4,5},{5,4},{6,7},{7,6},{8,9},{9,8},{10,11... | collective-permute-start | bytes 73736 | tf_op jit(solution)/shard_map/ppermute | solution.py:241
  12.7 4.1 %collective-permute-start.3 = (f32[48,128]{1,0:T(8,128)}, f32[48,128]{1,0:T(8,128)S(1)}, u32[]{:S(2)}, u32[]{:S(2)}) collective-permute-start(f32[48,128]{1,0:T(8,128)} %get-tuple-element.21), channel_id=1, source_target_pairs={{0,2},{1,3},{2,0},{3,1},{4,6},{5,7},{6,4},{7,5},{8,10},{9,11},{10,... | collective-permute-start | bytes 73736 | tf_op jit(solution)/shard_map/ppermute | solution.py:241
  14.3 3.5 %collective-permute-start.4 = (f32[48,128]{1,0:T(8,128)}, f32[48,128]{1,0:T(8,128)S(1)}, u32[]{:S(2)}, u32[]{:S(2)}) collective-permute-start(f32[48,128]{1,0:T(8,128)} %get-tuple-element.22), channel_id=1, source_target_pairs={{0,3},{1,2},{2,1},{3,0},{4,7},{5,6},{6,5},{7,4},{8,11},{9,10},{10,... | collective-permute-start | bytes 73736 | tf_op jit(solution)/shard_map/ppermute | solution.py:241
  14.6 0.7 %copy-start.1 = (f32[48,128]{1,0:T(8,128)S(1)}, f32[48,128]{1,0:T(8,128)}, u32[]{:S(2)}) copy-start(f32[48,128]{1,0:T(8,128)} %get-tuple-element.16.x) | copy-start | bytes 73732
  18.1 4.3 %collective-permute-start.5 = (f32[2,32,256]{2,1,0:T(8,128)S(1)}, f32[2,32,256]{2,1,0:T(8,128)S(1)}, u32[]{:S(2)}, u32[]{:S(2)}) collective-permute-start(f32[2,32,256]{2,1,0:T(8,128)S(1)} %get-tuple-element.23), channel_id=1, source_target_pairs={{0,2},{1,3},{2,0},{3,1},{4,6},{5,7},{6,4},{7,5},{8,10},{9,11},{10,... | collective-permute-start | bytes 196616 | tf_op jit(solution)/shard_map/ppermute | solution.py:241
  18.9 3.5 %collective-permute-start.7 = (f32[2,32,256]{2,1,0:T(8,128)S(1)}, f32[2,32,256]{2,1,0:T(8,128)S(1)}, u32[]{:S(2)}, u32[]{:S(2)}) collective-permute-start(f32[2,32,256]{2,1,0:T(8,128)S(1)} %get-tuple-element.24.refs_0_), channel_id=1, source_target_pairs={{0,1},{1,0},{2,3},{3,2},{4,5},{5,4},{6,7},{7,6},{8,9},{9,8},{10,11... | collective-permute-start | bytes 196616 | tf_op jit(solution)/shard_map/ppermute | solution.py:241
  22.4 1.3 %collective-permute-start.6 = (f32[2,32,256]{2,1,0:T(8,128)S(1)}, f32[2,32,256]{2,1,0:T(8,128)S(1)}, u32[]{:S(2)}, u32[]{:S(2)}) collective-permute-start(f32[2,32,256]{2,1,0:T(8,128)S(1)} %collective-permute-done.5.refs_2_), channel_id=1, source_target_pairs={{0,1},{1,0},{2,3},{3,2},{4,5},{5,4},{6,7},{7,6},{8,9},{9,8},{10,11... | collective-permute-start | bytes 196616 | tf_op jit(solution)/shard_map/ppermute | solution.py:241

commit v5 on v4

--- a/solution.py
+++ b/solution.py
@@ -9,7 +9,8 @@
 
 BF = jnp.bfloat16
 F32 = jnp.float32
-AHEAD = 6
+FIRST = 5
+AHEAD = 10
 NT = (((1,), (1,)), ((), ()))
 NN = (((1,), (0,)), ((), ()))
 
@@ -43,10 +44,12 @@
         for i, (src, dst) in enumerate([(feeds, feeds_v), (fringe, fringe_v), (noise, noise_v)])
     ]
     copies = [pltpu.make_async_copy(vis.at[f], buf.at[f], sems.at[f]) for f in range(channels)]
-    for copy in little + copies[:ahead]:
+    for copy in little + copies[:FIRST]:
         copy.start()
     for copy in little:
         copy.wait()
+    for copy in copies[FIRST:ahead]:
+        copy.start()
     onehot = lax.broadcasted_iota(jnp.int32, (classes, lines), 0) == feeds_v[...]
     weight = noise_v[...]
     real = fringe_v[:, 0, :]
@@ -251,10 +254,11 @@
     far = [mirrored(sent, [(a, blocks - 1 - a, c) for a in range(blocks) for c in range(devices)])]
     vis, _ = lax.optimization_barrier((vis, sent))
     sums = pool(vis, fringe, noise, feeds, devices, classes)
-    pooled = [across(x, r) for r, x in enumerate(sums)]
+    pooled = [across(sums[r], r) for r in sorted(range(devices), key=lambda r: r < cores)]
     first = lax.optimization_barrier((own, sums[0]))[0][:1]
     far.append(mirrored(first, [(a, blocks - a, 0) for a in range(1, blocks) if 2 * a != blocks]))
-    pooled[0] = hold(pooled[0])
+    at = next(n for n, x in enumerate(pooled) if x is sums[0])
+    pooled[at] = hold(sums[0])
     found = response(own, own_beam, far)
     cut = gradient(cuts, own, far, found, pooled)
     cut = [across(x, h * cores) for h, x in enumerate(cut)]

time: 24.5 us -> 24.2 us (0.988)
  waiting for transfers between devices: 6.12 us -> 5.81 us
  starting transfers between devices: 8.59 us -> 8.85 us
    ppermute x6, waiting for transfers between devices: 6.11 us -> 5.81 us  [across(): lax.ppermute(x, ('freq', 'bl'), [(c, c ^ r) for c in range(devices)])]
    ppermute x6, starting transfers between devices: 2.81 us -> 3.06 us  [across(): lax.ppermute(x, ('freq', 'bl'), [(c, c ^ r) for c in range(devices)])]
where the time goes in v5:
time: 24.2 us; the launch traced here: 24 us
  starting transfers between devices  8.85 us (37%)
  Pallas kernels  7.38 us (30%)
  waiting for transfers between devices  5.81 us (24%)
  local copies, waits for them, and re-layouts  1.86 us (8%)
    ppermute x6, waiting for transfers between devices, across(): lax.ppermute(x, ('freq', 'bl'), [(c, c ^ r) for c in range(devices)])  5.81 us
    ppermute x2, starting transfers between devices, mirrored(): lax.ppermute(sent, ('ma', 'freq', 'bl'), [(a * devices + c, b * devices +...  5.78 us
    pallas_call x1, Pallas kernels, pool(): pl.pallas_call(functools.partial(pool_kernel, devices, classes), in_specs...  5.43 us
    ppermute x6, starting transfers between devices, across(): lax.ppermute(x, ('freq', 'bl'), [(c, c ^ r) for c in range(devices)])  3.06 us
    pallas_call x2, Pallas kernels, join(): pl.pallas_call(functools.partial(join_kernel, ranks), in_specs=[pl.BlockS...  1.34 us
    dynamic_slice x1, local copies, waits for them, and re-layouts, body(): lax.dynamic_slice_in_dim(sky, slots + 1 - (place + 1) * each, each, 0)  1.11 us
    unnamed x4, local copies, waits for them, and re-layouts  0.74 us
  transfers between devices with their start and end apart: 8, of which 4 were waited for; matrix products, arithmetic and copies ran while one was open for 0% of the time, Pallas kernels for 27%

profile of v5, /device:TPU:0, one launch (start us, length us, event | category | flops | bytes accessed | tf_op | source)
XLA Modules:
  0.0 24.0 jit_solution(6836827874972459422)
XLA Ops:
  0.0 0.0 copy-start
  0.0 1.1 %constant_dynamic-slice_fusion.1 = (bf16[2,2,64,512]{3,2,1,0:T(8,128)(2,1)S(1)}, bf16[2,2,64,512]{3,2,1,0:T(8,128)(2,1)S(1)}) fusion(bf16[8,2,64,512]{3,2,1,0:T(8,128)(2,1)} %param.6, s32[]{:T(128)S(6)} %select_n.8, s32[]{:T(128)S(6)} %select_n.7), kind=kLoop, calls=%fused_computation.1 | loop fusion | bytes 1048584 | tf_op jit(solution)/shard_map/dynamic_slice | solution.py:251
  1.1 5.1 %collective-permute-start = (bf16[2,2,64,512]{3,2,1,0:T(8,128)(2,1)S(1)}, bf16[2,2,64,512]{3,2,1,0:T(8,128)(2,1)S(1)}, u32[]{:S(2)}, u32[]{:S(2)}) collective-permute-start(bf16[2,2,64,512]{3,2,1,0:T(8,128)(2,1)S(1)} %get-tuple-element.25), channel_id=1, source_target_pairs={{0,12},{1,13},{2,14},{3,15},{4,8},{5,9},{6,10},{7,11},{8,4},{9,5},... | collective-permute-start | bytes 786440 | tf_op jit(solution)/shard_map/ppermute | solution.py:247
  6.2 5.4 %shard_map.64 = (f32[48,128]{1,0:T(8,128)}, f32[48,128]{1,0:T(8,128)}, f32[48,128]{1,0:T(8,128)}, f32[48,128]{1,0:T(8,128)}) custom-call(bf16[16,8,2,64,256]{4,3,2,1,0:T(8,128)(2,1)} %vis, f32[16,2,256]{2,1,0:T(2,128)} %fringe.1, f32[16,256]{1,0:T(8,128)} %noise.1, s32[1,256]{1,0:T(1,128)} %bitcast.2), custom_call_target="tpu_custom_call" | custom-call | flops 805306368 | bytes 8388608 | tf_op jit(solution)/shard_map/pallas_call | solution.py:93
  11.7 0.7 %collective-permute-start.1 = (bf16[1,2,64,512]{3,2,1,0:T(8,128)(2,1)S(1)}, bf16[1,2,64,512]{3,2,1,0:T(8,128)(2,1)S(1)}, u32[]{:S(2)}, u32[]{:S(2)}) collective-permute-start(bf16[1,2,64,512]{3,2,1,0:T(8,128)(2,1)S(1)} %slice.3), channel_id=1, source_target_pairs={{4,12},{12,4},{20,28},{28,20}} | collective-permute-start | bytes 393224 | tf_op jit(solution)/shard_map/ppermute | solution.py:247
  12.4 1.6 %collective-permute-start.2 = (f32[48,128]{1,0:T(8,128)}, f32[48,128]{1,0:T(8,128)S(1)}, u32[]{:S(2)}, u32[]{:S(2)}) collective-permute-start(f32[48,128]{1,0:T(8,128)} %get-tuple-element.20), channel_id=1, source_target_pairs={{0,2},{1,3},{2,0},{3,1},{4,6},{5,7},{6,4},{7,5},{8,10},{9,11},{10,... | collective-permute-start | bytes 73736 | tf_op jit(solution)/shard_map/ppermute | solution.py:244
  13.9 0.0 collective-permute-start.3
  13.9 0.6 %collective-permute-start.4 = (f32[48,128]{1,0:T(8,128)}, f32[48,128]{1,0:T(8,128)S(1)}, u32[]{:S(2)}, u32[]{:S(2)}) collective-permute-start(f32[48,128]{1,0:T(8,128)} %get-tuple-element.22), channel_id=1, source_target_pairs={{0,1},{1,0},{2,3},{3,2},{4,5},{5,4},{6,7},{7,6},{8,9},{9,8},{10,11... | collective-permute-start | bytes 73736 | tf_op jit(solution)/shard_map/ppermute | solution.py:244
  14.6 0.0 copy-done
  14.6 0.0 copy-start.1
  14.6 0.7 %copy-done.1 = f32[48,128]{1,0:T(8,128)S(1)} copy-done((f32[48,128]{1,0:T(8,128)S(1)}, f32[48,128]{1,0:T(8,128)}, u32[]{:S(2)}) %copy-start.1) | copy-done | bytes 24600
  15.3 0.0 collective-permute-done.1.second
  15.3 0.0 collective-permute-done.first
  15.3 0.3 %shard_map.65 = (f32[32,64]{1,0:T(8,128)S(1)}, f32[32,64]{1,0:T(8,128)S(1)}) custom-call(bf16[2,2,64,512]{3,2,1,0:T(8,128)(2,1)S(1)} %get-tuple-element.17.sky, bf16[2,2,16,512]{3,2,1,0:T(8,128)(2,1)S(1)} %constant_dynamic-slice_fusion.beam, bf16[2,2,64,512]{3,2,1,0:T(8,128)(2,1)S(1)} %collective-permute-done.first, ...), custom_call_target="tpu_custom_call" | custom-call | tf_op jit(solution)/shard_map/pallas_call | solution.py:155
  15.6 0.9 %collective-permute-done.2.refs_2_ = f32[48,128]{1,0:T(8,128)S(1)} collective-permute-done((f32[48,128]{1,0:T(8,128)}, f32[48,128]{1,0:T(8,128)S(1)}, u32[]{:S(2)}, u32[]{:S(2)}) %collective-permute-start.2) | collective-permute-done | bytes 24608 | tf_op jit(solution)/shard_map/ppermute | solution.py:244
  16.5 0.9 %collective-permute-done.3.refs_3_ = f32[48,128]{1,0:T(8,128)S(1)} collective-permute-done((f32[48,128]{1,0:T(8,128)}, f32[48,128]{1,0:T(8,128)S(1)}, u32[]{:S(2)}, u32[]{:S(2)}) %collective-permute-start.3) | collective-permute-done | bytes 24608 | tf_op jit(solution)/shard_map/ppermute | solution.py:244
  17.4 0.0 collective-permute-done.4.refs_5_
  17.4 0.3 %shard_map.67 = (f32[2,32,256]{2,1,0:T(8,128)S(1)}, f32[2,32,256]{2,1,0:T(8,128)S(1)}) custom-call(bf16[2,2,64,512]{3,2,1,0:T(8,128)(2,1)S(1)} %get-tuple-element.17.sky, bf16[2,2,64,512]{3,2,1,0:T(8,128)(2,1)S(1)} %collective-permute-done.first, bf16[1,2,64,512]{3,2,1,0:T(8,128)(2,1)S(1)} %collective-permute-done.1.second, ...), custom_call_target="tpu_custom_call" | custom-call | tf_op jit(solution)/shard_map/pallas_call | solution.py:196
  17.8 0.9 %collective-permute-start.5 = (f32[2,32,256]{2,1,0:T(8,128)S(1)}, f32[2,32,256]{2,1,0:T(8,128)S(1)}, u32[]{:S(2)}, u32[]{:S(2)}) collective-permute-start(f32[2,32,256]{2,1,0:T(8,128)S(1)} %get-tuple-element.23), channel_id=1, source_target_pairs={{0,2},{1,3},{2,0},{3,1},{4,6},{5,7},{6,4},{7,5},{8,10},{9,11},{10,... | collective-permute-start | bytes 196616 | tf_op jit(solution)/shard_map/ppermute | solution.py:244
  18.6 0.0 collective-permute-start.7
  18.6 3.5 %collective-permute-done.5.refs_2_ = f32[2,32,256]{2,1,0:T(8,128)S(1)} collective-permute-done((f32[2,32,256]{2,1,0:T(8,128)S(1)}, f32[2,32,256]{2,1,0:T(8,128)S(1)}, u32[]{:S(2)}, u32[]{:S(2)}) %collective-permute-start.5) | collective-permute-done | bytes 65568 | tf_op jit(solution)/shard_map/ppermute | solution.py:244
  22.1 0.0 collective-permute-start.6
  22.1 0.0 collective-permute-done.7.refs_1_
  22.1 0.7 %shard_map.68.refs_1_ = f32[8,32,256]{2,1,0:T(8,128)} custom-call(f32[2,32,256]{2,1,0:T(8,128)S(1)} %get-tuple-element.24.refs_0_, f32[2,32,256]{2,1,0:T(8,128)S(1)} %collective-permute-done.7.refs_1_, f32[2,32,256]{2,1,0:T(8,128)S(1)} %collective-permute-done.5.refs_2_), custom_call_target="tpu_custom_call" | custom-call | tf_op jit(solution)/shard_map/pallas_call | solution.py:224
  22.8 0.5 %collective-permute-done.6.refs_0_ = f32[2,32,256]{2,1,0:T(8,128)S(1)} collective-permute-done((f32[2,32,256]{2,1,0:T(8,128)S(1)}, f32[2,32,256]{2,1,0:T(8,128)S(1)}, u32[]{:S(2)}, u32[]{:S(2)}) %collective-permute-start.6) | collective-permute-done | bytes 65568 | tf_op jit(solution)/shard_map/ppermute | solution.py:244
  23.3 0.6 %shard_map.69 = f32[8,32,256]{2,1,0:T(8,128)} custom-call(f32[2,32,256]{2,1,0:T(8,128)S(1)} %collective-permute-done.6.refs_0_, f32[8,32,256]{2,1,0:T(8,128)} %shard_map.68.refs_1_), custom_call_target="tpu_custom_call", output_to_operand_aliasing={{}: (1, {})} | custom-call | tf_op jit(solution)/shard_map/pallas_call | solution.py:224
  (3 shorter events, 0.0 us)
Async XLA Ops:
  0.0 14.6 %copy-start = (bf16[8,2,16,512]{3,2,1,0:T(8,128)(2,1)S(1)}, bf16[8,2,16,512]{3,2,1,0:T(8,128)(2,1)}, u32[]{:S(2)}) copy-start(bf16[8,2,16,512]{3,2,1,0:T(8,128)(2,1)} %param.7) | copy-start | bytes 786436
  1.1 14.2 %collective-permute-start = (bf16[2,2,64,512]{3,2,1,0:T(8,128)(2,1)S(1)}, bf16[2,2,64,512]{3,2,1,0:T(8,128)(2,1)S(1)}, u32[]{:S(2)}, u32[]{:S(2)}) collective-permute-start(bf16[2,2,64,512]{3,2,1,0:T(8,128)(2,1)S(1)} %get-tuple-element.25), channel_id=1, source_target_pairs={{0,12},{1,13},{2,14},{3,15},{4,8},{5,9},{6,10},{7,11},{8,4},{9,5},... | collective-permute-start | bytes 786440 | tf_op jit(solution)/shard_map/ppermute | solution.py:247
  11.7 3.6 %collective-permute-start.1 = (bf16[1,2,64,512]{3,2,1,0:T(8,128)(2,1)S(1)}, bf16[1,2,64,512]{3,2,1,0:T(8,128)(2,1)S(1)}, u32[]{:S(2)}, u32[]{:S(2)}) collective-permute-start(bf16[1,2,64,512]{3,2,1,0:T(8,128)(2,1)S(1)} %slice.3), channel_id=1, source_target_pairs={{4,12},{12,4},{20,28},{28,20}} | collective-permute-start | bytes 393224 | tf_op jit(solution)/shard_map/ppermute | solution.py:247
  12.4 4.1 %collective-permute-start.2 = (f32[48,128]{1,0:T(8,128)}, f32[48,128]{1,0:T(8,128)S(1)}, u32[]{:S(2)}, u32[]{:S(2)}) collective-permute-start(f32[48,128]{1,0:T(8,128)} %get-tuple-element.20), channel_id=1, source_target_pairs={{0,2},{1,3},{2,0},{3,1},{4,6},{5,7},{6,4},{7,5},{8,10},{9,11},{10,... | collective-permute-start | bytes 73736 | tf_op jit(solution)/shard_map/ppermute | solution.py:244
  13.9 3.5 %collective-permute-start.3 = (f32[48,128]{1,0:T(8,128)}, f32[48,128]{1,0:T(8,128)S(1)}, u32[]{:S(2)}, u32[]{:S(2)}) collective-permute-start(f32[48,128]{1,0:T(8,128)} %get-tuple-element.21), channel_id=1, source_target_pairs={{0,3},{1,2},{2,1},{3,0},{4,7},{5,6},{6,5},{7,4},{8,11},{9,10},{10,... | collective-permute-start | bytes 73736 | tf_op jit(solution)/shard_map/ppermute | solution.py:244
  13.9 3.5 %collective-permute-start.4 = (f32[48,128]{1,0:T(8,128)}, f32[48,128]{1,0:T(8,128)S(1)}, u32[]{:S(2)}, u32[]{:S(2)}) collective-permute-start(f32[48,128]{1,0:T(8,128)} %get-tuple-element.22), channel_id=1, source_target_pairs={{0,1},{1,0},{2,3},{3,2},{4,5},{5,4},{6,7},{7,6},{8,9},{9,8},{10,11... | collective-permute-start | bytes 73736 | tf_op jit(solution)/shard_map/ppermute | solution.py:244
  14.6 0.7 %copy-start.1 = (f32[48,128]{1,0:T(8,128)S(1)}, f32[48,128]{1,0:T(8,128)}, u32[]{:S(2)}) copy-start(f32[48,128]{1,0:T(8,128)} %get-tuple-element.16.x) | copy-start | bytes 73732
  17.8 4.3 %collective-permute-start.5 = (f32[2,32,256]{2,1,0:T(8,128)S(1)}, f32[2,32,256]{2,1,0:T(8,128)S(1)}, u32[]{:S(2)}, u32[]{:S(2)}) collective-permute-start(f32[2,32,256]{2,1,0:T(8,128)S(1)} %get-tuple-element.23), channel_id=1, source_target_pairs={{0,2},{1,3},{2,0},{3,1},{4,6},{5,7},{6,4},{7,5},{8,10},{9,11},{10,... | collective-permute-start | bytes 196616 | tf_op jit(solution)/shard_map/ppermute | solution.py:244
  18.6 3.5 %collective-permute-start.7 = (f32[2,32,256]{2,1,0:T(8,128)S(1)}, f32[2,32,256]{2,1,0:T(8,128)S(1)}, u32[]{:S(2)}, u32[]{:S(2)}) collective-permute-start(f32[2,32,256]{2,1,0:T(8,128)S(1)} %get-tuple-element.24.refs_0_), channel_id=1, source_target_pairs={{0,1},{1,0},{2,3},{3,2},{4,5},{5,4},{6,7},{7,6},{8,9},{9,8},{10,11... | collective-permute-start | bytes 196616 | tf_op jit(solution)/shard_map/ppermute | solution.py:244
  22.1 1.3 %collective-permute-start.6 = (f32[2,32,256]{2,1,0:T(8,128)S(1)}, f32[2,32,256]{2,1,0:T(8,128)S(1)}, u32[]{:S(2)}, u32[]{:S(2)}) collective-permute-start(f32[2,32,256]{2,1,0:T(8,128)S(1)} %collective-permute-done.5.refs_2_), channel_id=1, source_target_pairs={{0,1},{1,0},{2,3},{3,2},{4,5},{5,4},{6,7},{7,6},{8,9},{9,8},{10,11... | collective-permute-start | bytes 196616 | tf_op jit(solution)/shard_map/ppermute | solution.py:244

commit v6 on v5

v6 whole, which is shorter than its diff:
```python
import functools

import jax
import jax.numpy as jnp
from jax import lax
from jax.experimental import pallas as pl
from jax.experimental.pallas import tpu as pltpu
from jax.sharding import PartitionSpec as P

BF = jnp.bfloat16
F32 = jnp.float32
FIRST = 5
AHEAD = 10
NT = (((1,), (1,)), ((), ()))
NN = (((1,), (0,)), ((), ()))


def split3(x):
    top = x.astype(BF)
    rest = x - top.astype(F32)
    mid = rest.astype(BF)
    return top, mid, (rest - mid.astype(F32)).astype(BF)


def dot(a, b, dims):
    return lax.dot_general(a, b, dims, preferred_element_type=F32)


def my_core():
    return lax.axis_index("bl")


def rows(a, b):
    return jnp.concatenate([a, b], 0).astype(BF)


def pool_kernel(cores, classes, vis, fringe, noise, feeds, *refs):
    outs = refs[:cores]
    buf, fringe_v, noise_v, feeds_v, ready, sems, small = refs[cores:]
    channels, slots, _, skies, lines = vis.shape
    ahead = min(AHEAD, channels)
    little = [
        pltpu.make_async_copy(src, dst, small.at[i])
        for i, (src, dst) in enumerate([(feeds, feeds_v), (fringe, fringe_v), (noise, noise_v)])
    ]
    copies = [pltpu.make_async_copy(vis.at[f], buf.at[f], sems.at[f]) for f in range(channels)]
    for copy in little + copies[:FIRST]:
        copy.start()
    for copy in little:
        copy.wait()
    for copy in copies[FIRST:ahead]:
        copy.start()
    onehot = lax.broadcasted_iota(jnp.int32, (classes, lines), 0) == feeds_v[...]
    weight = noise_v[...]
    real = fringe_v[:, 0, :]
    imag = fringe_v[:, 1, :]
    gain = jnp.sum(weight * (real * real + imag * imag), axis=0, keepdims=True)
    gain = jnp.sum(jnp.where(onehot, gain, 0.0), axis=1, keepdims=True)
    parts_re = [p.astype(F32) for p in split3(weight * real)]
    parts_im = [p.astype(F32) for p in split3(-weight * imag)]

    def spread(part, f):
        return jnp.where(onehot, part[f : f + 1, :], 0.0)

    total = None
    for f in range(channels):
        rows_re = [spread(p, f) for p in parts_re]
        rows_im = [spread(p, f) for p in parts_im]
        left_re = jnp.concatenate([y for x in zip(rows_re, rows_im) for y in x], 0).astype(BF)
        left_im = jnp.concatenate([y for x in zip(rows_im, rows_re) for y in (-x[0], x[1])], 0).astype(BF)
        copies[f].wait()
        if f + ahead < channels:
            copies[f + ahead].start()
        for part, left in ((0, left_re), (1, left_im)):
            term = dot(left, buf[f, :, part].reshape(slots * skies, lines), NT)
            total = term if total is None else total + term
    wide = 2 * classes
    total = total[:wide] + total[wide : 2 * wide] + total[2 * wide :]
    width = slots * skies // cores
    for d in range(cores):
        ready[d, :wide] = total[:, d * width : (d + 1) * width]
        ready[d, wide:] = jnp.broadcast_to(gain, (classes, width))
    core = my_core()
    for r in range(cores):
        outs[r][...] = ready[core ^ r]


def pool(vis, fringe, noise, feeds, cores, classes):
    channels, slots, _, skies, lines = vis.shape
    width = slots * skies // cores
    vmem = pl.BlockSpec(memory_space=pltpu.VMEM)
    feeds = feeds.reshape(1, lines)
    return pl.pallas_call(
        functools.partial(pool_kernel, cores, classes),
        in_specs=[pl.BlockSpec(memory_space=pl.ANY)] * 4,
        out_specs=[vmem] * cores,
        out_shape=[jax.ShapeDtypeStruct((3 * classes, width), F32)] * cores,
        scratch_shapes=[
            pltpu.VMEM(vis.shape, BF),
            pltpu.VMEM(fringe.shape, F32),
            pltpu.VMEM(noise.shape, F32),
            pltpu.VMEM(feeds.shape, jnp.int32),
            pltpu.VMEM((cores, 3 * classes, width), F32),
            pltpu.SemaphoreType.DMA((channels,)),
            pltpu.SemaphoreType.DMA((3,)),
        ],
        compiler_params=pltpu.CompilerParams(vmem_limit_bytes=60 << 20),
        cost_estimate=pl.CostEstimate(
            flops=2 * 6 * classes * vis.size, bytes_accessed=2 * vis.size, transcendentals=0
        ),
    )(vis, fringe, noise, feeds)


def hold_kernel(x, out):
    out[...] = x[...]


def hold(x):
    vmem = pl.BlockSpec(memory_space=pltpu.VMEM)
    return pl.pallas_call(
        hold_kernel,
        in_specs=[vmem],
        out_specs=vmem,
        out_shape=jax.ShapeDtypeStruct(x.shape, x.dtype),
        compiler_params=pltpu.CompilerParams(vmem_limit_bytes=8 << 20),
    )(x)


def mirror(far, sky, i):
    each = sky.shape[0]
    first = my_core() == 0
    if i:
        return far[0][each - 1 - i + jnp.where(first, 1, 0)]
    block, blocks = lax.axis_index("ma"), lax.axis_size("ma")
    other = jnp.where((2 * block) % blocks == 0, sky[i], far[1][0])
    return jnp.where(first, other, far[0][each - 1])


def parity_of(slot):
    return jnp.where(slot % 2 == 0, 1.0, -1.0).astype(F32)


def response_kernel(cores, sky, beam, first, second, *refs):
    held, out = refs[:-1], refs[-1]
    each, _, skies, _ = sky.shape
    wide = 2 * beam.shape[2]
    below = out.shape[0] - wide
    out[:below] = functools.reduce(jnp.add, [ref[...] for ref in held])
    for i in range(each):
        other = mirror((first, second), sky, i)
        b_re, b_im = beam[i, 0].astype(F32), beam[i, 1].astype(F32)
        direct = dot(rows(b_re, b_im), sky[i, 0], NT) + dot(rows(-b_im, b_re), sky[i, 1], NT)
        crossed = dot(rows(b_re, b_im), other[0], NT) + dot(rows(b_im, -b_re), other[1], NT)
        out[below:, i * skies : (i + 1) * skies] = direct + parity_of(my_core() * each + i) * crossed


def response(sky, beam, far, held):
    vmem = pl.BlockSpec(memory_space=pltpu.VMEM)
    below, width = held[0].shape
    return pl.pallas_call(
        functools.partial(response_kernel, len(held)),
        in_specs=[vmem] * (2 + len(far) + len(held)),
        out_specs=vmem,
        out_shape=jax.ShapeDtypeStruct((below + 2 * beam.shape[2], width), F32),
        compiler_params=pltpu.CompilerParams(vmem_limit_bytes=8 << 20),
    )(sky, beam, *far, *held)


def grad_kernel(classes, sky, first, second, *refs):
    found, out = refs[:-1], refs[-1]
    each, _, skies, step = sky.shape
    wide = 2 * classes
    sums = functools.reduce(jnp.add, [ref[...] for ref in found])
    gain, resp = 0.5 * sums[wide : 3 * classes], sums[3 * classes :]
    for i in range(each):
        at = slice(i * skies, (i + 1) * skies)
        parity = parity_of(my_core() * each + i)
        other = mirror((first, second), sky, i)
        p_re = 0.5 * (gain[:, at] * resp[:classes, at] - sums[:classes, at])
        p_im = 0.5 * (gain[:, at] * resp[classes:, at] - sums[classes:wide, at])
        own = jnp.concatenate([jnp.concatenate([p_re, p_im], 1), jnp.concatenate([p_im, -p_re], 1)], 0)
        away = parity * jnp.concatenate([jnp.concatenate([p_re, -p_im], 1), jnp.concatenate([p_im, p_re], 1)], 0)
        own = jnp.concatenate(split3(own), 0)
        away = jnp.concatenate(split3(away), 0)
        grad = dot(own, sky[i].reshape(2 * skies, step), NN) + dot(away, other.reshape(2 * skies, step), NN)
        out[i] = grad[:wide] + grad[wide : 2 * wide] + grad[2 * wide :]


def gradient(classes, sky, far, found):
    each, _, _, step = sky.shape
    vmem = pl.BlockSpec(memory_space=pltpu.VMEM)
    return pl.pallas_call(
        functools.partial(grad_kernel, classes),
        in_specs=[vmem] * (1 + len(far) + len(found)),
        out_specs=vmem,
        out_shape=jax.ShapeDtypeStruct((each, 2 * classes, step), F32),
        compiler_params=pltpu.CompilerParams(vmem_limit_bytes=8 << 20),
    )(sky, *far, *found)


def join_kernel(*refs):
    pieces, out, sems = refs[:-2], refs[-2], refs[-1]
    each = pieces[0].shape[0]
    core = my_core()
    copies = [
        pltpu.make_async_copy(piece, out.at[pl.ds((core ^ r) * each, each)], sems.at[r])
        for r, piece in enumerate(pieces)
    ]
    for copy in copies:
        copy.start()
    for copy in copies:
        copy.wait()


def join(pieces):
    each, wide, step = pieces[0].shape
    return pl.pallas_call(
        join_kernel,
        in_specs=[pl.BlockSpec(memory_space=pltpu.VMEM)] * len(pieces),
        out_specs=pl.BlockSpec(memory_space=pl.ANY),
        out_shape=jax.ShapeDtypeStruct((each * len(pieces), wide, step), F32),
        scratch_shapes=[pltpu.SemaphoreType.DMA((len(pieces),))],
        compiler_params=pltpu.CompilerParams(vmem_limit_bytes=8 << 20),
    )(*pieces)


def body(sky, beam, vis, fringe, noise, feeds):
    slots, _, _, degrees = sky.shape
    classes = beam.shape[2]
    blocks, cuts, cores = (lax.axis_size(x) for x in ("ma", "freq", "bl"))
    devices = cuts * cores
    each = slots // cores
    step = degrees // cuts
    core = my_core()
    left = lax.axis_index("freq") * step

    def across(x, r):
        return lax.ppermute(x, ("freq", "bl"), [(c, c ^ r) for c in range(devices)]) if r else x

    def mirrored(sent, pairs):
        return lax.ppermute(
            sent, ("ma", "freq", "bl"), [(a * devices + c, b * devices + c) for a, b, c in pairs]
        )

    def share(x, start):
        return lax.dynamic_slice(x, (start, 0, 0, left), (each, *x.shape[1:3], step))

    sent = share(sky, jnp.minimum(slots + 1 - (core + 1) * each, slots - each))
    own = share(sky, core * each)
    own_beam = share(beam, core * each)
    far = [mirrored(sent, [(a, blocks - 1 - a, c) for a in range(blocks) for c in range(devices)])]
    vis, _ = lax.optimization_barrier((vis, sent))
    sums = pool(vis, fringe, noise, feeds, cores, classes)
    held = [across(x, r) for r, x in enumerate(sums)]
    first = lax.optimization_barrier((own, sums[0]))[0][:1]
    turned = [(a, blocks - a) for a in range(1, blocks) if 2 * a != blocks]
    far.append(mirrored(first, [(a, b, c) for a, b in turned for c in range(0, devices, cores)]))
    held[0] = hold(held[0])
    found = response(own, own_beam, far, held)
    found = [across(found, h * cores) for h in range(cuts)]
    grad = gradient(classes, own, far, found)
    out = join([across(grad, r) for r in range(cores)])
    return out.reshape(slots, 2, classes, step)


def solution(mesh):
    in_specs = (
        P("ma", None, "grp", None),
        P("ma", None, None, None),
        P("freq", "ma", None, "grp", "bl"),
        P("freq", None, "bl"),
        P("freq", "bl"),
        P("bl"),
    )
    out_specs = P("ma", None, "grp", "freq")
    return jax.shard_map(body, mesh=mesh, in_specs=in_specs, out_specs=out_specs, check_vma=False)
```

time: 24.2 us -> 23.3 us (0.963)
  the two profiles are of different devices: /device:TPU:0 before, /device:TPU:15 now
where the time goes in v6:
time: 23.3 us; the launch traced here: 23.1 us
  starting transfers between devices  9.11 us (39%)
  Pallas kernels  6.78 us (29%)
  waiting for transfers between devices  5.24 us (22%)
  local copies, waits for them, and re-layouts  1.92 us (8%)
    ppermute x3, starting transfers between devices, across(): lax.ppermute(x, ('freq', 'bl'), [(c, c ^ r) for c in range(devices)])  7.08 us
    pallas_call x1, Pallas kernels, pool(): pl.pallas_call(functools.partial(pool_kernel, cores, classes), in_specs=[...  5.42 us
    ppermute x3, waiting for transfers between devices, across(): lax.ppermute(x, ('freq', 'bl'), [(c, c ^ r) for c in range(devices)])  4.3 us
    ppermute x2, starting transfers between devices, mirrored(): lax.ppermute(sent, ('ma', 'freq', 'bl'), [(a * devices + c, b * devices +...  2.03 us
    dynamic_slice x2, local copies, waits for them, and re-layouts, share(): lax.dynamic_slice(x, (start, 0, 0, left), (each, *x.shape[1:3], step))  1.11 us
    ppermute x2, waiting for transfers between devices, mirrored(): lax.ppermute(sent, ('ma', 'freq', 'bl'), [(a * devices + c, b * devices +...  0.94 us
    unnamed x4, local copies, waits for them, and re-layouts  0.8 us
    pallas_call x1, Pallas kernels, join(): pl.pallas_call(join_kernel, in_specs=[pl.BlockSpec(memory_space=pltpu.VME...  0.71 us
  transfers between devices with their start and end apart: 5, of which 4 were waited for; matrix products, arithmetic and copies ran while one was open for 0% of the time, Pallas kernels for 23%

profile of v6, /device:TPU:15, one launch (start us, length us, event | category | flops | bytes accessed | tf_op | source)
XLA Modules:
  0.0 23.1 jit_solution(10019668672819130810)
XLA Ops:
  0.0 0.0 copy-start
  0.0 1.1 %constant_dynamic-slice_fusion.1 = (bf16[4,2,64,256]{3,2,1,0:T(8,128)(2,1)S(1)}, bf16[4,2,64,256]{3,2,1,0:T(8,128)(2,1)S(1)}) fusion(bf16[8,2,64,512]{3,2,1,0:T(8,128)(2,1)} %param.6, s32[]{:T(128)S(6)} %select_n.14, s32[]{:T(128)S(6)} %select_n.13, s32[]{:T(128)S(6)} %select_n.12), kind=kLoop, calls=%fused_computation.1 | loop fusion | bytes 1048588 | tf_op jit(solution)/shard_map/dynamic_slice | solution.py:246
  1.1 1.4 %collective-permute-start = (bf16[4,2,64,256]{3,2,1,0:T(8,128)(2,1)S(1)}, bf16[4,2,64,256]{3,2,1,0:T(8,128)(2,1)S(1)}, u32[]{:S(2)}, u32[]{:S(2)}) collective-permute-start(bf16[4,2,64,256]{3,2,1,0:T(8,128)(2,1)S(1)} %get-tuple-element.13), channel_id=1, source_target_pairs={{0,12},{1,13},{2,14},{3,15},{4,8},{5,9},{6,10},{7,11},{8,4},{9,5},... | collective-permute-start | bytes 786440 | tf_op jit(solution)/shard_map/ppermute | solution.py:241
  2.5 5.4 %shard_map.64 = (f32[48,256]{1,0:T(8,128)}, f32[48,256]{1,0:T(8,128)}) custom-call(bf16[16,8,2,64,256]{4,3,2,1,0:T(8,128)(2,1)} %vis, f32[16,2,256]{2,1,0:T(2,128)} %fringe.1, f32[16,256]{1,0:T(8,128)} %noise.1, s32[1,256]{1,0:T(1,128)} %bitcast.2), custom_call_target="tpu_custom_call" | custom-call | flops 805306368 | bytes 8388608 | tf_op jit(solution)/shard_map/pallas_call | solution.py:93
  7.9 0.7 %collective-permute-start.1 = (bf16[1,2,64,256]{3,2,1,0:T(8,128)(2,1)S(1)}, bf16[1,2,64,256]{3,2,1,0:T(8,128)(2,1)S(1)}, u32[]{:S(2)}, u32[]{:S(2)}) collective-permute-start(bf16[1,2,64,256]{3,2,1,0:T(8,128)(2,1)S(1)} %slice.3), channel_id=1, source_target_pairs={{4,12},{6,14},{12,4},{14,6},{20,28},{22,30},{28,20},{30,22}} | collective-permute-start | bytes 196616 | tf_op jit(solution)/shard_map/ppermute | solution.py:241
  8.6 3.5 %collective-permute-start.2 = (f32[48,256]{1,0:T(8,128)}, f32[48,256]{1,0:T(8,128)S(1)}, u32[]{:S(2)}, u32[]{:S(2)}) collective-permute-start(f32[48,256]{1,0:T(8,128)} %get-tuple-element.12), channel_id=1, source_target_pairs={{0,1},{1,0},{2,3},{3,2},{4,5},{5,4},{6,7},{7,6},{8,9},{9,8},{10,11... | collective-permute-start | bytes 147464 | tf_op jit(solution)/shard_map/ppermute | solution.py:238
  12.1 0.0 copy-done
  12.1 0.0 copy-start.1
  12.1 0.8 %copy-done.1 = f32[48,256]{1,0:T(8,128)S(1)} copy-done((f32[48,256]{1,0:T(8,128)S(1)}, f32[48,256]{1,0:T(8,128)}, u32[]{:S(2)}) %copy-start.1) | copy-done | bytes 49176
  12.9 0.3 %collective-permute-done.2.refs_1_ = f32[48,256]{1,0:T(8,128)S(1)} collective-permute-done((f32[48,256]{1,0:T(8,128)}, f32[48,256]{1,0:T(8,128)S(1)}, u32[]{:S(2)}, u32[]{:S(2)}) %collective-permute-start.2) | collective-permute-done | bytes 49184 | tf_op jit(solution)/shard_map/ppermute | solution.py:238
  13.2 0.0 collective-permute-done.1.second
  13.2 0.9 %collective-permute-done.first = bf16[4,2,64,256]{3,2,1,0:T(8,128)(2,1)S(1)} collective-permute-done((bf16[4,2,64,256]{3,2,1,0:T(8,128)(2,1)S(1)}, bf16[4,2,64,256]{3,2,1,0:T(8,128)(2,1)S(1)}, u32[]{:S(2)}, u32[]{:S(2)}) %collective-permute-start) | collective-permute-done | bytes 262176 | tf_op jit(solution)/shard_map/ppermute | solution.py:241
  14.2 0.3 %shard_map.66.refs_0_ = f32[80,256]{1,0:T(8,128)S(1)} custom-call(bf16[4,2,64,256]{3,2,1,0:T(8,128)(2,1)S(1)} %get-tuple-element.11.sky, bf16[4,2,16,256]{3,2,1,0:T(8,128)(2,1)S(1)} %constant_dynamic-slice_fusion.beam, bf16[4,2,64,256]{3,2,1,0:T(8,128)(2,1)S(1)} %collective-permute-done.first, bf16[1,2,64,256]{3,2,1,0:T(8,128)(2,1)S(1)} %collective-permute-done.1.second, ...), custom_call_target="tpu_custom_call" | custom-call | tf_op jit(solution)/shard_map/pallas_call | solution.py:160
  14.5 0.3 %collective-permute-start.3 = (f32[80,256]{1,0:T(8,128)S(1)}, f32[80,256]{1,0:T(8,128)S(1)}, u32[]{:S(2)}, u32[]{:S(2)}) collective-permute-start(f32[80,256]{1,0:T(8,128)S(1)} %shard_map.66.refs_0_), channel_id=1, source_target_pairs={{0,2},{1,3},{2,0},{3,1},{4,6},{5,7},{6,4},{7,5},{8,10},{9,11},{10,... | collective-permute-start | bytes 245768 | tf_op jit(solution)/shard_map/ppermute | solution.py:238
  14.8 3.0 %collective-permute-done.3.refs_1_ = f32[80,256]{1,0:T(8,128)S(1)} collective-permute-done((f32[80,256]{1,0:T(8,128)S(1)}, f32[80,256]{1,0:T(8,128)S(1)}, u32[]{:S(2)}, u32[]{:S(2)}) %collective-permute-start.3) | collective-permute-done | bytes 81952 | tf_op jit(solution)/shard_map/ppermute | solution.py:238
  17.8 0.3 %shard_map.67.refs_0_ = f32[4,32,256]{2,1,0:T(8,128)S(1)} custom-call(bf16[4,2,64,256]{3,2,1,0:T(8,128)(2,1)S(1)} %get-tuple-element.11.sky, bf16[4,2,64,256]{3,2,1,0:T(8,128)(2,1)S(1)} %collective-permute-done.first, bf16[1,2,64,256]{3,2,1,0:T(8,128)(2,1)S(1)} %collective-permute-done.1.second, f32[80,256]{1,0:T(8,128)S(1)} %shard_map.66.refs_0_, ...), custom_call_target="tpu_custom_call" | custom-call | tf_op jit(solution)/shard_map/pallas_call | solution.py:192
  18.1 3.3 %collective-permute-start.4 = (f32[4,32,256]{2,1,0:T(8,128)S(1)}, f32[4,32,256]{2,1,0:T(8,128)S(1)}, u32[]{:S(2)}, u32[]{:S(2)}) collective-permute-start(f32[4,32,256]{2,1,0:T(8,128)S(1)} %shard_map.67.refs_0_), channel_id=1, source_target_pairs={{0,1},{1,0},{2,3},{3,2},{4,5},{5,4},{6,7},{7,6},{8,9},{9,8},{10,11... | collective-permute-start | bytes 393224 | tf_op jit(solution)/shard_map/ppermute | solution.py:238
  21.4 1.0 %collective-permute-done.4.refs_1_ = f32[4,32,256]{2,1,0:T(8,128)S(1)} collective-permute-done((f32[4,32,256]{2,1,0:T(8,128)S(1)}, f32[4,32,256]{2,1,0:T(8,128)S(1)}, u32[]{:S(2)}, u32[]{:S(2)}) %collective-permute-start.4) | collective-permute-done | bytes 131104 | tf_op jit(solution)/shard_map/ppermute | solution.py:238
  22.4 0.7 %shard_map.68 = f32[8,32,256]{2,1,0:T(8,128)} custom-call(f32[4,32,256]{2,1,0:T(8,128)S(1)} %shard_map.67.refs_0_, f32[4,32,256]{2,1,0:T(8,128)S(1)} %collective-permute-done.4.refs_1_), custom_call_target="tpu_custom_call" | custom-call | tf_op jit(solution)/shard_map/pallas_call | solution.py:217
  (3 shorter events, 0.0 us)
Async XLA Ops:
  0.0 12.1 %copy-start = (bf16[8,2,16,512]{3,2,1,0:T(8,128)(2,1)S(1)}, bf16[8,2,16,512]{3,2,1,0:T(8,128)(2,1)}, u32[]{:S(2)}) copy-start(bf16[8,2,16,512]{3,2,1,0:T(8,128)(2,1)} %param.7) | copy-start | bytes 786436
  1.1 13.0 %collective-permute-start = (bf16[4,2,64,256]{3,2,1,0:T(8,128)(2,1)S(1)}, bf16[4,2,64,256]{3,2,1,0:T(8,128)(2,1)S(1)}, u32[]{:S(2)}, u32[]{:S(2)}) collective-permute-start(bf16[4,2,64,256]{3,2,1,0:T(8,128)(2,1)S(1)} %get-tuple-element.13), channel_id=1, source_target_pairs={{0,12},{1,13},{2,14},{3,15},{4,8},{5,9},{6,10},{7,11},{8,4},{9,5},... | collective-permute-start | bytes 786440 | tf_op jit(solution)/shard_map/ppermute | solution.py:241
  7.9 5.3 %collective-permute-start.1 = (bf16[1,2,64,256]{3,2,1,0:T(8,128)(2,1)S(1)}, bf16[1,2,64,256]{3,2,1,0:T(8,128)(2,1)S(1)}, u32[]{:S(2)}, u32[]{:S(2)}) collective-permute-start(bf16[1,2,64,256]{3,2,1,0:T(8,128)(2,1)S(1)} %slice.3), channel_id=1, source_target_pairs={{4,12},{6,14},{12,4},{14,6},{20,28},{22,30},{28,20},{30,22}} | collective-permute-start | bytes 196616 | tf_op jit(solution)/shard_map/ppermute | solution.py:241
  8.6 4.6 %collective-permute-start.2 = (f32[48,256]{1,0:T(8,128)}, f32[48,256]{1,0:T(8,128)S(1)}, u32[]{:S(2)}, u32[]{:S(2)}) collective-permute-start(f32[48,256]{1,0:T(8,128)} %get-tuple-element.12), channel_id=1, source_target_pairs={{0,1},{1,0},{2,3},{3,2},{4,5},{5,4},{6,7},{7,6},{8,9},{9,8},{10,11... | collective-permute-start | bytes 147464 | tf_op jit(solution)/shard_map/ppermute | solution.py:238
  12.1 0.8 %copy-start.1 = (f32[48,256]{1,0:T(8,128)S(1)}, f32[48,256]{1,0:T(8,128)}, u32[]{:S(2)}) copy-start(f32[48,256]{1,0:T(8,128)} %get-tuple-element.10.x) | copy-start | bytes 147460
  14.5 3.3 %collective-permute-start.3 = (f32[80,256]{1,0:T(8,128)S(1)}, f32[80,256]{1,0:T(8,128)S(1)}, u32[]{:S(2)}, u32[]{:S(2)}) collective-permute-start(f32[80,256]{1,0:T(8,128)S(1)} %shard_map.66.refs_0_), channel_id=1, source_target_pairs={{0,2},{1,3},{2,0},{3,1},{4,6},{5,7},{6,4},{7,5},{8,10},{9,11},{10,... | collective-permute-start | bytes 245768 | tf_op jit(solution)/shard_map/ppermute | solution.py:238
  18.1 4.3 %collective-permute-start.4 = (f32[4,32,256]{2,1,0:T(8,128)S(1)}, f32[4,32,256]{2,1,0:T(8,128)S(1)}, u32[]{:S(2)}, u32[]{:S(2)}) collective-permute-start(f32[4,32,256]{2,1,0:T(8,128)S(1)} %shard_map.67.refs_0_), channel_id=1, source_target_pairs={{0,1},{1,0},{2,3},{3,2},{4,5},{5,4},{6,7},{7,6},{8,9},{9,8},{10,11... | collective-permute-start | bytes 393224 | tf_op jit(solution)/shard_map/ppermute | solution.py:238

commit v7 on v6

--- a/solution.py
+++ b/solution.py
@@ -246,13 +246,14 @@
         return lax.dynamic_slice(x, (start, 0, 0, left), (each, *x.shape[1:3], step))
 
     sent = share(sky, jnp.minimum(slots + 1 - (core + 1) * each, slots - each))
-    own = share(sky, core * each)
-    own_beam = share(beam, core * each)
     far = [mirrored(sent, [(a, blocks - 1 - a, c) for a in range(blocks) for c in range(devices)])]
     vis, _ = lax.optimization_barrier((vis, sent))
     sums = pool(vis, fringe, noise, feeds, cores, classes)
     held = [across(x, r) for r, x in enumerate(sums)]
-    first = lax.optimization_barrier((own, sums[0]))[0][:1]
+    later, later_beam, _ = lax.optimization_barrier((sky, beam, sums[0]))
+    own = share(later, core * each)
+    own_beam = share(later_beam, core * each)
+    first = own[:1]
     turned = [(a, blocks - a) for a in range(1, blocks) if 2 * a != blocks]
     far.append(mirrored(first, [(a, b, c) for a, b in turned for c in range(0, devices, cores)]))
     held[0] = hold(held[0])

time: 23.3 us -> 23.5 us (level)
  the two profiles are of different devices: /device:TPU:15 before, /device:TPU:9 now
where the time goes in v7:
time: 23.5 us; the launch traced here: 23.2 us
  starting transfers between devices  9.82 us (42%)
  Pallas kernels  6.81 us (29%)
  waiting for transfers between devices  3.64 us (15%)
  local copies, waits for them, and re-layouts  2.93 us (12%)
    ppermute x3, starting transfers between devices, across(): lax.ppermute(x, ('freq', 'bl'), [(c, c ^ r) for c in range(devices)])  7.79 us
    pallas_call x1, Pallas kernels, pool(): pl.pallas_call(functools.partial(pool_kernel, cores, classes), in_specs=[...  5.45 us
    ppermute x3, waiting for transfers between devices, across(): lax.ppermute(x, ('freq', 'bl'), [(c, c ^ r) for c in range(devices)])  3.07 us
    ppermute x2, starting transfers between devices, mirrored(): lax.ppermute(sent, ('ma', 'freq', 'bl'), [(a * devices + c, b * devices +...  2.03 us
    unnamed x4, local copies, waits for them, and re-layouts  2.02 us
    dynamic_slice x3, local copies, waits for them, and re-layouts, share(): lax.dynamic_slice(x, (start, 0, 0, left), (each, *x.shape[1:3], step))  0.89 us
    pallas_call x1, Pallas kernels, join(): pl.pallas_call(join_kernel, in_specs=[pl.BlockSpec(memory_space=pltpu.VME...  0.71 us
    ppermute x2, waiting for transfers between devices, mirrored(): lax.ppermute(sent, ('ma', 'freq', 'bl'), [(a * devices + c, b * devices +...  0.57 us
  transfers between devices with their start and end apart: 5, of which 3 were waited for; matrix products, arithmetic and copies ran while one was open for 4% of the time, Pallas kernels for 23%

profile of v7, /device:TPU:9, one launch (start us, length us, event | category | flops | bytes accessed | tf_op | source)
XLA Modules:
  0.0 23.2 jit_solution(15132684733036781011)
XLA Ops:
  0.0 0.0 copy-start
  0.0 1.2 %copy-done = bf16[8,2,64,512]{3,2,1,0:T(8,128)(2,1)S(1)} copy-done((bf16[8,2,64,512]{3,2,1,0:T(8,128)(2,1)S(1)}, bf16[8,2,64,512]{3,2,1,0:T(8,128)(2,1)}, u32[]{:S(2)}) %copy-start) | copy-done | bytes 1048600
  1.2 1.4 %collective-permute-start = (bf16[4,2,64,256]{3,2,1,0:T(8,128)(2,1)S(1)}, bf16[4,2,64,256]{3,2,1,0:T(8,128)(2,1)S(1)}, u32[]{:S(2)}, u32[]{:S(2)}) collective-permute-start(bf16[4,2,64,256]{3,2,1,0:T(8,128)(2,1)S(1)} %constant_dynamic-slice_fusion.3), channel_id=1, source_target_pairs={{0,12},{1,13},{2,14},{3,15},{4,8},{5,9},{6,10},{7,11},{8,4},{9,5},... | collective-permute-start | bytes 786440 | tf_op jit(solution)/shard_map/ppermute | solution.py:241
  2.6 5.4 %shard_map.64 = (f32[48,256]{1,0:T(8,128)}, f32[48,256]{1,0:T(8,128)}) custom-call(bf16[16,8,2,64,256]{4,3,2,1,0:T(8,128)(2,1)} %vis, f32[16,2,256]{2,1,0:T(2,128)} %fringe.1, f32[16,256]{1,0:T(8,128)} %noise.1, s32[1,256]{1,0:T(1,128)} %bitcast.2), custom_call_target="tpu_custom_call" | custom-call | flops 805306368 | bytes 8388608 | tf_op jit(solution)/shard_map/pallas_call | solution.py:93
  8.1 0.7 %collective-permute-start.1 = (bf16[1,2,64,256]{3,2,1,0:T(8,128)(2,1)S(1)}, bf16[1,2,64,256]{3,2,1,0:T(8,128)(2,1)S(1)}, u32[]{:S(2)}, u32[]{:S(2)}) collective-permute-start(bf16[1,2,64,256]{3,2,1,0:T(8,128)(2,1)S(1)} %constant_dynamic-slice_fusion), channel_id=1, source_target_pairs={{4,12},{6,14},{12,4},{14,6},{20,28},{22,30},{28,20},{30,22}} | collective-permute-start | bytes 196616 | tf_op jit(solution)/shard_map/ppermute | solution.py:241
  8.8 3.3 %collective-permute-start.2 = (f32[48,256]{1,0:T(8,128)}, f32[48,256]{1,0:T(8,128)S(1)}, u32[]{:S(2)}, u32[]{:S(2)}) collective-permute-start(f32[48,256]{1,0:T(8,128)} %get-tuple-element.14), channel_id=1, source_target_pairs={{0,1},{1,0},{2,3},{3,2},{4,5},{5,4},{6,7},{7,6},{8,9},{9,8},{10,11... | collective-permute-start | bytes 147464 | tf_op jit(solution)/shard_map/ppermute | solution.py:238
  12.1 0.9 %constant_dynamic-slice_fusion.1.beam = bf16[4,2,16,256]{3,2,1,0:T(8,128)(2,1)S(1)} fusion(bf16[8,2,16,512]{3,2,1,0:T(8,128)(2,1)} %param.7, s32[]{:T(128)S(6)} %select_n.14, s32[]{:T(128)S(6)} %select_n.13), kind=kLoop, calls=%fused_computation.1 | loop fusion | bytes 131080 | tf_op jit(solution)/shard_map/dynamic_slice | solution.py:246
  12.9 0.0 copy-start.1
  12.9 0.8 %copy-done.1 = f32[48,256]{1,0:T(8,128)S(1)} copy-done((f32[48,256]{1,0:T(8,128)S(1)}, f32[48,256]{1,0:T(8,128)}, u32[]{:S(2)}) %copy-start.1) | copy-done | bytes 49176
  13.7 0.0 collective-permute-done.2.refs_1_
  13.7 0.0 collective-permute-done.1.second
  13.7 0.6 %collective-permute-done.first = bf16[4,2,64,256]{3,2,1,0:T(8,128)(2,1)S(1)} collective-permute-done((bf16[4,2,64,256]{3,2,1,0:T(8,128)(2,1)S(1)}, bf16[4,2,64,256]{3,2,1,0:T(8,128)(2,1)S(1)}, u32[]{:S(2)}, u32[]{:S(2)}) %collective-permute-start) | collective-permute-done | bytes 262176 | tf_op jit(solution)/shard_map/ppermute | solution.py:241
  14.3 0.3 %shard_map.66.refs_0_ = f32[80,256]{1,0:T(8,128)S(1)} custom-call(bf16[4,2,64,256]{3,2,1,0:T(8,128)(2,1)S(1)} %constant_dynamic-slice_fusion.2.sky, bf16[4,2,16,256]{3,2,1,0:T(8,128)(2,1)S(1)} %constant_dynamic-slice_fusion.1.beam, bf16[4,2,64,256]{3,2,1,0:T(8,128)(2,1)S(1)} %collective-permute-done.first, ...), custom_call_target="tpu_custom_call" | custom-call | tf_op jit(solution)/shard_map/pallas_call | solution.py:160
  14.6 1.2 %collective-permute-start.3 = (f32[80,256]{1,0:T(8,128)S(1)}, f32[80,256]{1,0:T(8,128)S(1)}, u32[]{:S(2)}, u32[]{:S(2)}) collective-permute-start(f32[80,256]{1,0:T(8,128)S(1)} %shard_map.66.refs_0_), channel_id=1, source_target_pairs={{0,2},{1,3},{2,0},{3,1},{4,6},{5,7},{6,4},{7,5},{8,10},{9,11},{10,... | collective-permute-start | bytes 245768 | tf_op jit(solution)/shard_map/ppermute | solution.py:238
  15.9 2.1 %collective-permute-done.3.refs_1_ = f32[80,256]{1,0:T(8,128)S(1)} collective-permute-done((f32[80,256]{1,0:T(8,128)S(1)}, f32[80,256]{1,0:T(8,128)S(1)}, u32[]{:S(2)}, u32[]{:S(2)}) %collective-permute-start.3) | collective-permute-done | bytes 81952 | tf_op jit(solution)/shard_map/ppermute | solution.py:238
  17.9 0.3 %shard_map.67.refs_0_ = f32[4,32,256]{2,1,0:T(8,128)S(1)} custom-call(bf16[4,2,64,256]{3,2,1,0:T(8,128)(2,1)S(1)} %constant_dynamic-slice_fusion.2.sky, bf16[4,2,64,256]{3,2,1,0:T(8,128)(2,1)S(1)} %collective-permute-done.first, bf16[1,2,64,256]{3,2,1,0:T(8,128)(2,1)S(1)} %collective-permute-done.1.second, f32[80,256]{1,0:T(8,128)S(1)} %shard_map.66.refs_0_, ...), custom_call_target="tpu_custom_call" | custom-call | tf_op jit(solution)/shard_map/pallas_call | solution.py:192
  18.2 3.3 %collective-permute-start.4 = (f32[4,32,256]{2,1,0:T(8,128)S(1)}, f32[4,32,256]{2,1,0:T(8,128)S(1)}, u32[]{:S(2)}, u32[]{:S(2)}) collective-permute-start(f32[4,32,256]{2,1,0:T(8,128)S(1)} %shard_map.67.refs_0_), channel_id=1, source_target_pairs={{0,1},{1,0},{2,3},{3,2},{4,5},{5,4},{6,7},{7,6},{8,9},{9,8},{10,11... | collective-permute-start | bytes 393224 | tf_op jit(solution)/shard_map/ppermute | solution.py:238
  21.5 1.0 %collective-permute-done.4.refs_1_ = f32[4,32,256]{2,1,0:T(8,128)S(1)} collective-permute-done((f32[4,32,256]{2,1,0:T(8,128)S(1)}, f32[4,32,256]{2,1,0:T(8,128)S(1)}, u32[]{:S(2)}, u32[]{:S(2)}) %collective-permute-start.4) | collective-permute-done | bytes 131104 | tf_op jit(solution)/shard_map/ppermute | solution.py:238
  22.5 0.7 %shard_map.68 = f32[8,32,256]{2,1,0:T(8,128)} custom-call(f32[4,32,256]{2,1,0:T(8,128)S(1)} %shard_map.67.refs_0_, f32[4,32,256]{2,1,0:T(8,128)S(1)} %collective-permute-done.4.refs_1_), custom_call_target="tpu_custom_call" | custom-call | tf_op jit(solution)/shard_map/pallas_call | solution.py:217
  (4 shorter events, 0.1 us)
Async XLA Ops:
  0.0 1.2 %copy-start = (bf16[8,2,64,512]{3,2,1,0:T(8,128)(2,1)S(1)}, bf16[8,2,64,512]{3,2,1,0:T(8,128)(2,1)}, u32[]{:S(2)}) copy-start(bf16[8,2,64,512]{3,2,1,0:T(8,128)(2,1)} %param.6) | copy-start | bytes 3145732
  1.2 13.0 %collective-permute-start = (bf16[4,2,64,256]{3,2,1,0:T(8,128)(2,1)S(1)}, bf16[4,2,64,256]{3,2,1,0:T(8,128)(2,1)S(1)}, u32[]{:S(2)}, u32[]{:S(2)}) collective-permute-start(bf16[4,2,64,256]{3,2,1,0:T(8,128)(2,1)S(1)} %constant_dynamic-slice_fusion.3), channel_id=1, source_target_pairs={{0,12},{1,13},{2,14},{3,15},{4,8},{5,9},{6,10},{7,11},{8,4},{9,5},... | collective-permute-start | bytes 786440 | tf_op jit(solution)/shard_map/ppermute | solution.py:241
  8.1 5.6 %collective-permute-start.1 = (bf16[1,2,64,256]{3,2,1,0:T(8,128)(2,1)S(1)}, bf16[1,2,64,256]{3,2,1,0:T(8,128)(2,1)S(1)}, u32[]{:S(2)}, u32[]{:S(2)}) collective-permute-start(bf16[1,2,64,256]{3,2,1,0:T(8,128)(2,1)S(1)} %constant_dynamic-slice_fusion), channel_id=1, source_target_pairs={{4,12},{6,14},{12,4},{14,6},{20,28},{22,30},{28,20},{30,22}} | collective-permute-start | bytes 196616 | tf_op jit(solution)/shard_map/ppermute | solution.py:241
  8.8 5.0 %collective-permute-start.2 = (f32[48,256]{1,0:T(8,128)}, f32[48,256]{1,0:T(8,128)S(1)}, u32[]{:S(2)}, u32[]{:S(2)}) collective-permute-start(f32[48,256]{1,0:T(8,128)} %get-tuple-element.14), channel_id=1, source_target_pairs={{0,1},{1,0},{2,3},{3,2},{4,5},{5,4},{6,7},{7,6},{8,9},{9,8},{10,11... | collective-permute-start | bytes 147464 | tf_op jit(solution)/shard_map/ppermute | solution.py:238
  12.9 0.8 %copy-start.1 = (f32[48,256]{1,0:T(8,128)S(1)}, f32[48,256]{1,0:T(8,128)}, u32[]{:S(2)}) copy-start(f32[48,256]{1,0:T(8,128)} %get-tuple-element.11.x) | copy-start | bytes 147460
  14.6 3.3 %collective-permute-start.3 = (f32[80,256]{1,0:T(8,128)S(1)}, f32[80,256]{1,0:T(8,128)S(1)}, u32[]{:S(2)}, u32[]{:S(2)}) collective-permute-start(f32[80,256]{1,0:T(8,128)S(1)} %shard_map.66.refs_0_), channel_id=1, source_target_pairs={{0,2},{1,3},{2,0},{3,1},{4,6},{5,7},{6,4},{7,5},{8,10},{9,11},{10,... | collective-permute-start | bytes 245768 | tf_op jit(solution)/shard_map/ppermute | solution.py:238
  18.2 4.3 %collective-permute-start.4 = (f32[4,32,256]{2,1,0:T(8,128)S(1)}, f32[4,32,256]{2,1,0:T(8,128)S(1)}, u32[]{:S(2)}, u32[]{:S(2)}) collective-permute-start(f32[4,32,256]{2,1,0:T(8,128)S(1)} %shard_map.67.refs_0_), channel_id=1, source_target_pairs={{0,1},{1,0},{2,3},{3,2},{4,5},{5,4},{6,7},{7,6},{8,9},{9,8},{10,11... | collective-permute-start | bytes 393224 | tf_op jit(solution)/shard_map/ppermute | solution.py:238

commit v8 on v6

--- a/solution.py
+++ b/solution.py
@@ -249,12 +249,12 @@
     own = share(sky, core * each)
     own_beam = share(beam, core * each)
     far = [mirrored(sent, [(a, blocks - 1 - a, c) for a in range(blocks) for c in range(devices)])]
-    vis, _ = lax.optimization_barrier((vis, sent))
+    first = lax.optimization_barrier((own, sent))[0][:1]
+    turned = [(a, blocks - a) for a in range(1, blocks) if 2 * a != blocks]
+    far.append(mirrored(first, [(a, b, c) for a, b in turned for c in range(0, devices, cores)]))
+    vis, _, _ = lax.optimization_barrier((vis, sent, first))
     sums = pool(vis, fringe, noise, feeds, cores, classes)
     held = [across(x, r) for r, x in enumerate(sums)]
-    first = lax.optimization_barrier((own, sums[0]))[0][:1]
-    turned = [(a, blocks - a) for a in range(1, blocks) if 2 * a != blocks]
-    far.append(mirrored(first, [(a, b, c) for a, b in turned for c in range(0, devices, cores)]))
     held[0] = hold(held[0])
     found = response(own, own_beam, far, held)
     found = [across(found, h * cores) for h in range(cuts)]

time: 23.3 us -> 23.3 us (level)
  the two profiles are of different devices: /device:TPU:15 before, /device:TPU:13 now
where the time goes in v8:
time: 23.3 us; the launch traced here: 23.1 us
  starting transfers between devices  9.32 us (40%)
  Pallas kernels  6.81 us (29%)
  waiting for transfers between devices  5 us (21%)
  local copies, waits for them, and re-layouts  1.91 us (8%)
    ppermute x3, starting transfers between devices, across(): lax.ppermute(x, ('freq', 'bl'), [(c, c ^ r) for c in range(devices)])  7.31 us
    pallas_call x1, Pallas kernels, pool(): pl.pallas_call(functools.partial(pool_kernel, cores, classes), in_specs=[...  5.46 us
    ppermute x3, waiting for transfers between devices, across(): lax.ppermute(x, ('freq', 'bl'), [(c, c ^ r) for c in range(devices)])  3.34 us
    ppermute x2, starting transfers between devices, mirrored(): lax.ppermute(sent, ('ma', 'freq', 'bl'), [(a * devices + c, b * devices +...  2.01 us
    ppermute x2, waiting for transfers between devices, mirrored(): lax.ppermute(sent, ('ma', 'freq', 'bl'), [(a * devices + c, b * devices +...  1.66 us
    dynamic_slice x2, local copies, waits for them, and re-layouts, share(): lax.dynamic_slice(x, (start, 0, 0, left), (each, *x.shape[1:3], step))  1.11 us
    unnamed x4, local copies, waits for them, and re-layouts  0.8 us
    pallas_call x1, Pallas kernels, join(): pl.pallas_call(join_kernel, in_specs=[pl.BlockSpec(memory_space=pltpu.VME...  0.71 us
  transfers between devices with their start and end apart: 5, of which 4 were waited for; matrix products, arithmetic and copies ran while one was open for 0% of the time, Pallas kernels for 24%

profile of v8, /device:TPU:13, one launch (start us, length us, event | category | flops | bytes accessed | tf_op | source)
XLA Modules:
  0.0 23.1 jit_solution(3459744713539855156)
XLA Ops:
  0.0 0.0 copy-start
  0.0 1.1 %constant_dynamic-slice_fusion.1 = (bf16[4,2,64,256]{3,2,1,0:T(8,128)(2,1)S(1)}, bf16[4,2,64,256]{3,2,1,0:T(8,128)(2,1)S(1)}) fusion(bf16[8,2,64,512]{3,2,1,0:T(8,128)(2,1)} %param.6, s32[]{:T(128)S(6)} %select_n.14, s32[]{:T(128)S(6)} %select_n.13, s32[]{:T(128)S(6)} %select_n.12), kind=kLoop, calls=%fused_computation.1 | loop fusion | bytes 1048588 | tf_op jit(solution)/shard_map/dynamic_slice | solution.py:246
  1.1 1.4 %collective-permute-start = (bf16[4,2,64,256]{3,2,1,0:T(8,128)(2,1)S(1)}, bf16[4,2,64,256]{3,2,1,0:T(8,128)(2,1)S(1)}, u32[]{:S(2)}, u32[]{:S(2)}) collective-permute-start(bf16[4,2,64,256]{3,2,1,0:T(8,128)(2,1)S(1)} %get-tuple-element.13), channel_id=1, source_target_pairs={{0,12},{1,13},{2,14},{3,15},{4,8},{5,9},{6,10},{7,11},{8,4},{9,5},... | collective-permute-start | bytes 786440 | tf_op jit(solution)/shard_map/ppermute | solution.py:241
  2.5 0.7 %collective-permute-start.1 = (bf16[1,2,64,256]{3,2,1,0:T(8,128)(2,1)S(1)}, bf16[1,2,64,256]{3,2,1,0:T(8,128)(2,1)S(1)}, u32[]{:S(2)}, u32[]{:S(2)}) collective-permute-start(bf16[1,2,64,256]{3,2,1,0:T(8,128)(2,1)S(1)} %slice.3), channel_id=1, source_target_pairs={{4,12},{6,14},{12,4},{14,6},{20,28},{22,30},{28,20},{30,22}} | collective-permute-start | bytes 196616 | tf_op jit(solution)/shard_map/ppermute | solution.py:241
  3.1 5.5 %shard_map.64 = (f32[48,256]{1,0:T(8,128)}, f32[48,256]{1,0:T(8,128)}) custom-call(bf16[16,8,2,64,256]{4,3,2,1,0:T(8,128)(2,1)} %vis, f32[16,2,256]{2,1,0:T(2,128)} %fringe.1, f32[16,256]{1,0:T(8,128)} %noise.1, s32[1,256]{1,0:T(1,128)} %bitcast.2), custom_call_target="tpu_custom_call" | custom-call | flops 805306368 | bytes 8388608 | tf_op jit(solution)/shard_map/pallas_call | solution.py:93
  8.6 3.5 %collective-permute-start.2 = (f32[48,256]{1,0:T(8,128)}, f32[48,256]{1,0:T(8,128)S(1)}, u32[]{:S(2)}, u32[]{:S(2)}) collective-permute-start(f32[48,256]{1,0:T(8,128)} %get-tuple-element.12), channel_id=1, source_target_pairs={{0,1},{1,0},{2,3},{3,2},{4,5},{5,4},{6,7},{7,6},{8,9},{9,8},{10,11... | collective-permute-start | bytes 147464 | tf_op jit(solution)/shard_map/ppermute | solution.py:238
  12.1 0.0 copy-done
  12.1 0.0 copy-start.1
  12.1 0.8 %copy-done.1 = f32[48,256]{1,0:T(8,128)S(1)} copy-done((f32[48,256]{1,0:T(8,128)S(1)}, f32[48,256]{1,0:T(8,128)}, u32[]{:S(2)}) %copy-start.1) | copy-done | bytes 49176
  12.9 0.3 %collective-permute-done.2.refs_1_ = f32[48,256]{1,0:T(8,128)S(1)} collective-permute-done((f32[48,256]{1,0:T(8,128)}, f32[48,256]{1,0:T(8,128)S(1)}, u32[]{:S(2)}, u32[]{:S(2)}) %collective-permute-start.2) | collective-permute-done | bytes 49184 | tf_op jit(solution)/shard_map/ppermute | solution.py:238
  13.2 0.0 collective-permute-done.1.second
  13.2 1.7 %collective-permute-done.first = bf16[4,2,64,256]{3,2,1,0:T(8,128)(2,1)S(1)} collective-permute-done((bf16[4,2,64,256]{3,2,1,0:T(8,128)(2,1)S(1)}, bf16[4,2,64,256]{3,2,1,0:T(8,128)(2,1)S(1)}, u32[]{:S(2)}, u32[]{:S(2)}) %collective-permute-start) | collective-permute-done | bytes 262176 | tf_op jit(solution)/shard_map/ppermute | solution.py:241
  14.9 0.3 %shard_map.66.refs_0_ = f32[80,256]{1,0:T(8,128)S(1)} custom-call(bf16[4,2,64,256]{3,2,1,0:T(8,128)(2,1)S(1)} %get-tuple-element.9.sky, bf16[4,2,16,256]{3,2,1,0:T(8,128)(2,1)S(1)} %constant_dynamic-slice_fusion.beam, bf16[4,2,64,256]{3,2,1,0:T(8,128)(2,1)S(1)} %collective-permute-done.first, bf16[1,2,64,256]{3,2,1,0:T(8,128)(2,1)S(1)} %collective-permute-done.1.second, ...), custom_call_target="tpu_custom_call" | custom-call | tf_op jit(solution)/shard_map/pallas_call | solution.py:160
  15.2 1.2 %collective-permute-start.3 = (f32[80,256]{1,0:T(8,128)S(1)}, f32[80,256]{1,0:T(8,128)S(1)}, u32[]{:S(2)}, u32[]{:S(2)}) collective-permute-start(f32[80,256]{1,0:T(8,128)S(1)} %shard_map.66.refs_0_), channel_id=1, source_target_pairs={{0,2},{1,3},{2,0},{3,1},{4,6},{5,7},{6,4},{7,5},{8,10},{9,11},{10,... | collective-permute-start | bytes 245768 | tf_op jit(solution)/shard_map/ppermute | solution.py:238
  16.4 2.1 %collective-permute-done.3.refs_1_ = f32[80,256]{1,0:T(8,128)S(1)} collective-permute-done((f32[80,256]{1,0:T(8,128)S(1)}, f32[80,256]{1,0:T(8,128)S(1)}, u32[]{:S(2)}, u32[]{:S(2)}) %collective-permute-start.3) | collective-permute-done | bytes 81952 | tf_op jit(solution)/shard_map/ppermute | solution.py:238
  18.5 0.3 %shard_map.67.refs_0_ = f32[4,32,256]{2,1,0:T(8,128)S(1)} custom-call(bf16[4,2,64,256]{3,2,1,0:T(8,128)(2,1)S(1)} %get-tuple-element.9.sky, bf16[4,2,64,256]{3,2,1,0:T(8,128)(2,1)S(1)} %collective-permute-done.first, bf16[1,2,64,256]{3,2,1,0:T(8,128)(2,1)S(1)} %collective-permute-done.1.second, f32[80,256]{1,0:T(8,128)S(1)} %shard_map.66.refs_0_, ...), custom_call_target="tpu_custom_call" | custom-call | tf_op jit(solution)/shard_map/pallas_call | solution.py:192
  18.8 2.6 %collective-permute-start.4 = (f32[4,32,256]{2,1,0:T(8,128)S(1)}, f32[4,32,256]{2,1,0:T(8,128)S(1)}, u32[]{:S(2)}, u32[]{:S(2)}) collective-permute-start(f32[4,32,256]{2,1,0:T(8,128)S(1)} %shard_map.67.refs_0_), channel_id=1, source_target_pairs={{0,1},{1,0},{2,3},{3,2},{4,5},{5,4},{6,7},{7,6},{8,9},{9,8},{10,11... | collective-permute-start | bytes 393224 | tf_op jit(solution)/shard_map/ppermute | solution.py:238
  21.4 1.0 %collective-permute-done.4.refs_1_ = f32[4,32,256]{2,1,0:T(8,128)S(1)} collective-permute-done((f32[4,32,256]{2,1,0:T(8,128)S(1)}, f32[4,32,256]{2,1,0:T(8,128)S(1)}, u32[]{:S(2)}, u32[]{:S(2)}) %collective-permute-start.4) | collective-permute-done | bytes 131104 | tf_op jit(solution)/shard_map/ppermute | solution.py:238
  22.4 0.7 %shard_map.68 = f32[8,32,256]{2,1,0:T(8,128)} custom-call(f32[4,32,256]{2,1,0:T(8,128)S(1)} %shard_map.67.refs_0_, f32[4,32,256]{2,1,0:T(8,128)S(1)} %collective-permute-done.4.refs_1_), custom_call_target="tpu_custom_call" | custom-call | tf_op jit(solution)/shard_map/pallas_call | solution.py:217
  (3 shorter events, 0.0 us)
Async XLA Ops:
  0.0 12.1 %copy-start = (bf16[8,2,16,512]{3,2,1,0:T(8,128)(2,1)S(1)}, bf16[8,2,16,512]{3,2,1,0:T(8,128)(2,1)}, u32[]{:S(2)}) copy-start(bf16[8,2,16,512]{3,2,1,0:T(8,128)(2,1)} %param.7) | copy-start | bytes 786436
  1.1 13.7 %collective-permute-start = (bf16[4,2,64,256]{3,2,1,0:T(8,128)(2,1)S(1)}, bf16[4,2,64,256]{3,2,1,0:T(8,128)(2,1)S(1)}, u32[]{:S(2)}, u32[]{:S(2)}) collective-permute-start(bf16[4,2,64,256]{3,2,1,0:T(8,128)(2,1)S(1)} %get-tuple-element.13), channel_id=1, source_target_pairs={{0,12},{1,13},{2,14},{3,15},{4,8},{5,9},{6,10},{7,11},{8,4},{9,5},... | collective-permute-start | bytes 786440 | tf_op jit(solution)/shard_map/ppermute | solution.py:241
  2.5 10.7 %collective-permute-start.1 = (bf16[1,2,64,256]{3,2,1,0:T(8,128)(2,1)S(1)}, bf16[1,2,64,256]{3,2,1,0:T(8,128)(2,1)S(1)}, u32[]{:S(2)}, u32[]{:S(2)}) collective-permute-start(bf16[1,2,64,256]{3,2,1,0:T(8,128)(2,1)S(1)} %slice.3), channel_id=1, source_target_pairs={{4,12},{6,14},{12,4},{14,6},{20,28},{22,30},{28,20},{30,22}} | collective-permute-start | bytes 196616 | tf_op jit(solution)/shard_map/ppermute | solution.py:241
  8.6 4.6 %collective-permute-start.2 = (f32[48,256]{1,0:T(8,128)}, f32[48,256]{1,0:T(8,128)S(1)}, u32[]{:S(2)}, u32[]{:S(2)}) collective-permute-start(f32[48,256]{1,0:T(8,128)} %get-tuple-element.12), channel_id=1, source_target_pairs={{0,1},{1,0},{2,3},{3,2},{4,5},{5,4},{6,7},{7,6},{8,9},{9,8},{10,11... | collective-permute-start | bytes 147464 | tf_op jit(solution)/shard_map/ppermute | solution.py:238
  12.1 0.8 %copy-start.1 = (f32[48,256]{1,0:T(8,128)S(1)}, f32[48,256]{1,0:T(8,128)}, u32[]{:S(2)}) copy-start(f32[48,256]{1,0:T(8,128)} %get-tuple-element.11.x) | copy-start | bytes 147460
  15.2 3.3 %collective-permute-start.3 = (f32[80,256]{1,0:T(8,128)S(1)}, f32[80,256]{1,0:T(8,128)S(1)}, u32[]{:S(2)}, u32[]{:S(2)}) collective-permute-start(f32[80,256]{1,0:T(8,128)S(1)} %shard_map.66.refs_0_), channel_id=1, source_target_pairs={{0,2},{1,3},{2,0},{3,1},{4,6},{5,7},{6,4},{7,5},{8,10},{9,11},{10,... | collective-permute-start | bytes 245768 | tf_op jit(solution)/shard_map/ppermute | solution.py:238
  18.8 3.6 %collective-permute-start.4 = (f32[4,32,256]{2,1,0:T(8,128)S(1)}, f32[4,32,256]{2,1,0:T(8,128)S(1)}, u32[]{:S(2)}, u32[]{:S(2)}) collective-permute-start(f32[4,32,256]{2,1,0:T(8,128)S(1)} %shard_map.67.refs_0_), channel_id=1, source_target_pairs={{0,1},{1,0},{2,3},{3,2},{4,5},{5,4},{6,7},{7,6},{8,9},{9,8},{10,11... | collective-permute-start | bytes 393224 | tf_op jit(solution)/shard_map/ppermute | solution.py:238

commit v9 on v6

--- a/solution.py
+++ b/solution.py
@@ -198,13 +198,13 @@
     )(sky, *far, *found)
 
 
-def join_kernel(*refs):
-    pieces, out, sems = refs[:-2], refs[-2], refs[-1]
+def join_kernel(ranks, *refs):
+    pieces, out, sems = refs[: len(ranks)], refs[-2], refs[-1]
     each = pieces[0].shape[0]
     core = my_core()
     copies = [
-        pltpu.make_async_copy(piece, out.at[pl.ds((core ^ r) * each, each)], sems.at[r])
-        for r, piece in enumerate(pieces)
+        pltpu.make_async_copy(piece, out.at[pl.ds((core ^ r) * each, each)], sems.at[n])
+        for n, (r, piece) in enumerate(zip(ranks, pieces))
     ]
     for copy in copies:
         copy.start()
@@ -212,16 +212,19 @@
         copy.wait()
 
 
-def join(pieces):
+def join(cores, ranks, pieces, begun=None):
     each, wide, step = pieces[0].shape
-    return pl.pallas_call(
-        join_kernel,
-        in_specs=[pl.BlockSpec(memory_space=pltpu.VMEM)] * len(pieces),
-        out_specs=pl.BlockSpec(memory_space=pl.ANY),
-        out_shape=jax.ShapeDtypeStruct((each * len(pieces), wide, step), F32),
+    more = [] if begun is None else [begun]
+    anywhere = pl.BlockSpec(memory_space=pl.ANY)
+    return pl.pallas_call(
+        functools.partial(join_kernel, ranks),
+        in_specs=[pl.BlockSpec(memory_space=pltpu.VMEM)] * len(pieces) + [anywhere] * len(more),
+        out_specs=anywhere,
+        out_shape=jax.ShapeDtypeStruct((each * cores, wide, step), F32),
         scratch_shapes=[pltpu.SemaphoreType.DMA((len(pieces),))],
-        compiler_params=pltpu.CompilerParams(vmem_limit_bytes=8 << 20),
-    )(*pieces)
+        input_output_aliases={len(pieces): 0} if more else {},
+        compiler_params=pltpu.CompilerParams(vmem_limit_bytes=8 << 20),
+    )(*pieces, *more)
 
 
 def body(sky, beam, vis, fringe, noise, feeds):
@@ -259,7 +262,9 @@
     found = response(own, own_beam, far, held)
     found = [across(found, h * cores) for h in range(cuts)]
     grad = gradient(classes, own, far, found)
-    out = join([across(grad, r) for r in range(cores)])
+    out = join(cores, [0], [grad])
+    if cores > 1:
+        out = join(cores, list(range(1, cores)), [across(grad, r) for r in range(1, cores)], out)
     return out.reshape(slots, 2, classes, step)
 
 

time: 23.3 us -> 23.3 us (level)
  waiting for transfers between devices: 5.24 us -> 4.57 us
  Pallas kernels: 6.78 us -> 7.39 us
    ppermute x3, waiting for transfers between devices: 4.3 us -> 3.63 us  [across(): lax.ppermute(x, ('freq', 'bl'), [(c, c ^ r) for c in range(devices)])]
    pallas_call x1 -> x2, Pallas kernels: 0.71 us -> 1.32 us  [join(): pl.pallas_call(functools.partial(join_kernel, ranks), in_specs=[pl.BlockS...]
  transfers between devices with their start and end apart: 5 -> 5, of which waited for: 4 -> 4; matrix products, arithmetic and copies ran while one was open for 0% -> 0% of each run, Pallas kernels for 23% -> 26%
where the time goes in v9:
time: 23.3 us; the launch traced here: 23 us
  starting transfers between devices  9.11 us (39%)
  Pallas kernels  7.39 us (32%)
  waiting for transfers between devices  4.57 us (20%)
  local copies, waits for them, and re-layouts  1.92 us (8%)
    ppermute x3, starting transfers between devices, across(): lax.ppermute(x, ('freq', 'bl'), [(c, c ^ r) for c in range(devices)])  7.08 us
    pallas_call x1, Pallas kernels, pool(): pl.pallas_call(functools.partial(pool_kernel, cores, classes), in_specs=[...  5.42 us
    ppermute x3, waiting for transfers between devices, across(): lax.ppermute(x, ('freq', 'bl'), [(c, c ^ r) for c in range(devices)])  3.63 us
    ppermute x2, starting transfers between devices, mirrored(): lax.ppermute(sent, ('ma', 'freq', 'bl'), [(a * devices + c, b * devices +...  2.03 us
    pallas_call x2, Pallas kernels, join(): pl.pallas_call(functools.partial(join_kernel, ranks), in_specs=[pl.BlockS...  1.32 us
    dynamic_slice x2, local copies, waits for them, and re-layouts, share(): lax.dynamic_slice(x, (start, 0, 0, left), (each, *x.shape[1:3], step))  1.11 us
    ppermute x2, waiting for transfers between devices, mirrored(): lax.ppermute(sent, ('ma', 'freq', 'bl'), [(a * devices + c, b * devices +...  0.94 us
    unnamed x4, local copies, waits for them, and re-layouts  0.8 us
  transfers between devices with their start and end apart: 5, of which 4 were waited for; matrix products, arithmetic and copies ran while one was open for 0% of the time, Pallas kernels for 26%

profile of v9, /device:TPU:15, one launch (start us, length us, event | category | flops | bytes accessed | tf_op | source)
XLA Modules:
  0.0 23.0 jit_solution(17151892577086166801)
XLA Ops:
  0.0 0.0 copy-start
  0.0 1.1 %constant_dynamic-slice_fusion.1 = (bf16[4,2,64,256]{3,2,1,0:T(8,128)(2,1)S(1)}, bf16[4,2,64,256]{3,2,1,0:T(8,128)(2,1)S(1)}) fusion(bf16[8,2,64,512]{3,2,1,0:T(8,128)(2,1)} %param.6, s32[]{:T(128)S(6)} %select_n.14, s32[]{:T(128)S(6)} %select_n.13, s32[]{:T(128)S(6)} %select_n.12), kind=kLoop, calls=%fused_computation.1 | loop fusion | bytes 1048588 | tf_op jit(solution)/shard_map/dynamic_slice | solution.py:249
  1.1 1.4 %collective-permute-start = (bf16[4,2,64,256]{3,2,1,0:T(8,128)(2,1)S(1)}, bf16[4,2,64,256]{3,2,1,0:T(8,128)(2,1)S(1)}, u32[]{:S(2)}, u32[]{:S(2)}) collective-permute-start(bf16[4,2,64,256]{3,2,1,0:T(8,128)(2,1)S(1)} %get-tuple-element.13), channel_id=1, source_target_pairs={{0,12},{1,13},{2,14},{3,15},{4,8},{5,9},{6,10},{7,11},{8,4},{9,5},... | collective-permute-start | bytes 786440 | tf_op jit(solution)/shard_map/ppermute | solution.py:244
  2.5 5.4 %shard_map.64 = (f32[48,256]{1,0:T(8,128)}, f32[48,256]{1,0:T(8,128)}) custom-call(bf16[16,8,2,64,256]{4,3,2,1,0:T(8,128)(2,1)} %vis, f32[16,2,256]{2,1,0:T(2,128)} %fringe.1, f32[16,256]{1,0:T(8,128)} %noise.1, s32[1,256]{1,0:T(1,128)} %bitcast.2), custom_call_target="tpu_custom_call" | custom-call | flops 805306368 | bytes 8388608 | tf_op jit(solution)/shard_map/pallas_call | solution.py:93
  7.9 0.7 %collective-permute-start.1 = (bf16[1,2,64,256]{3,2,1,0:T(8,128)(2,1)S(1)}, bf16[1,2,64,256]{3,2,1,0:T(8,128)(2,1)S(1)}, u32[]{:S(2)}, u32[]{:S(2)}) collective-permute-start(bf16[1,2,64,256]{3,2,1,0:T(8,128)(2,1)S(1)} %slice.3), channel_id=1, source_target_pairs={{4,12},{6,14},{12,4},{14,6},{20,28},{22,30},{28,20},{30,22}} | collective-permute-start | bytes 196616 | tf_op jit(solution)/shard_map/ppermute | solution.py:244
  8.6 3.5 %collective-permute-start.2 = (f32[48,256]{1,0:T(8,128)}, f32[48,256]{1,0:T(8,128)S(1)}, u32[]{:S(2)}, u32[]{:S(2)}) collective-permute-start(f32[48,256]{1,0:T(8,128)} %get-tuple-element.12), channel_id=1, source_target_pairs={{0,1},{1,0},{2,3},{3,2},{4,5},{5,4},{6,7},{7,6},{8,9},{9,8},{10,11... | collective-permute-start | bytes 147464 | tf_op jit(solution)/shard_map/ppermute | solution.py:241
  12.1 0.0 copy-done
  12.1 0.0 copy-start.1
  12.1 0.8 %copy-done.1 = f32[48,256]{1,0:T(8,128)S(1)} copy-done((f32[48,256]{1,0:T(8,128)S(1)}, f32[48,256]{1,0:T(8,128)}, u32[]{:S(2)}) %copy-start.1) | copy-done | bytes 49176
  12.9 0.3 %collective-permute-done.2.refs_1_ = f32[48,256]{1,0:T(8,128)S(1)} collective-permute-done((f32[48,256]{1,0:T(8,128)}, f32[48,256]{1,0:T(8,128)S(1)}, u32[]{:S(2)}, u32[]{:S(2)}) %collective-permute-start.2) | collective-permute-done | bytes 49184 | tf_op jit(solution)/shard_map/ppermute | solution.py:241
  13.2 0.0 collective-permute-done.1.second
  13.2 0.9 %collective-permute-done.first = bf16[4,2,64,256]{3,2,1,0:T(8,128)(2,1)S(1)} collective-permute-done((bf16[4,2,64,256]{3,2,1,0:T(8,128)(2,1)S(1)}, bf16[4,2,64,256]{3,2,1,0:T(8,128)(2,1)S(1)}, u32[]{:S(2)}, u32[]{:S(2)}) %collective-permute-start) | collective-permute-done | bytes 262176 | tf_op jit(solution)/shard_map/ppermute | solution.py:244
  14.2 0.3 %shard_map.66.refs_0_ = f32[80,256]{1,0:T(8,128)S(1)} custom-call(bf16[4,2,64,256]{3,2,1,0:T(8,128)(2,1)S(1)} %get-tuple-element.11.sky, bf16[4,2,16,256]{3,2,1,0:T(8,128)(2,1)S(1)} %constant_dynamic-slice_fusion.beam, bf16[4,2,64,256]{3,2,1,0:T(8,128)(2,1)S(1)} %collective-permute-done.first, bf16[1,2,64,256]{3,2,1,0:T(8,128)(2,1)S(1)} %collective-permute-done.1.second, ...), custom_call_target="tpu_custom_call" | custom-call | tf_op jit(solution)/shard_map/pallas_call | solution.py:160
  14.5 0.3 %collective-permute-start.3 = (f32[80,256]{1,0:T(8,128)S(1)}, f32[80,256]{1,0:T(8,128)S(1)}, u32[]{:S(2)}, u32[]{:S(2)}) collective-permute-start(f32[80,256]{1,0:T(8,128)S(1)} %shard_map.66.refs_0_), channel_id=1, source_target_pairs={{0,2},{1,3},{2,0},{3,1},{4,6},{5,7},{6,4},{7,5},{8,10},{9,11},{10,... | collective-permute-start | bytes 245768 | tf_op jit(solution)/shard_map/ppermute | solution.py:241
  14.8 3.0 %collective-permute-done.3.refs_1_ = f32[80,256]{1,0:T(8,128)S(1)} collective-permute-done((f32[80,256]{1,0:T(8,128)S(1)}, f32[80,256]{1,0:T(8,128)S(1)}, u32[]{:S(2)}, u32[]{:S(2)}) %collective-permute-start.3) | collective-permute-done | bytes 81952 | tf_op jit(solution)/shard_map/ppermute | solution.py:241
  17.8 0.3 %shard_map.67.refs_0_ = f32[4,32,256]{2,1,0:T(8,128)S(1)} custom-call(bf16[4,2,64,256]{3,2,1,0:T(8,128)(2,1)S(1)} %get-tuple-element.11.sky, bf16[4,2,64,256]{3,2,1,0:T(8,128)(2,1)S(1)} %collective-permute-done.first, bf16[1,2,64,256]{3,2,1,0:T(8,128)(2,1)S(1)} %collective-permute-done.1.second, f32[80,256]{1,0:T(8,128)S(1)} %shard_map.66.refs_0_, ...), custom_call_target="tpu_custom_call" | custom-call | tf_op jit(solution)/shard_map/pallas_call | solution.py:192
  18.1 3.3 %collective-permute-start.4 = (f32[4,32,256]{2,1,0:T(8,128)S(1)}, f32[4,32,256]{2,1,0:T(8,128)S(1)}, u32[]{:S(2)}, u32[]{:S(2)}) collective-permute-start(f32[4,32,256]{2,1,0:T(8,128)S(1)} %shard_map.67.refs_0_), channel_id=1, source_target_pairs={{0,1},{1,0},{2,3},{3,2},{4,5},{5,4},{6,7},{7,6},{8,9},{9,8},{10,11... | collective-permute-start | bytes 393224 | tf_op jit(solution)/shard_map/ppermute | solution.py:241
  21.4 0.7 %shard_map.68.refs_1_ = f32[8,32,256]{2,1,0:T(8,128)} custom-call(f32[4,32,256]{2,1,0:T(8,128)S(1)} %shard_map.67.refs_0_), custom_call_target="tpu_custom_call" | custom-call | tf_op jit(solution)/shard_map/pallas_call | solution.py:219
  22.1 0.3 %collective-permute-done.4.refs_0_ = f32[4,32,256]{2,1,0:T(8,128)S(1)} collective-permute-done((f32[4,32,256]{2,1,0:T(8,128)S(1)}, f32[4,32,256]{2,1,0:T(8,128)S(1)}, u32[]{:S(2)}, u32[]{:S(2)}) %collective-permute-start.4) | collective-permute-done | bytes 131104 | tf_op jit(solution)/shard_map/ppermute | solution.py:241
  22.4 0.7 %shard_map.69 = f32[8,32,256]{2,1,0:T(8,128)} custom-call(f32[4,32,256]{2,1,0:T(8,128)S(1)} %collective-permute-done.4.refs_0_, f32[8,32,256]{2,1,0:T(8,128)} %shard_map.68.refs_1_), custom_call_target="tpu_custom_call", output_to_operand_aliasing={{}: (1, {})} | custom-call | tf_op jit(solution)/shard_map/pallas_call | solution.py:219
  (3 shorter events, 0.0 us)
Async XLA Ops:
  0.0 12.1 %copy-start = (bf16[8,2,16,512]{3,2,1,0:T(8,128)(2,1)S(1)}, bf16[8,2,16,512]{3,2,1,0:T(8,128)(2,1)}, u32[]{:S(2)}) copy-start(bf16[8,2,16,512]{3,2,1,0:T(8,128)(2,1)} %param.7) | copy-start | bytes 786436
  1.1 13.0 %collective-permute-start = (bf16[4,2,64,256]{3,2,1,0:T(8,128)(2,1)S(1)}, bf16[4,2,64,256]{3,2,1,0:T(8,128)(2,1)S(1)}, u32[]{:S(2)}, u32[]{:S(2)}) collective-permute-start(bf16[4,2,64,256]{3,2,1,0:T(8,128)(2,1)S(1)} %get-tuple-element.13), channel_id=1, source_target_pairs={{0,12},{1,13},{2,14},{3,15},{4,8},{5,9},{6,10},{7,11},{8,4},{9,5},... | collective-permute-start | bytes 786440 | tf_op jit(solution)/shard_map/ppermute | solution.py:244
  7.9 5.3 %collective-permute-start.1 = (bf16[1,2,64,256]{3,2,1,0:T(8,128)(2,1)S(1)}, bf16[1,2,64,256]{3,2,1,0:T(8,128)(2,1)S(1)}, u32[]{:S(2)}, u32[]{:S(2)}) collective-permute-start(bf16[1,2,64,256]{3,2,1,0:T(8,128)(2,1)S(1)} %slice.3), channel_id=1, source_target_pairs={{4,12},{6,14},{12,4},{14,6},{20,28},{22,30},{28,20},{30,22}} | collective-permute-start | bytes 196616 | tf_op jit(solution)/shard_map/ppermute | solution.py:244
  8.6 4.6 %collective-permute-start.2 = (f32[48,256]{1,0:T(8,128)}, f32[48,256]{1,0:T(8,128)S(1)}, u32[]{:S(2)}, u32[]{:S(2)}) collective-permute-start(f32[48,256]{1,0:T(8,128)} %get-tuple-element.12), channel_id=1, source_target_pairs={{0,1},{1,0},{2,3},{3,2},{4,5},{5,4},{6,7},{7,6},{8,9},{9,8},{10,11... | collective-permute-start | bytes 147464 | tf_op jit(solution)/shard_map/ppermute | solution.py:241
  12.1 0.8 %copy-start.1 = (f32[48,256]{1,0:T(8,128)S(1)}, f32[48,256]{1,0:T(8,128)}, u32[]{:S(2)}) copy-start(f32[48,256]{1,0:T(8,128)} %get-tuple-element.10.x) | copy-start | bytes 147460
  14.5 3.3 %collective-permute-start.3 = (f32[80,256]{1,0:T(8,128)S(1)}, f32[80,256]{1,0:T(8,128)S(1)}, u32[]{:S(2)}, u32[]{:S(2)}) collective-permute-start(f32[80,256]{1,0:T(8,128)S(1)} %shard_map.66.refs_0_), channel_id=1, source_target_pairs={{0,2},{1,3},{2,0},{3,1},{4,6},{5,7},{6,4},{7,5},{8,10},{9,11},{10,... | collective-permute-start | bytes 245768 | tf_op jit(solution)/shard_map/ppermute | solution.py:241
  18.1 4.3 %collective-permute-start.4 = (f32[4,32,256]{2,1,0:T(8,128)S(1)}, f32[4,32,256]{2,1,0:T(8,128)S(1)}, u32[]{:S(2)}, u32[]{:S(2)}) collective-permute-start(f32[4,32,256]{2,1,0:T(8,128)S(1)} %shard_map.67.refs_0_), channel_id=1, source_target_pairs={{0,1},{1,0},{2,3},{3,2},{4,5},{5,4},{6,7},{7,6},{8,9},{9,8},{10,11... | collective-permute-start | bytes 393224 | tf_op jit(solution)/shard_map/ppermute | solution.py:241
